TPU v7x, 128 devices: a whole 4x4x4 slice. The times are simulated.
128 devices in a mesh: seq: 32 (over y_hi, x, z), head: 4 (over y_lo, core).
Axes of the slice: x: 4, y: 4 (y_hi: 2, y_lo: 2; y = y_hi * 2 + y_lo), z: 4, core: 2. Of those that a mesh axis runs over, the one named last changes fastest.
Arguments:
- queries: bfloat16 [16384, 20, 128], P('seq', 'head'), may hold values from -17 to 17
- key_rows: bfloat16 [16384, 20, 128], P('seq', 'head'), may hold values from -17 to 17
- value_rows: bfloat16 [16384, 20, 128], P('seq', 'head'), may hold values from -6 to 6
- out_weight: bfloat16 [20, 128, 5120], P('head'), may hold values from -0.5 to 0.5
- tile_mask: int32 [128, 128], replicated, may hold values from 0 to 1, as said below
Outputs:
- mixed: bfloat16 [16384, 5120], P('seq', 'head')
Inputs may be any that keep to these rules, and one draw needn't show every extreme that they name: tile_mask[a, b] = 1 exactly when tiles a and b lie in the same or adjacent slabs, a slab being 8 consecutive tiles, and their places in the slab's grid of 2 rows by 4 columns differ by at most one row and one column; each slab assigns its 8 tiles to the 8 places of its grid in its own arbitrary order. tile_mask is symmetric with ones on its diagonal, and zero between tokens whose devices along seq are more than 3 apart.
All inputs are finite; a program needn't handle non-finite values.
Results may differ from a plain program's by a relative error of at most 0.009.
Values may be sent and summed in bfloat16 or wider, within the bound.
No kernel may reach another device: no remote copies, remote signals or barrier semaphores. Data moves between devices by JAX's collectives and lax.ppermute only.
A program may use at most 128 MiB of HBM per device.

v0:
```python
import jax
import jax.numpy as jnp
from jax import lax
from jax.sharding import PartitionSpec as P

TILE = 128
REACH = 3


NEG = -1e30


def shifted(block, axis, distance):
    devices = range(lax.axis_size(axis))
    route = [((i - distance) % len(devices), i) for i in devices]
    return lax.ppermute(block, axis, route)


def token_mask(tile_mask, anchor, holder, tile_count):
    tile_block = lax.dynamic_slice(
        tile_mask, (anchor * tile_count, holder * tile_count), (tile_count, tile_count)
    )
    widened = jnp.broadcast_to(
        tile_block[:, None, :, None] > 0, (tile_count, TILE, tile_count, TILE)
    )
    return (widened.reshape(tile_count * TILE, tile_count * TILE), jnp.any(tile_block > 0))


def update(state_now, query_rows, key_rows, value_rows, live_tokens):
    acc_rows, running_max, running_sum = state_now
    inv_scale = query_rows.shape[-1] ** (-0.5)
    scores = (
        jnp.einsum("qhe,khe->hqk", query_rows, key_rows, preferred_element_type=jnp.float32)
        * inv_scale
    )
    masked = jnp.where(live_tokens[None], scores, NEG)
    top_new = jnp.maximum(running_max, jnp.max(masked, axis=-1))
    weights = jnp.where(live_tokens[None], jnp.exp(scores - top_new[:, :, None]), 0.0)
    shrink = jnp.exp(running_max - top_new)
    sum_new = running_sum * shrink + jnp.sum(weights, axis=-1)
    summed = jnp.einsum(
        "hqk,khe->qhe", weights.astype(jnp.bfloat16), value_rows, preferred_element_type=jnp.float32
    )
    acc_new = acc_rows * jnp.transpose(shrink)[:, :, None] + summed
    return (acc_new, top_new, sum_new)


def visit(state_now, query_rows, key_rows, value_rows, tile_mask, anchor, holder, tile_count):
    live_tokens, any_live = token_mask(tile_mask, anchor, holder, tile_count)
    return update(state_now, query_rows, key_rows, value_rows, live_tokens)


def finish(state_now):
    acc_rows, running_max, running_sum = state_now
    return (acc_rows / jnp.transpose(running_sum)[:, :, None]).astype(jnp.bfloat16)


def local(queries, key_rows, value_rows, out_weight, tile_mask):
    tok_rows, heads_here, head_size = queries.shape
    tile_count = tok_rows // TILE
    cycle_size = lax.axis_size("seq")
    own_index = lax.axis_index("seq")
    fresh = (
        jnp.zeros((tok_rows, heads_here, head_size), jnp.float32),
        jnp.full((heads_here, tok_rows), NEG, jnp.float32),
        jnp.zeros((heads_here, tok_rows), jnp.float32),
    )
    moving = shifted(queries, "seq", -REACH)
    anchor = (own_index + REACH) % cycle_size
    state_now = visit(fresh, moving, key_rows, value_rows, tile_mask, anchor, own_index, tile_count)
    for section in range(2 * REACH):
        moving = shifted(moving, "seq", 1)
        state_now = shifted((state_now[0], state_now[1], state_now[2]), "seq", 1)
        anchor = (own_index + REACH - section - 1) % cycle_size
        state_now = visit(
            state_now, moving, key_rows, value_rows, tile_mask, anchor, own_index, tile_count
        )
    attended = shifted(finish(state_now), "seq", -REACH)
    flat_rows = attended.reshape(tok_rows, heads_here * head_size)
    weight_flat = out_weight.reshape(heads_here * head_size, out_weight.shape[-1])
    partial_value = jnp.dot(flat_rows, weight_flat, preferred_element_type=jnp.float32)
    return lax.psum_scatter(partial_value, "head", scatter_dimension=1, tiled=True).astype(
        jnp.bfloat16
    )


def solution(mesh):
    placed = (
        P("seq", "head", None),
        P("seq", "head", None),
        P("seq", "head", None),
        P("head", None, None),
        P(),
    )
    return jax.shard_map(
        local, mesh=mesh, in_specs=placed, out_specs=P("seq", "head"), check_vma=False
    )
```

profile of v0, /device:TPU:17, one launch (start us, length us, event | category | flops | bytes accessed | tf_op | source)
XLA Modules:
  0.0 467.0 jit_solution(14436764391514950136)
XLA Ops:
  6.5 3.6 collective-permute-start
  11.5 13.5 %collective-permute-done = bf16[512,5,128]{2,0,1:T(8,128)(2,1)S(1)} collective-permute-done((bf16[512,5,128]{2,0,1:T(8,128)(2,1)}, bf16[512,5,128]{2,0,1:T(8,128)(2,1)S(1)}, u32[]{:S(2)}, u32[]{:S(2)}) %collective-permute-start) | collective-permute-done | bytes 655392 | tf_op jit(solution)/shard_map/ppermute | solution.py:16
  26.0 1.1 fusion
  27.2 2.8 fusion.77
  30.5 1.3 collective-permute-start.3
  33.4 46.0 %collective-permute-done.3 = bf16[512,5,128]{2,0,1:T(8,128)(2,1)S(1)} collective-permute-done((bf16[512,5,128]{2,0,1:T(8,128)(2,1)S(1)}, bf16[512,5,128]{2,0,1:T(8,128)(2,1)S(1)}, u32[]{:S(2)}, u32[]{:S(2)}) %collective-permute-start.3) | collective-permute-done | bytes 655392 | tf_op jit(solution)/shard_map/ppermute | solution.py:16
  80.4 2.2 copy-done.1
  82.7 3.9 multiply_add_fusion.4
  89.6 44.8 %collective-permute-done.6 = bf16[512,5,128]{2,0,1:T(8,128)(2,1)S(1)} collective-permute-done((bf16[512,5,128]{2,0,1:T(8,128)(2,1)S(1)}, bf16[512,5,128]{2,0,1:T(8,128)(2,1)S(1)}, u32[]{:S(2)}, u32[]{:S(2)}) %collective-permute-start.6) | collective-permute-done | bytes 655392 | tf_op jit(solution)/shard_map/ppermute | solution.py:16
  135.5 3.2 multiply_add_fusion.3
  138.9 1.1 fusion.2
  140.3 1.1 fusion.4
  141.4 43.8 %collective-permute-done.9 = bf16[512,5,128]{2,0,1:T(8,128)(2,1)S(1)} collective-permute-done((bf16[512,5,128]{2,0,1:T(8,128)(2,1)S(1)}, bf16[512,5,128]{2,0,1:T(8,128)(2,1)S(1)}, u32[]{:S(2)}, u32[]{:S(2)}) %collective-permute-start.9) | collective-permute-done | bytes 655392 | tf_op jit(solution)/shard_map/ppermute | solution.py:16
  186.3 2.0 multiply_add_fusion.2
  188.6 1.1 fusion.6
  189.8 30.0 %collective-permute-done.21 = f32[5,512]{1,0:T(8,128)S(1)} collective-permute-done((f32[5,512]{1,0:T(8,128)S(1)}, f32[5,512]{1,0:T(8,128)S(1)}, u32[]{:S(2)}, u32[]{:S(2)}) %collective-permute-start.21) | collective-permute-done | bytes 10272 | tf_op jit(solution)/shard_map/ppermute | solution.py:16
  219.9 14.3 %collective-permute-done.12 = bf16[512,5,128]{2,0,1:T(8,128)(2,1)S(1)} collective-permute-done((bf16[512,5,128]{2,0,1:T(8,128)(2,1)S(1)}, bf16[512,5,128]{2,0,1:T(8,128)(2,1)S(1)}, u32[]{:S(2)}, u32[]{:S(2)}) %collective-permute-start.12) | collective-permute-done | bytes 655392 | tf_op jit(solution)/shard_map/ppermute | solution.py:16
  235.2 9.9 %collective-permute-start.14 = (f32[5,512]{1,0:T(8,128)S(1)}, f32[5,512]{1,0:T(8,128)S(1)}, u32[]{:S(2)}, u32[]{:S(2)}) collective-permute-start(f32[5,512]{1,0:T(8,128)S(1)} %get-tuple-element.10), channel_id=1, source_target_pairs={{124,0},{0,4},{4,8},{8,12},{12,16},{16,20},{20,24},{24,28},{28,32}... | collective-permute-start | bytes 30728 | tf_op jit(solution)/shard_map/ppermute | solution.py:16
  245.2 2.0 multiply_add_fusion.1
  247.3 1.1 fusion.8
  248.5 12.9 %collective-permute-done.15 = bf16[512,5,128]{2,0,1:T(8,128)(2,1)S(1)} collective-permute-done((bf16[512,5,128]{2,0,1:T(8,128)(2,1)S(1)}, bf16[512,5,128]{2,0,1:T(8,128)(2,1)S(1)}, u32[]{:S(2)}, u32[]{:S(2)}) %collective-permute-start.15) | collective-permute-done | bytes 655392 | tf_op jit(solution)/shard_map/ppermute | solution.py:16
  262.6 1.1 fusion.10
  263.7 25.7 %collective-permute-done.13 = f32[512,5,128]{2,0,1:T(8,128)S(1)} collective-permute-done((f32[512,5,128]{2,0,1:T(8,128)S(1)}, f32[512,5,128]{2,0,1:T(8,128)S(1)}, u32[]{:S(2)}, u32[]{:S(2)}) %collective-permute-start.13) | collective-permute-done | bytes 1310752 | tf_op jit(solution)/shard_map/ppermute | solution.py:16
  289.5 2.0 multiply_add_fusion
  291.6 12.6 %collective-permute-done.18 = bf16[512,5,128]{2,0,1:T(8,128)(2,1)S(1)} collective-permute-done((bf16[512,5,128]{2,0,1:T(8,128)(2,1)S(1)}, bf16[512,5,128]{2,0,1:T(8,128)(2,1)S(1)}, u32[]{:S(2)}, u32[]{:S(2)}) %collective-permute-start.18) | collective-permute-done | bytes 655392 | tf_op jit(solution)/shard_map/ppermute | solution.py:16
  305.3 1.1 fusion.12
  306.4 26.2 %collective-permute-done.24 = f32[5,512]{1,0:T(8,128)S(1)} collective-permute-done((f32[5,512]{1,0:T(8,128)S(1)}, f32[5,512]{1,0:T(8,128)S(1)}, u32[]{:S(2)}, u32[]{:S(2)}) %collective-permute-start.24) | collective-permute-done | bytes 10272 | tf_op jit(solution)/shard_map/ppermute | solution.py:16
  332.7 2.3 divide_convert_fusion
  335.1 10.8 %collective-permute-done.25 = bf16[512,5,128]{2,0,1:T(8,128)(2,1)S(1)} collective-permute-done((bf16[512,5,128]{2,0,1:T(8,128)(2,1)S(1)}, bf16[512,5,128]{2,0,1:T(8,128)(2,1)S(1)}, u32[]{:S(2)}, u32[]{:S(2)}) %collective-permute-start.25) | collective-permute-done | bytes 655392 | tf_op jit(solution)/shard_map/ppermute | solution.py:16
  345.9 6.8 %convolution_bitcast_fusion = f32[512,5120]{1,0:T(8,128)} fusion(bf16[512,5,128]{2,0,1:T(8,128)(2,1)S(1)} %collective-permute-done.25, bf16[5,128,5120]{2,1,0:T(8,128)(2,1)S(1)} %bitcast.149), kind=kOutput, calls=%fused_computation | convolution fusion | flops 3355443200 | bytes 17694720 | tf_op jit(solution)/shard_map/dot_general | solution.py:81
  352.8 104.3 %reduce-scatter.2.cloned.1.call-done = f32[512,1280]{1,0:T(8,128)} async-done(((f32[512,5120]{1,0:T(8,128)}), f32[512,1280]{1,0:T(8,128)}) %reduce-scatter.2.cloned.1.call-update) | async-done | bytes 2621456 | tf_op jit(solution)/shard_map/reduce_scatter | solution.py:82
  457.1 2.9 convert_element_type.35
  (100 shorter events, 15.2 us)
Async XLA Ops:
  6.5 18.4 %copy-start = (bf16[512,5,128]{2,0,1:T(8,128)(2,1)S(1)}, bf16[512,5,128]{2,0,1:T(8,128)(2,1)}, u32[]{:S(2)}) copy-start(bf16[512,5,128]{2,0,1:T(8,128)(2,1)} %param.6) | copy-start | bytes 1966084
  6.5 450.5 %reduce-scatter.2.cloned.1.call-start = ((), (), s32[]{:S(2)}) async-start(), calls=%async_computation.1 | async-start | bytes 13107200 | tf_op jit(solution)/shard_map/reduce_scatter | solution.py:82
  6.5 18.4 %collective-permute-start = (bf16[512,5,128]{2,0,1:T(8,128)(2,1)}, bf16[512,5,128]{2,0,1:T(8,128)(2,1)S(1)}, u32[]{:S(2)}, u32[]{:S(2)}) collective-permute-start(bf16[512,5,128]{2,0,1:T(8,128)(2,1)} %param.5), channel_id=1, source_target_pairs={{12,0},{16,4},{20,8},{24,12},{28,16},{32,20},{36,24},{40,28},{44,3... | collective-permute-start | bytes 1966088 | tf_op jit(solution)/shard_map/ppermute | solution.py:16
  29.9 50.5 %collective-permute-start.1 = (f32[512,5,128]{2,0,1:T(8,128)}, f32[512,5,128]{2,0,1:T(8,128)}, u32[]{:S(2)}, u32[]{:S(2)}) collective-permute-start(f32[512,5,128]{2,0,1:T(8,128)} %fusion.77), channel_id=1, source_target_pairs={{124,0},{0,4},{4,8},{8,12},{12,16},{16,20},{20,24},{24,28},{28,32}... | collective-permute-start | bytes 3932168 | tf_op jit(solution)/shard_map/ppermute | solution.py:16
  30.5 48.9 %collective-permute-start.3 = (bf16[512,5,128]{2,0,1:T(8,128)(2,1)S(1)}, bf16[512,5,128]{2,0,1:T(8,128)(2,1)S(1)}, u32[]{:S(2)}, u32[]{:S(2)}) collective-permute-start(bf16[512,5,128]{2,0,1:T(8,128)(2,1)S(1)} %collective-permute-done), channel_id=1, source_target_pairs={{124,0},{0,4},{4,8},{8,12},{12,16},{16,20},{20,24},{24,28},{28,32}... | collective-permute-start | bytes 1966088 | tf_op jit(solution)/shard_map/ppermute | solution.py:16
  32.3 48.1 %collective-permute-start.2 = (f32[5,512]{1,0:T(8,128)S(1)}, f32[5,512]{1,0:T(8,128)S(1)}, u32[]{:S(2)}, u32[]{:S(2)}) collective-permute-start(f32[5,512]{1,0:T(8,128)S(1)} %broadcast_maximum_fusion), channel_id=1, source_target_pairs={{124,0},{0,4},{4,8},{8,12},{12,16},{16,20},{20,24},{24,28},{28,32}... | collective-permute-start | bytes 30728 | tf_op jit(solution)/shard_map/ppermute | solution.py:16
  86.5 49.0 %collective-permute-start.4 = (f32[512,5,128]{2,0,1:T(8,128)}, f32[512,5,128]{2,0,1:T(8,128)}, u32[]{:S(2)}, u32[]{:S(2)}) collective-permute-start(f32[512,5,128]{2,0,1:T(8,128)} %multiply_add_fusion.4), channel_id=1, source_target_pairs={{124,0},{0,4},{4,8},{8,12},{12,16},{16,20},{20,24},{24,28},{28,32}... | collective-permute-start | bytes 3932168 | tf_op jit(solution)/shard_map/ppermute | solution.py:16
  86.5 47.9 %collective-permute-start.6 = (bf16[512,5,128]{2,0,1:T(8,128)(2,1)S(1)}, bf16[512,5,128]{2,0,1:T(8,128)(2,1)S(1)}, u32[]{:S(2)}, u32[]{:S(2)}) collective-permute-start(bf16[512,5,128]{2,0,1:T(8,128)(2,1)S(1)} %collective-permute-done.3), channel_id=1, source_target_pairs={{124,0},{0,4},{4,8},{8,12},{12,16},{16,20},{20,24},{24,28},{28,32}... | collective-permute-start | bytes 1966088 | tf_op jit(solution)/shard_map/ppermute | solution.py:16
  88.5 47.0 %copy-start.3 = (bf16[512,5,128]{2,0,1:T(8,128)(2,1)S(1)}, bf16[512,5,128]{2,0,1:T(8,128)(2,1)}, u32[]{:S(2)}) copy-start(bf16[512,5,128]{2,0,1:T(8,128)(2,1)} %param.7) | copy-start | bytes 1966084
  88.9 51.2 %collective-permute-start.19 = (f32[5,512]{1,0:T(8,128)S(1)}, f32[5,512]{1,0:T(8,128)S(1)}, u32[]{:S(2)}, u32[]{:S(2)}) collective-permute-start(f32[5,512]{1,0:T(8,128)S(1)} %get-tuple-element.24), channel_id=1, source_target_pairs={{124,0},{0,4},{4,8},{8,12},{12,16},{16,20},{20,24},{24,28},{28,32}... | collective-permute-start | bytes 30728 | tf_op jit(solution)/shard_map/ppermute | solution.py:16
  89.0 46.5 %collective-permute-start.5 = (f32[5,512]{1,0:T(8,128)S(1)}, f32[5,512]{1,0:T(8,128)S(1)}, u32[]{:S(2)}, u32[]{:S(2)}) collective-permute-start(f32[5,512]{1,0:T(8,128)S(1)} %get-tuple-element.16), channel_id=1, source_target_pairs={{124,0},{0,4},{4,8},{8,12},{12,16},{16,20},{20,24},{24,28},{28,32}... | collective-permute-start | bytes 30728 | tf_op jit(solution)/shard_map/ppermute | solution.py:16
  135.5 3.4 slice-start
  138.8 47.5 %collective-permute-start.7 = (f32[512,5,128]{2,0,1:T(8,128)S(1)}, f32[512,5,128]{2,0,1:T(8,128)S(1)}, u32[]{:S(2)}, u32[]{:S(2)}) collective-permute-start(f32[512,5,128]{2,0,1:T(8,128)S(1)} %multiply_add_fusion.3), channel_id=1, source_target_pairs={{124,0},{0,4},{4,8},{8,12},{12,16},{16,20},{20,24},{24,28},{28,32}... | collective-permute-start | bytes 3932168 | tf_op jit(solution)/shard_map/ppermute | solution.py:16
  140.0 45.2 %collective-permute-start.9 = (bf16[512,5,128]{2,0,1:T(8,128)(2,1)S(1)}, bf16[512,5,128]{2,0,1:T(8,128)(2,1)S(1)}, u32[]{:S(2)}, u32[]{:S(2)}) collective-permute-start(bf16[512,5,128]{2,0,1:T(8,128)(2,1)S(1)} %collective-permute-done.6), channel_id=1, source_target_pairs={{124,0},{0,4},{4,8},{8,12},{12,16},{16,20},{20,24},{24,28},{28,32}... | collective-permute-start | bytes 1966088 | tf_op jit(solution)/shard_map/ppermute | solution.py:16
  140.1 48.3 %collective-permute-start.20 = (f32[5,512]{1,0:T(8,128)S(1)}, f32[5,512]{1,0:T(8,128)S(1)}, u32[]{:S(2)}, u32[]{:S(2)}) collective-permute-start(f32[5,512]{1,0:T(8,128)S(1)} %multiply_add_fusion.9), channel_id=1, source_target_pairs={{124,0},{0,4},{4,8},{8,12},{12,16},{16,20},{20,24},{24,28},{28,32}... | collective-permute-start | bytes 30728 | tf_op jit(solution)/shard_map/ppermute | solution.py:16
  140.2 46.1 %collective-permute-start.8 = (f32[5,512]{1,0:T(8,128)S(1)}, f32[5,512]{1,0:T(8,128)S(1)}, u32[]{:S(2)}, u32[]{:S(2)}) collective-permute-start(f32[5,512]{1,0:T(8,128)S(1)} %get-tuple-element.14), channel_id=1, source_target_pairs={{124,0},{0,4},{4,8},{8,12},{12,16},{16,20},{20,24},{24,28},{28,32}... | collective-permute-start | bytes 30728 | tf_op jit(solution)/shard_map/ppermute | solution.py:16
  188.3 56.9 %collective-permute-start.10 = (f32[512,5,128]{2,0,1:T(8,128)S(1)}, f32[512,5,128]{2,0,1:T(8,128)S(1)}, u32[]{:S(2)}, u32[]{:S(2)}) collective-permute-start(f32[512,5,128]{2,0,1:T(8,128)S(1)} %multiply_add_fusion.2), channel_id=1, source_target_pairs={{124,0},{0,4},{4,8},{8,12},{12,16},{16,20},{20,24},{24,28},{28,32}... | collective-permute-start | bytes 3932168 | tf_op jit(solution)/shard_map/ppermute | solution.py:16
  188.4 31.4 %collective-permute-start.21 = (f32[5,512]{1,0:T(8,128)S(1)}, f32[5,512]{1,0:T(8,128)S(1)}, u32[]{:S(2)}, u32[]{:S(2)}) collective-permute-start(f32[5,512]{1,0:T(8,128)S(1)} %multiply_add_fusion.8), channel_id=1, source_target_pairs={{124,0},{0,4},{4,8},{8,12},{12,16},{16,20},{20,24},{24,28},{28,32}... | collective-permute-start | bytes 30728 | tf_op jit(solution)/shard_map/ppermute | solution.py:16
  188.5 46.7 %collective-permute-start.11 = (f32[5,512]{1,0:T(8,128)S(1)}, f32[5,512]{1,0:T(8,128)S(1)}, u32[]{:S(2)}, u32[]{:S(2)}) collective-permute-start(f32[5,512]{1,0:T(8,128)S(1)} %get-tuple-element.12), channel_id=1, source_target_pairs={{124,0},{0,4},{4,8},{8,12},{12,16},{16,20},{20,24},{24,28},{28,32}... | collective-permute-start | bytes 30728 | tf_op jit(solution)/shard_map/ppermute | solution.py:16
  188.6 45.6 %collective-permute-start.12 = (bf16[512,5,128]{2,0,1:T(8,128)(2,1)S(1)}, bf16[512,5,128]{2,0,1:T(8,128)(2,1)S(1)}, u32[]{:S(2)}, u32[]{:S(2)}) collective-permute-start(bf16[512,5,128]{2,0,1:T(8,128)(2,1)S(1)} %collective-permute-done.9), channel_id=1, source_target_pairs={{124,0},{0,4},{4,8},{8,12},{12,16},{16,20},{20,24},{24,28},{28,32}... | collective-permute-start | bytes 1966088 | tf_op jit(solution)/shard_map/ppermute | solution.py:16
  219.8 28.6 %collective-permute-start.22 = (f32[5,512]{1,0:T(8,128)S(1)}, f32[5,512]{1,0:T(8,128)S(1)}, u32[]{:S(2)}, u32[]{:S(2)}) collective-permute-start(f32[5,512]{1,0:T(8,128)S(1)} %multiply_add_fusion.7), channel_id=1, source_target_pairs={{124,0},{0,4},{4,8},{8,12},{12,16},{16,20},{20,24},{24,28},{28,32}... | collective-permute-start | bytes 30728 | tf_op jit(solution)/shard_map/ppermute | solution.py:16
  235.2 27.2 %collective-permute-start.14 = (f32[5,512]{1,0:T(8,128)S(1)}, f32[5,512]{1,0:T(8,128)S(1)}, u32[]{:S(2)}, u32[]{:S(2)}) collective-permute-start(f32[5,512]{1,0:T(8,128)S(1)} %get-tuple-element.10), channel_id=1, source_target_pairs={{124,0},{0,4},{4,8},{8,12},{12,16},{16,20},{20,24},{24,28},{28,32}... | collective-permute-start | bytes 30728 | tf_op jit(solution)/shard_map/ppermute | solution.py:16
  245.1 16.3 %collective-permute-start.15 = (bf16[512,5,128]{2,0,1:T(8,128)(2,1)S(1)}, bf16[512,5,128]{2,0,1:T(8,128)(2,1)S(1)}, u32[]{:S(2)}, u32[]{:S(2)}) collective-permute-start(bf16[512,5,128]{2,0,1:T(8,128)(2,1)S(1)} %collective-permute-done.12), channel_id=1, source_target_pairs={{124,0},{0,4},{4,8},{8,12},{12,16},{16,20},{20,24},{24,28},{28,32}... | collective-permute-start | bytes 1966088 | tf_op jit(solution)/shard_map/ppermute | solution.py:16
  247.2 42.3 %collective-permute-start.13 = (f32[512,5,128]{2,0,1:T(8,128)S(1)}, f32[512,5,128]{2,0,1:T(8,128)S(1)}, u32[]{:S(2)}, u32[]{:S(2)}) collective-permute-start(f32[512,5,128]{2,0,1:T(8,128)S(1)} %multiply_add_fusion.1), channel_id=1, source_target_pairs={{124,0},{0,4},{4,8},{8,12},{12,16},{16,20},{20,24},{24,28},{28,32}... | collective-permute-start | bytes 3932168 | tf_op jit(solution)/shard_map/ppermute | solution.py:16
  248.4 43.1 %collective-permute-start.23 = (f32[5,512]{1,0:T(8,128)S(1)}, f32[5,512]{1,0:T(8,128)S(1)}, u32[]{:S(2)}, u32[]{:S(2)}) collective-permute-start(f32[5,512]{1,0:T(8,128)S(1)} %multiply_add_fusion.6), channel_id=1, source_target_pairs={{124,0},{0,4},{4,8},{8,12},{12,16},{16,20},{20,24},{24,28},{28,32}... | collective-permute-start | bytes 30728 | tf_op jit(solution)/shard_map/ppermute | solution.py:16
  262.5 42.8 %collective-permute-start.17 = (f32[5,512]{1,0:T(8,128)S(1)}, f32[5,512]{1,0:T(8,128)S(1)}, u32[]{:S(2)}, u32[]{:S(2)}) collective-permute-start(f32[5,512]{1,0:T(8,128)S(1)} %get-tuple-element.8), channel_id=1, source_target_pairs={{124,0},{0,4},{4,8},{8,12},{12,16},{16,20},{20,24},{24,28},{28,32}... | collective-permute-start | bytes 30728 | tf_op jit(solution)/shard_map/ppermute | solution.py:16
  262.6 41.7 %collective-permute-start.18 = (bf16[512,5,128]{2,0,1:T(8,128)(2,1)S(1)}, bf16[512,5,128]{2,0,1:T(8,128)(2,1)S(1)}, u32[]{:S(2)}, u32[]{:S(2)}) collective-permute-start(bf16[512,5,128]{2,0,1:T(8,128)(2,1)S(1)} %collective-permute-done.15), channel_id=1, source_target_pairs={{124,0},{0,4},{4,8},{8,12},{12,16},{16,20},{20,24},{24,28},{28,32}... | collective-permute-start | bytes 1966088 | tf_op jit(solution)/shard_map/ppermute | solution.py:16
  291.4 41.2 %collective-permute-start.16 = (f32[512,5,128]{2,0,1:T(8,128)S(1)}, f32[512,5,128]{2,0,1:T(8,128)S(1)}, u32[]{:S(2)}, u32[]{:S(2)}) collective-permute-start(f32[512,5,128]{2,0,1:T(8,128)S(1)} %multiply_add_fusion), channel_id=1, source_target_pairs={{124,0},{0,4},{4,8},{8,12},{12,16},{16,20},{20,24},{24,28},{28,32}... | collective-permute-start | bytes 3932168 | tf_op jit(solution)/shard_map/ppermute | solution.py:16
  291.6 41.1 %collective-permute-start.24 = (f32[5,512]{1,0:T(8,128)S(1)}, f32[5,512]{1,0:T(8,128)S(1)}, u32[]{:S(2)}, u32[]{:S(2)}) collective-permute-start(f32[5,512]{1,0:T(8,128)S(1)} %multiply_add_fusion.5), channel_id=1, source_target_pairs={{124,0},{0,4},{4,8},{8,12},{12,16},{16,20},{20,24},{24,28},{28,32}... | collective-permute-start | bytes 30728 | tf_op jit(solution)/shard_map/ppermute | solution.py:16
  305.3 40.6 %slice-start.2 = ((s8[6553600]{0:T(1024)(128)(4,1)}), s8[4194304]{0:T(1024)(128)(4,1)S(1)}, s32[]{:S(2)}) async-start(s8[6553600]{0:T(1024)(128)(4,1)} %bitcast.148), calls=%async_computation.4 | async-start | bytes 8388608
  332.7 13.3 %slice-start.3 = ((s8[6553600]{0:T(1024)(128)(4,1)}), s8[2359296]{0:T(1024)(128)(4,1)S(1)}, s32[]{:S(2)}) async-start(s8[6553600]{0:T(1024)(128)(4,1)} %bitcast.148), calls=%async_computation.5 | async-start | bytes 4718592
  335.0 10.9 %collective-permute-start.25 = (bf16[512,5,128]{2,0,1:T(8,128)(2,1)S(1)}, bf16[512,5,128]{2,0,1:T(8,128)(2,1)S(1)}, u32[]{:S(2)}, u32[]{:S(2)}) collective-permute-start(bf16[512,5,128]{2,0,1:T(8,128)(2,1)S(1)} %divide_convert_fusion), channel_id=1, source_target_pairs={{12,0},{16,4},{20,8},{24,12},{28,16},{32,20},{36,24},{40,28},{44,3... | collective-permute-start | bytes 1966088 | tf_op jit(solution)/shard_map/ppermute | solution.py:16
  (3 other events, 7.8 us)
Sparse Core Ops, SparseCore 0:
  352.9 104.1 reduce-scatter.1
where the time goes:
time: 471 us; the launch traced here: 467 us
  waiting for transfers between devices  385 us (82%)
  matrix products  32.2 us (7%)
  starting transfers between devices  18.5 us (4%)
  between operations  14.3 us (3%)
  other arithmetic  11.7 us (2%)
  local copies, waits for them, and re-layouts  5.43 us (1%)
    ppermute x26, waiting for transfers between devices, shifted(): return lax.ppermute(block, axis, route)  281 us
    reduce_scatter x1, waiting for transfers between devices, local(): lax.psum_scatter(partial_value, 'head', scatter_dimension=1, tiled=True)  104 us
    ppermute x26, starting transfers between devices, shifted(): return lax.ppermute(block, axis, route)  18.5 us
    dot_general x7, matrix products, update(): jnp.einsum('hqk,khe->qhe', weights.astype(jnp.bfloat16), value_rows, pref...  18.1 us
  transfers between devices with their start and end apart: 27, of which 12 were waited for; matrix products, arithmetic and copies ran while one was open for 6% of the time, Pallas kernels for 0%

commit v1 on v0

v1 whole, which is shorter than its diff:
```python
import functools

import jax
import jax.numpy as jnp
from jax import lax
from jax.experimental import pallas as pl
from jax.experimental.pallas import tpu as pltpu
from jax.sharding import PartitionSpec as P

TILE = 128
SLAB = 8
ROW = 4
NEG = -1e30
LOG2E = 1.4426950408889634
AXES = ("seq", "head")
VMEM_LIMIT = 56 * 1024 * 1024


def route(rows, target):
    pairs = []
    for row in range(rows):
        for z in range(ROW):
            for yl in range(2):
                for c in range(2):
                    to = target(row, z, yl, c)
                    if to is not None:
                        dst = ((to[0] * ROW + to[1]) * 2 + to[2]) * 2 + to[3]
                        pairs.append((((row * ROW + z) * 2 + yl) * 2 + c, dst))
    return pairs


def send(block, rows, target):
    return lax.ppermute(block, AXES, route(rows, target))


def along_z(blocks, rows):
    plus, two, minus = (
        send(blocks[j - 1], rows, lambda r, z, yl, c, j=j: (r, (z + j) % ROW, yl, c)) for j in (1, 2, 3)
    )
    return [minus, two, plus]


def after(first, *then):
    tied = lax.optimization_barrier((tuple(first), tuple(then)))
    return list(tied[0]), list(tied[1])


def tile_places(tile_mask, row):
    padded = jnp.pad(tile_mask, SLAB)
    near = lax.dynamic_slice(padded, (row * 2 * SLAB, row * 2 * SLAB), (4 * SLAB, 4 * SLAB))
    live = (near > 0).astype(jnp.int32)
    grid = live.reshape(4, SLAB, 4, SLAB)
    within = jnp.stack([grid[t, :, t, :] for t in range(4)])
    degree = jnp.sum(within, axis=-1)
    ids = jnp.arange(SLAB, dtype=jnp.int32)
    edge = degree == 4
    first = jnp.min(jnp.where(edge[1], ids, SLAB))
    side_one = jnp.sum(jnp.where((ids == first)[:, None], live[SLAB : 2 * SLAB], 0), axis=0).reshape(4, SLAB)
    second = jnp.min(jnp.where(edge[2] & (side_one[2] > 0), ids, SLAB))
    side_two = jnp.sum(jnp.where((ids == second)[:, None], live[2 * SLAB : 3 * SLAB], 0), axis=0).reshape(4, SLAB)
    side = jnp.concatenate([side_one[:3], side_two[3:]]) > 0
    column = jnp.where(side, jnp.where(edge, 0, 1), jnp.where(edge, 3, 2))
    same = (column[:, :, None] == column[:, None, :]) & (ids[None, :] < ids[:, None])[None]
    place = column * 2 + jnp.sum(same.astype(jnp.int32), axis=-1)
    place = jnp.where(degree == 0, ids[None, :], place)
    return jnp.clip(place, 0, SLAB - 1).reshape(4 * SLAB)


ANYWHERE = pl.BlockSpec(memory_space=pltpu.VMEM)
SCALARS = pl.BlockSpec(memory_space=pltpu.SMEM)


def call(kernel, outs, scratch, operands, scalars, flops=0, moved=0, exps=0):
    return pl.pallas_call(
        kernel,
        out_shape=outs,
        in_specs=[SCALARS] * scalars + [ANYWHERE] * (len(operands) - scalars),
        out_specs=jax.tree.map(lambda _: ANYWHERE, outs),
        scratch_shapes=scratch,
        compiler_params=pltpu.CompilerParams(vmem_limit_bytes=VMEM_LIMIT),
        cost_estimate=pl.CostEstimate(flops=flops, bytes_accessed=moved, transcendentals=exps),
    )(*operands)


def pick_kernel(where_ref, own, one, two, three, up, down):
    z = where_ref[0]
    for at in range(ROW):

        @pl.when(z == at)
        def _():
            ring = (own, one, two, three)
            up[0] = ring[(2 - at) % ROW][...]
            up[1] = ring[(3 - at) % ROW][...]
            down[0] = ring[(0 - at) % ROW][...]
            down[1] = ring[(1 - at) % ROW][...]


def pick_one_kernel(where_ref, own, one, two, three, out):
    z = where_ref[0]
    for at in range(ROW):

        @pl.when(z == at)
        def _():
            ring = (own, one, two, three)
            base = 2 if at < 2 else 0
            out[0] = ring[(base - at) % ROW][...]
            out[1] = ring[(base + 1 - at) % ROW][...]


def spot(index):
    return pl.ds(pl.multiple_of(index * TILE, TILE), TILE)


def spread(where_ref, place_ref, ring, targets):
    z = where_ref[0]
    for j in range(ROW):
        block = lax.rem(z + j, ROW)
        for i in range(4):
            at = spot((block // 2) * SLAB + place_ref[SLAB + block * 4 + i])
            for target, piece in zip(targets, ring[j]):
                target[at, :] = piece[i * TILE : (i + 1) * TILE, :]


def softmax_rows(q, parts, valid, scale):
    scores = [
        lax.dot_general(q, keys, (((1,), (1,)), ((), ())), preferred_element_type=jnp.float32) for keys, _ in parts
    ]
    tops = [jnp.max(s, axis=-1, keepdims=True) for s in scores]
    tops[-1] = jnp.where(valid, tops[-1], NEG)
    top = functools.reduce(jnp.maximum, tops)
    total, summed = 0.0, 0.0
    for at, (s, (_, values)) in enumerate(zip(scores, parts)):
        weights = jnp.exp2((s - top) * (scale * LOG2E))
        part_total = jnp.sum(weights, axis=-1, keepdims=True)
        part_sum = jnp.dot(weights.astype(jnp.bfloat16), values, preferred_element_type=jnp.float32)
        if at == len(parts) - 1:
            part_total = jnp.where(valid, part_total, 0.0)
            part_sum = jnp.where(valid, part_sum, 0.0)
        total, summed = total + part_total, summed + part_sum
    return summed / total


WINDOW = ((0, 512), (0, 768), (256, 1024), (512, 1024))


def main_kernel(
    where_ref, place_ref, kv0, kv1, kv2, kv3, q0, q1, q2, q3, up, down, o0, o1, o2, o3, ks, vs, qs, os
):
    scale = q0.shape[-1] ** -0.5
    ring = [(kv.at[0], kv.at[1], q) for kv, q in zip((kv0, kv1, kv2, kv3), (q0, q1, q2, q3))]
    spread(where_ref, place_ref, ring, (ks.at[1024:3072], vs.at[1024:3072], qs))
    for side, first, slab in ((up, 0, 0), (down, 24, 3)):
        for b in range(2):
            for i in range(4):
                at = spot(slab * SLAB + place_ref[first + b * 4 + i])
                rows = slice(i * TILE, (i + 1) * TILE)
                ks[at, :] = side[b, 0, rows, :]
                vs[at, :] = side[b, 1, rows, :]
    for s in range(2):
        valid = where_ref[1 + s] > 0
        order = (1, 2, 0) if s == 0 else (1, 2, 3)
        for column, (low, high) in enumerate(WINDOW):
            rows = slice(s * 1024 + column * 256, s * 1024 + column * 256 + 256)
            parts = [(ks[t * 1024 + low : t * 1024 + high, :], vs[t * 1024 + low : t * 1024 + high, :]) for t in order]
            os[rows, :] = softmax_rows(qs[rows, :], parts, valid, scale).astype(jnp.bfloat16)
    z = where_ref[0]
    for j, out in enumerate((o0, o1, o2, o3)):
        block = lax.rem(z + j, ROW)
        for i in range(4):
            at = spot((block // 2) * SLAB + place_ref[SLAB + block * 4 + i])
            out[i * TILE : (i + 1) * TILE, :] = os[at, :]


def rest_kernel(where_ref, place_ref, kv0, kv1, kv2, kv3, q, halo, out, ks, vs):
    scale = q.shape[-1] ** -0.5
    z = where_ref[0]
    ring = [(kv.at[0], kv.at[1]) for kv in (kv0, kv1, kv2, kv3)]
    spread(where_ref, place_ref, ring, (ks.at[0:2048], vs.at[0:2048]))
    first = jnp.where(z < 2, 0, 24)
    valid = jnp.where(z < 2, where_ref[1], where_ref[2]) > 0
    for b in range(2):
        for i in range(4):
            at = spot(2 * SLAB + place_ref[first + b * 4 + i])
            rows = slice(i * TILE, (i + 1) * TILE)
            ks[at, :] = halo[b, 0, rows, :]
            vs[at, :] = halo[b, 1, rows, :]

    @pl.loop(0, 4)
    def _(i):
        column = place_ref[SLAB + z * 4 + i] // 2
        low = jnp.maximum(column - 1, 0) * 256
        here = spot(i)
        edge = (column == 0) | (column == 3)

        def work(width):
            parts = []
            for t in range(3):
                at = pl.ds(pl.multiple_of(t * 1024 + low, 256), width)
                parts.append((ks[at, :], vs[at, :]))
            out[here, :] = softmax_rows(q[here, :], parts, valid, scale).astype(jnp.bfloat16)

        @pl.when(edge)
        def _():
            work(512)

        @pl.when(jnp.logical_not(edge))
        def _():
            work(768)


def place_heads(z, main, rest, wide, base):
    for j in range(ROW):
        head = lax.rem(z + j, ROW)
        at = pl.multiple_of(base + head * TILE, TILE)
        wide[:, pl.ds(at, TILE)] = main[j]
    wide[:, base + ROW * TILE : base + (ROW + 1) * TILE] = rest[...]


def project_kernel(where_ref, m0, r0, w0, m1, r1, w1, out, wide):
    z = where_ref[0]
    place_heads(z, m0, r0, wide, 0)
    place_heads(z, m1, r1, wide, 640)

    @pl.loop(0, out.shape[1] // 256)
    def _(n):
        at = pl.ds(pl.multiple_of(n * 256, 256), 256)
        out[:, at] = jnp.dot(wide[:, :640], w0[:, at], preferred_element_type=jnp.float32) + jnp.dot(
            wide[:, 640:], w1[:, at], preferred_element_type=jnp.float32
        )


def finish_kernel(where_ref, m0, r0, w0, m1, r1, w1, before, out, wide):
    z = where_ref[0]
    place_heads(z, m0, r0, wide, 0)
    place_heads(z, m1, r1, wide, 640)

    @pl.loop(0, out.shape[1] // 256)
    def _(n):
        at = pl.ds(pl.multiple_of(n * 256, 256), 256)
        part = jnp.dot(wide[:, :640], w0[:, at], preferred_element_type=jnp.float32) + jnp.dot(
            wide[:, 640:], w1[:, at], preferred_element_type=jnp.float32
        )
        out[:, at] = (part + before[:, at]).astype(out.dtype)


def local(queries, key_rows, value_rows, out_weight, tile_mask):
    tok, heads, size = queries.shape
    rows = lax.axis_size("seq") // ROW
    seq, head = lax.axis_index("seq"), lax.axis_index("head")
    row, z = seq // ROW, seq % ROW
    yl, c = head // 2, head % 2
    bf = jnp.bfloat16
    wide_cols = out_weight.shape[-1] // 2
    cols = wide_cols // 2
    where = jnp.stack([z, (row > 0).astype(jnp.int32), (row < rows - 1).astype(jnp.int32), c]).astype(jnp.int32)

    with jax.named_scope("lay_out"):
        kv = jnp.stack([key_rows, value_rows]).transpose(2, 0, 1, 3)
        qh = queries.transpose(1, 0, 2)

    def ring_slices(array):
        return [lax.dynamic_index_in_dim(array, (z + j) % ROW, 0, keepdims=False) for j in range(ROW)]

    kv_own, *kv_out = ring_slices(kv)
    q_own, *q_out = ring_slices(qh)
    kv_rest, q_rest = kv[ROW], qh[ROW]

    with jax.named_scope("keys_values_z"):
        kv_in = along_z(kv_out, rows)
    with jax.named_scope("weights_y"):
        flat = out_weight.reshape(heads * size, 2 * wide_cols)
        theirs = lax.dynamic_slice_in_dim(flat, (1 - yl) * wide_cols, wide_cols, 1)

        def y_step(r, z, yl, c):
            yh, x = r // ROW, r % ROW
            y = (yh * 2 + yl + (1 if c == 0 else -1)) % 4
            return ((y // 2) * ROW + x, z, y % 2, c)

        w_far = send(theirs, rows, y_step)

    def sibling(block):
        return send(block, rows, lambda r, z, yl, c: (r, z, yl, 1 - c))

    with jax.named_scope("places"):
        place = tile_places(tile_mask, row)

    with jax.named_scope("queries_z"):
        kv_in, q_out = after(kv_in, *q_out)
        q_in = along_z(q_out, rows)
    with jax.named_scope("pick"):
        halo = jax.ShapeDtypeStruct((2, 2, tok, size), bf)
        to_next, to_prev = call(pick_kernel, (halo, halo), [], [where, kv_own, *kv_in], 1, moved=4 * 2**20)
    with jax.named_scope("keys_values_x"):
        from_prev = send(to_next, rows, lambda r, z, yl, c: (r + 1, z, yl, c) if r + 1 < rows else None)
        from_next = send(to_prev, rows, lambda r, z, yl, c: (r - 1, z, yl, c) if r > 0 else None)
    with jax.named_scope("rest_z"):
        q_in, (kv_rest_out,) = after(q_in, kv_rest)
        rest_in = along_z([kv_rest_out] * 3, rows)
    with jax.named_scope("main_attention"):
        block = jax.ShapeDtypeStruct((tok, size), bf)
        row_tok = ROW * tok
        o_own, *o_out = call(
            main_kernel,
            (block,) * 4,
            [
                pltpu.VMEM((2 * row_tok, size), bf),
                pltpu.VMEM((2 * row_tok, size), bf),
                pltpu.VMEM((row_tok, size), bf),
                pltpu.VMEM((row_tok, size), bf),
            ],
            [where, place, kv_own, *kv_in, q_own, *q_in, from_prev, from_next],
            2,
            flops=4 * 240 * TILE**3,
            moved=8 * 2**20,
            exps=240 * TILE**2,
        )
    with jax.named_scope("attended_z"):
        o_in = along_z(o_out, rows)
    with jax.named_scope("rest_pick"):
        to_rest = call(pick_one_kernel, halo, [], [where, kv_rest, *rest_in], 1, moved=2 * 2**20)
    with jax.named_scope("rest_x"):

        def rest_step(r, z, yl, c):
            to = r + 1 if z < 2 else r - 1
            return (to, z, yl, c) if 0 <= to < rows else None

        rest_halo = send(to_rest, rows, rest_step)
    with jax.named_scope("rest_attention"):
        o_rest = call(
            rest_kernel,
            block,
            [pltpu.VMEM((6 * tok, size), bf), pltpu.VMEM((6 * tok, size), bf)],
            [where, place, kv_rest, *rest_in, q_rest, rest_halo],
            2,
            flops=4 * 60 * TILE**3,
            moved=4 * 2**20,
            exps=60 * TILE**2,
        )

    def y_pair(block):
        return send(block, rows, lambda r, z, yl, c: (r, z, 1 - yl, c))

    main = jnp.stack([o_own, *o_in])
    with jax.named_scope("main_y"):
        main_far = y_pair(main)
    with jax.named_scope("main_core"):
        main_sib = sibling(main)
    with jax.named_scope("rest_y"):
        rest_far = y_pair(o_rest)
    with jax.named_scope("rest_core"):
        rest_sib = sibling(o_rest)
    with jax.named_scope("weights_core"):
        def halves(array, base):
            mine = lax.dynamic_slice_in_dim(array, base + c * cols, cols, 1)
            other = lax.dynamic_slice_in_dim(array, base + (1 - c) * cols, cols, 1)
            return mine, other

        w_own, w_own_other = halves(flat, yl * wide_cols)
        w_y, w_y_other = halves(w_far, 0)
        w_sib = sibling(w_own_other)
        w_y_sib = sibling(w_y_other)
    with jax.named_scope("main_far_core"):
        main_far_sib = sibling(main_far)
    with jax.named_scope("rest_far_core"):
        rest_far_sib = sibling(rest_far)
    wide = pltpu.VMEM((tok, 2 * heads * size), bf)
    with jax.named_scope("project"):
        near = call(
            project_kernel,
            jax.ShapeDtypeStruct((tok, cols), jnp.float32),
            [wide],
            [where, main, o_rest, w_own, main_sib, rest_sib, w_sib],
            1,
            flops=2 * tok * 2 * heads * size * cols,
            moved=8 * 2**20,
        )
    with jax.named_scope("finish"):
        return call(
            finish_kernel,
            jax.ShapeDtypeStruct((tok, cols), bf),
            [wide],
            [where, main_far, rest_far, w_y, main_far_sib, rest_far_sib, w_y_sib, near],
            1,
            flops=2 * tok * 2 * heads * size * cols,
            moved=8 * 2**20,
        )


def solution(mesh):
    placed = (
        P("seq", "head", None),
        P("seq", "head", None),
        P("seq", "head", None),
        P("head", None, None),
        P(),
    )
    return jax.shard_map(local, mesh=mesh, in_specs=placed, out_specs=P("seq", "head"), check_vma=False)
```

time: 471 us -> 146 us (0.31)
  waiting for transfers between devices: 385 us -> 36 us
  Pallas kernels: 0 us -> 32.5 us
  matrix products: 32.2 us -> 0 us
  starting transfers between devices: 18.5 us -> 43.5 us
  local copies, waits for them, and re-layouts: 5.43 us -> 22.8 us
  between operations: 14.3 us -> 0.23 us
    ppermute x26 -> x24, waiting for transfers between devices: 281 us -> 36 us  [send(): return lax.ppermute(block, AXES, route(rows, target))]
    reduce_scatter x1 -> x0, waiting for transfers between devices: 104 us -> none  [local(): lax.psum_scatter(partial_value, 'head', scatter_dimension=1, tiled=True)]
    pallas_call x0 -> x6, Pallas kernels: none -> 32.5 us  [call(): pl.pallas_call(kernel, out_shape=outs, in_specs=[SCALARS] * scalars + [AN...]
    dot_general x15 -> x0, matrix products: 32.2 us -> none  [the longest x7 18.1 us: update(): jnp.einsum('hqk,khe->qhe', weights.astype(jnp.bfloat16), value_rows, pref...]
    ppermute x26 -> x24, starting transfers between devices: 18.5 us -> 43.5 us  [send(): return lax.ppermute(block, AXES, route(rows, target))]
    dynamic_slice x0 -> x3, local copies, waits for them, and re-layouts: none -> 8.66 us  [the longest x2 4.83 us: halves(): other = lax.dynamic_slice_in_dim(array, base + (1 - c) * cols, cols, 1)]
    reduce_sum x7 -> x4, other arithmetic: 7.78 us -> 1.01 us  [the longest x1 0.56 us: tile_places(): jnp.sum(jnp.where((ids == first)[:, None], live[SLAB:2 * SLAB], 0), axis=0)]
  transfers between devices with their start and end apart: 27 -> 24, of which waited for: 12 -> 8; matrix products, arithmetic and copies ran while one was open for 6% -> 16% of each run, Pallas kernels for 0% -> 17%
where the time goes in v1:
time: 146 us; the launch traced here: 145 us
  starting transfers between devices  43.5 us (30%)
  waiting for transfers between devices  36 us (25%)
  Pallas kernels  32.5 us (22%)
  local copies, waits for them, and re-layouts  22.8 us (16%)
  other arithmetic  10.4 us (7%)
    ppermute x24, starting transfers between devices, send(): return lax.ppermute(block, AXES, route(rows, target))  43.5 us
    ppermute x24, waiting for transfers between devices, send(): return lax.ppermute(block, AXES, route(rows, target))  36 us
    pallas_call x6, Pallas kernels, call(): pl.pallas_call(kernel, out_shape=outs, in_specs=[SCALARS] * scalars + [AN...  32.5 us
    unnamed x42, local copies, waits for them, and re-layouts  6.67 us
    dynamic_slice x2, local copies, waits for them, and re-layouts, halves(): other = lax.dynamic_slice_in_dim(array, base + (1 - c) * cols, cols, 1)  4.83 us
    dynamic_slice x1, local copies, waits for them, and re-layouts, local(): theirs = lax.dynamic_slice_in_dim(flat, (1 - yl) * wide_cols, wide_cols, 1)  3.82 us
  transfers between devices with their start and end apart: 24, of which 8 were waited for; matrix products, arithmetic and copies ran while one was open for 16% of the time, Pallas kernels for 17%

profile of v1, /device:TPU:17, one launch (start us, length us, event | category | flops | bytes accessed | tf_op | source)
XLA Modules:
  0.0 145.4 jit_solution(14849095584048477679)
XLA Ops:
  0.0 3.8 %constant_dynamic-slice_fusion.3 = bf16[640,2560]{1,0:T(8,128)(2,1)} fusion(bf16[640,5120]{1,0:T(8,128)(2,1)} %bitcast.51, s32[]{:T(128)S(6)} %select_n.160), kind=kLoop, calls=%fused_computation.33 | loop fusion | bytes 6553604 | tf_op jit(solution)/shard_map/weights_y/dynamic_slice | solution.py:272
  4.0 2.3 %fusion.8 = (bf16[2,512,128]{2,1,0:T(8,128)(2,1)}, bf16[2,512,128]{2,1,0:T(8,128)(2,1)}, bf16[2,512,128]{2,1,0:T(8,128)(2,1)}, bf16[2,512,128]{2,1,0:T(8,128)(2,1)}) fusion(s32[]{:T(128)S(6)} %select_n.158, bf16[1,512,5,128]{3,1,0,2:T(8,128)(2,1)} %bitcast.53, bf16[1,512,5,128]{3,1,0,2:T(8,128)(2,1)} %bitcast.55, s32[]{:T(128)S(6)} %select_n.152, ...), kind=kLoop, calls=%fused_computation.18 | loop fusion | flops 524288 | bytes 2359312 | tf_op jit(solution)/shard_map/jit(dynamic_index_in_dim)/squeeze | solution.py:262
  6.3 3.8 %collective-permute-start = (bf16[2,512,128]{2,1,0:T(8,128)(2,1)}, bf16[2,512,128]{2,1,0:T(8,128)(2,1)S(1)}, u32[]{:S(2)}, u32[]{:S(2)}) collective-permute-start(bf16[2,512,128]{2,1,0:T(8,128)(2,1)} %get-tuple-element.43), channel_id=1, source_target_pairs={{0,12},{1,13},{2,14},{3,15},{4,0},{5,1},{6,2},{7,3},{8,4},{9,5},{1... | collective-permute-start | bytes 786440 | tf_op jit(solution)/shard_map/keys_values_z/ppermute | solution.py:33
  17.3 1.4 fusion.15
  22.3 1.8 %dynamic-slice_bitcast_fusion = (bf16[512,128]{1,0:T(8,128)(2,1)}, bf16[512,128]{1,0:T(8,128)(2,1)S(1)}, bf16[512,128]{1,0:T(8,128)(2,1)S(1)}, bf16[512,128]{1,0:T(8,128)(2,1)S(1)}) fusion(bf16[512,5,128]{2,0,1:T(8,128)(2,1)} %param.5, s32[]{:T(128)S(6)} %select_n.152, s32[]{:T(128)S(6)} %select_n.154, s32[]{:T(128)S(6)} %select_n.156, s32[]{:T(128)S(6)} %select_n.158), kind=kLoop, calls=%fused_computation.22 | loop fusion | bytes 1048592 | tf_op jit(solution)/shard_map/jit(dynamic_index_in_dim)/squeeze | solution.py:262
  24.1 3.4 %constant_dynamic-slice_fusion.4 = (bf16[640,1280]{1,0:T(8,128)(2,1)S(1)}, bf16[640,1280]{1,0:T(8,128)(2,1)}) fusion(bf16[640,5120]{1,0:T(8,128)(2,1)} %bitcast.52, s32[]{:T(128)S(6)} %select_n.164, s32[]{:T(128)S(6)} %select_n.163), kind=kLoop, calls=%fused_computation.34 | loop fusion | bytes 6553608 | tf_op jit(solution)/shard_map/weights_core/dynamic_slice | solution.py:355
  27.5 2.0 %collective-permute-start.3 = (bf16[512,128]{1,0:T(8,128)(2,1)S(1)}, bf16[512,128]{1,0:T(8,128)(2,1)S(1)}, u32[]{:S(2)}, u32[]{:S(2)}) collective-permute-start(bf16[512,128]{1,0:T(8,128)(2,1)S(1)} %get-tuple-element.24), channel_id=1, source_target_pairs={{0,12},{1,13},{2,14},{3,15},{4,0},{5,1},{6,2},{7,3},{8,4},{9,5},{1... | collective-permute-start | bytes 393224 | tf_op jit(solution)/shard_map/queries_z/ppermute | solution.py:33
  29.7 1.8 %collective-permute-start.4 = (bf16[512,128]{1,0:T(8,128)(2,1)S(1)}, bf16[512,128]{1,0:T(8,128)(2,1)S(1)}, u32[]{:S(2)}, u32[]{:S(2)}) collective-permute-start(bf16[512,128]{1,0:T(8,128)(2,1)S(1)} %get-tuple-element.25), channel_id=1, source_target_pairs={{0,8},{1,9},{2,10},{3,11},{4,12},{5,13},{6,14},{7,15},{8,0},{9,1},... | collective-permute-start | bytes 393224 | tf_op jit(solution)/shard_map/queries_z/ppermute | solution.py:33
  31.6 2.2 %pick.1 = (bf16[2,2,512,128]{3,2,1,0:T(8,128)(2,1)}, bf16[2,2,512,128]{3,2,1,0:T(8,128)(2,1)}) custom-call(s32[4]{0:T(128)} %pad_add_fusion.where_ref, bf16[2,512,128]{2,1,0:T(8,128)(2,1)} %get-tuple-element.42.own.kv0, bf16[2,512,128]{2,1,0:T(8,128)(2,1)} %copy-done.7, bf16[2,512,128]{2,1,0:T(8,128)(2,1)} %collective-permute-done.1.two.kv2, ...), custom_call_target="tpu_custom_call" | custom-call | bytes 4194304 | tf_op jit(solution)/shard_map/pick/pallas_call | solution.py:74
  33.8 3.1 %collective-permute-start.6 = (bf16[2,2,512,128]{3,2,1,0:T(8,128)(2,1)}, bf16[2,2,512,128]{3,2,1,0:T(8,128)(2,1)S(1)}, u32[]{:S(2)}, u32[]{:S(2)}) collective-permute-start(bf16[2,2,512,128]{3,2,1,0:T(8,128)(2,1)} %get-tuple-element.30), channel_id=1, source_target_pairs={{0,16},{1,17},{2,18},{3,19},{4,20},{5,21},{6,22},{7,23},{8,24},{9,... | collective-permute-start | bytes 1572872 | tf_op jit(solution)/shard_map/keys_values_x/ppermute | solution.py:33
  37.0 5.8 %collective-permute-start.7 = (bf16[2,2,512,128]{3,2,1,0:T(8,128)(2,1)}, bf16[2,2,512,128]{3,2,1,0:T(8,128)(2,1)S(1)}, u32[]{:S(2)}, u32[]{:S(2)}) collective-permute-start(bf16[2,2,512,128]{3,2,1,0:T(8,128)(2,1)} %get-tuple-element.31), channel_id=1, source_target_pairs={{16,0},{17,1},{18,2},{19,3},{20,4},{21,5},{22,6},{23,7},{24,8},{25... | collective-permute-start | bytes 1572872 | tf_op jit(solution)/shard_map/keys_values_x/ppermute | solution.py:33
  43.5 3.7 %collective-permute-start.23 = (bf16[640,1280]{1,0:T(8,128)(2,1)S(1)}, bf16[640,1280]{1,0:T(8,128)(2,1)S(1)}, u32[]{:S(2)}, u32[]{:S(2)}) collective-permute-start(bf16[640,1280]{1,0:T(8,128)(2,1)S(1)} %get-tuple-element.37), channel_id=1, source_target_pairs={{0,1},{1,0},{2,3},{3,2},{4,5},{5,4},{6,7},{7,6},{8,9},{9,8},{10,11... | collective-permute-start | bytes 4915208 | tf_op jit(solution)/shard_map/weights_core/ppermute | solution.py:33
  47.9 1.4 constant_dynamic-slice_fusion.1
  49.3 6.7 %collective-permute-start.20 = (bf16[640,1280]{1,0:T(8,128)(2,1)S(1)}, bf16[640,1280]{1,0:T(8,128)(2,1)S(1)}, u32[]{:S(2)}, u32[]{:S(2)}) collective-permute-start(bf16[640,1280]{1,0:T(8,128)(2,1)S(1)} %get-tuple-element.39), channel_id=1, source_target_pairs={{0,1},{1,0},{2,3},{3,2},{4,5},{5,4},{6,7},{7,6},{8,9},{9,8},{10,11... | collective-permute-start | bytes 4915208 | tf_op jit(solution)/shard_map/weights_core/ppermute | solution.py:33
  57.6 8.9 %main_attention.1 = (bf16[512,128]{1,0:T(8,128)(2,1)}, bf16[512,128]{1,0:T(8,128)(2,1)}, bf16[512,128]{1,0:T(8,128)(2,1)}, bf16[512,128]{1,0:T(8,128)(2,1)}) custom-call(s32[4]{0:T(128)} %pad_add_fusion.where_ref, s32[32]{0:T(128)} %reshape.134.place_ref, bf16[2,512,128]{2,1,0:T(8,128)(2,1)} %get-tuple-element.42.own.kv0, bf16[2,512,128]{2,1,0:T(8,128)(2,1)} %copy-done.7, ...), custom_call_target="tpu_custom_call" | custom-call | flops 2013265920 | bytes 8388608 | tf_op jit(solution)/shard_map/main_attention/pallas_call | solution.py:74
  66.6 3.8 %collective-permute-start.8 = (bf16[512,128]{1,0:T(8,128)(2,1)}, bf16[512,128]{1,0:T(8,128)(2,1)S(1)}, u32[]{:S(2)}, u32[]{:S(2)}) collective-permute-start(bf16[512,128]{1,0:T(8,128)(2,1)} %get-tuple-element.33), channel_id=1, source_target_pairs={{0,12},{1,13},{2,14},{3,15},{4,0},{5,1},{6,2},{7,3},{8,4},{9,5},{1... | collective-permute-start | bytes 393224 | tf_op jit(solution)/shard_map/attended_z/ppermute | solution.py:33
  70.5 3.1 %collective-permute-done.8 = bf16[512,128]{1,0:T(8,128)(2,1)S(1)} collective-permute-done((bf16[512,128]{1,0:T(8,128)(2,1)}, bf16[512,128]{1,0:T(8,128)(2,1)S(1)}, u32[]{:S(2)}, u32[]{:S(2)}) %collective-permute-start.8) | collective-permute-done | bytes 131104 | tf_op jit(solution)/shard_map/attended_z/ppermute | solution.py:33
  73.8 2.9 %collective-permute-done.9 = bf16[512,128]{1,0:T(8,128)(2,1)S(1)} collective-permute-done((bf16[512,128]{1,0:T(8,128)(2,1)}, bf16[512,128]{1,0:T(8,128)(2,1)S(1)}, u32[]{:S(2)}, u32[]{:S(2)}) %collective-permute-start.9) | collective-permute-done | bytes 131104 | tf_op jit(solution)/shard_map/attended_z/ppermute | solution.py:33
  76.7 1.4 collective-permute-start.13
  78.1 1.7 %collective-permute-done.10 = bf16[512,128]{1,0:T(8,128)(2,1)S(1)} collective-permute-done((bf16[512,128]{1,0:T(8,128)(2,1)}, bf16[512,128]{1,0:T(8,128)(2,1)S(1)}, u32[]{:S(2)}, u32[]{:S(2)}) %collective-permute-start.10) | collective-permute-done | bytes 131104 | tf_op jit(solution)/shard_map/attended_z/ppermute | solution.py:33
  79.8 4.0 %collective-permute-start.14 = (bf16[2,512,128]{2,1,0:T(8,128)(2,1)S(1)}, bf16[2,512,128]{2,1,0:T(8,128)(2,1)S(1)}, u32[]{:S(2)}, u32[]{:S(2)}) collective-permute-start(bf16[2,512,128]{2,1,0:T(8,128)(2,1)S(1)} %copy-done.5), channel_id=1, source_target_pairs={{0,4},{1,5},{2,6},{3,7},{4,8},{5,9},{6,10},{7,11},{8,12},{9,13},{1... | collective-permute-start | bytes 786440 | tf_op jit(solution)/shard_map/rest_z/ppermute | solution.py:33
  84.9 1.5 %collective-permute-done.13.two.kv2 = bf16[2,512,128]{2,1,0:T(8,128)(2,1)S(1)} collective-permute-done((bf16[2,512,128]{2,1,0:T(8,128)(2,1)S(1)}, bf16[2,512,128]{2,1,0:T(8,128)(2,1)S(1)}, u32[]{:S(2)}, u32[]{:S(2)}) %collective-permute-start.13) | collective-permute-done | bytes 262176 | tf_op jit(solution)/shard_map/rest_z/ppermute | solution.py:33
  86.4 6.9 %collective-permute-done.14.three.kv3 = bf16[2,512,128]{2,1,0:T(8,128)(2,1)S(1)} collective-permute-done((bf16[2,512,128]{2,1,0:T(8,128)(2,1)S(1)}, bf16[2,512,128]{2,1,0:T(8,128)(2,1)S(1)}, u32[]{:S(2)}, u32[]{:S(2)}) %collective-permute-start.14) | collective-permute-done | bytes 262176 | tf_op jit(solution)/shard_map/rest_z/ppermute | solution.py:33
  94.0 2.0 %rest_pick.1 = bf16[2,2,512,128]{3,2,1,0:T(8,128)(2,1)} custom-call(s32[4]{0:T(128)} %pad_add_fusion.where_ref, bf16[2,512,128]{2,1,0:T(8,128)(2,1)} %slice_bitcast_fusion.own.kv0, bf16[2,512,128]{2,1,0:T(8,128)(2,1)} %copy-done.8, bf16[2,512,128]{2,1,0:T(8,128)(2,1)} %copy-done.9, bf16[2,512,128]{2,1,0:T(8,128)(2,1)} %copy-done.10), custom_call_target="tpu_custom_call" | custom-call | bytes 2097152 | tf_op jit(solution)/shard_map/rest_pick/pallas_call | solution.py:74
  96.1 1.9 %collective-permute-start.15 = (bf16[2,2,512,128]{3,2,1,0:T(8,128)(2,1)}, bf16[2,2,512,128]{3,2,1,0:T(8,128)(2,1)}, u32[]{:S(2)}, u32[]{:S(2)}) collective-permute-start(bf16[2,2,512,128]{3,2,1,0:T(8,128)(2,1)} %rest_pick.1), channel_id=1, source_target_pairs={{0,16},{1,17},{2,18},{3,19},{4,20},{5,21},{6,22},{7,23},{16,32},{1... | collective-permute-start | bytes 1572872 | tf_op jit(solution)/shard_map/rest_x/ppermute | solution.py:33
  99.3 1.6 %slice_bitcast_fusion.1.q = bf16[512,128]{1,0:T(8,128)(2,1)} fusion(bf16[5,512,128]{2,1,0:T(8,128)(2,1)} %bitcast.57), kind=kLoop, calls=%fused_computation.21 | loop fusion | bytes 262144 | tf_op jit(solution)/shard_map/squeeze | solution.py:266
  100.9 13.8 %collective-permute-done.15.halo = bf16[2,2,512,128]{3,2,1,0:T(8,128)(2,1)} collective-permute-done((bf16[2,2,512,128]{3,2,1,0:T(8,128)(2,1)}, bf16[2,2,512,128]{3,2,1,0:T(8,128)(2,1)}, u32[]{:S(2)}, u32[]{:S(2)}) %collective-permute-start.15) | collective-permute-done | bytes 524320 | tf_op jit(solution)/shard_map/rest_x/ppermute | solution.py:33
  114.7 5.1 %rest_attention.1.r0 = bf16[512,128]{1,0:T(8,128)(2,1)} custom-call(s32[4]{0:T(128)} %pad_add_fusion.where_ref, s32[32]{0:T(128)} %reshape.134.place_ref, bf16[2,512,128]{2,1,0:T(8,128)(2,1)} %slice_bitcast_fusion.own.kv0, bf16[2,512,128]{2,1,0:T(8,128)(2,1)} %copy-done.8, bf16[2,512,128]{2,1,0:T(8,128)(2,1)} %copy-done.9, bf16[2,512,128]{2,1,0:T(8,128)(2,1)} %copy-done.10, ...), custom_call_target="tpu_custom_call" | custom-call | flops 503316480 | bytes 4194304 | tf_op jit(solution)/shard_map/rest_attention/pallas_call | solution.py:74
  119.7 1.6 %collective-permute-start.22 = (bf16[512,128]{1,0:T(8,128)(2,1)}, bf16[512,128]{1,0:T(8,128)(2,1)S(1)}, u32[]{:S(2)}, u32[]{:S(2)}) collective-permute-start(bf16[512,128]{1,0:T(8,128)(2,1)} %rest_attention.1.r0), channel_id=1, source_target_pairs={{0,1},{1,0},{2,3},{3,2},{4,5},{5,4},{6,7},{7,6},{8,9},{9,8},{10,11... | collective-permute-start | bytes 393224 | tf_op jit(solution)/shard_map/rest_core/ppermute | solution.py:33
  122.5 4.9 %collective-permute-done.16.r0 = bf16[512,128]{1,0:T(8,128)(2,1)S(1)} collective-permute-done((bf16[512,128]{1,0:T(8,128)(2,1)}, bf16[512,128]{1,0:T(8,128)(2,1)S(1)}, u32[]{:S(2)}, u32[]{:S(2)}) %collective-permute-start.16) | collective-permute-done | bytes 131104 | tf_op jit(solution)/shard_map/rest_y/ppermute | solution.py:33
  130.0 6.9 %project.1.before = f32[512,1280]{1,0:T(8,128)} custom-call(s32[4]{0:T(128)} %pad_add_fusion.where_ref, bf16[4,512,128]{2,1,0:T(8,128)(2,1)} %copy-done.2, bf16[512,128]{1,0:T(8,128)(2,1)} %rest_attention.1.r0, bf16[640,1280]{1,0:T(8,128)(2,1)} %get-tuple-element.38.w0, bf16[4,512,128]{2,1,0:T(8,128)(2,1)} %copy-done.6, bf16[512,128]{1,0:T(8,128)(2,1)} %copy-done.13, ...), custom_call_target="tpu_custom_call" | custom-call | flops 1677721600 | bytes 8388608 | tf_op jit(solution)/shard_map/project/pallas_call | solution.py:74
  138.2 7.3 %finish.1 = bf16[512,1280]{1,0:T(8,128)(2,1)} custom-call(s32[4]{0:T(128)} %pad_add_fusion.where_ref, bf16[4,512,128]{2,1,0:T(8,128)(2,1)} %collective-permute-done.11.m0, bf16[512,128]{1,0:T(8,128)(2,1)} %copy-done.11, bf16[640,1280]{1,0:T(8,128)(2,1)} %get-tuple-element.40.w0, bf16[4,512,128]{2,1,0:T(8,128)(2,1)} %collective-permute-done.18.m1, ...), custom_call_target="tpu_custom_call" | custom-call | flops 1677721600 | bytes 8388608 | tf_op jit(solution)/shard_map/finish/pallas_call | solution.py:74
  (92 shorter events, 22.7 us)
Async XLA Ops:
  3.8 44.1 %collective-permute-start.17 = (bf16[640,2560]{1,0:T(8,128)(2,1)}, bf16[640,2560]{1,0:T(8,128)(2,1)S(1)}, u32[]{:S(2)}, u32[]{:S(2)}) collective-permute-start(bf16[640,2560]{1,0:T(8,128)(2,1)} %constant_dynamic-slice_fusion.3), channel_id=1, source_target_pairs={{0,2},{1,67},{2,64},{3,1},{4,6},{5,71},{6,68},{7,5},{8,10},{9,75},... | collective-permute-start | bytes 9830408 | tf_op jit(solution)/shard_map/weights_y/ppermute | solution.py:33
  6.3 21.2 %collective-permute-start = (bf16[2,512,128]{2,1,0:T(8,128)(2,1)}, bf16[2,512,128]{2,1,0:T(8,128)(2,1)S(1)}, u32[]{:S(2)}, u32[]{:S(2)}) collective-permute-start(bf16[2,512,128]{2,1,0:T(8,128)(2,1)} %get-tuple-element.43), channel_id=1, source_target_pairs={{0,12},{1,13},{2,14},{3,15},{4,0},{5,1},{6,2},{7,3},{8,4},{9,5},{1... | collective-permute-start | bytes 786440 | tf_op jit(solution)/shard_map/keys_values_z/ppermute | solution.py:33
  10.0 17.5 %collective-permute-start.1 = (bf16[2,512,128]{2,1,0:T(8,128)(2,1)}, bf16[2,512,128]{2,1,0:T(8,128)(2,1)}, u32[]{:S(2)}, u32[]{:S(2)}) collective-permute-start(bf16[2,512,128]{2,1,0:T(8,128)(2,1)} %get-tuple-element.44), channel_id=1, source_target_pairs={{0,8},{1,9},{2,10},{3,11},{4,12},{5,13},{6,14},{7,15},{8,0},{9,1},... | collective-permute-start | bytes 786440 | tf_op jit(solution)/shard_map/keys_values_z/ppermute | solution.py:33
  10.0 17.5 %collective-permute-start.2 = (bf16[2,512,128]{2,1,0:T(8,128)(2,1)}, bf16[2,512,128]{2,1,0:T(8,128)(2,1)}, u32[]{:S(2)}, u32[]{:S(2)}) collective-permute-start(bf16[2,512,128]{2,1,0:T(8,128)(2,1)} %get-tuple-element.41), channel_id=1, source_target_pairs={{0,4},{1,5},{2,6},{3,7},{4,8},{5,9},{6,10},{7,11},{8,12},{9,13},{1... | collective-permute-start | bytes 786440 | tf_op jit(solution)/shard_map/keys_values_z/ppermute | solution.py:33
  24.1 5.5 %copy-start.1 = (bf16[512,5,128]{2,0,1:T(8,128)(2,1)S(1)}, bf16[512,5,128]{2,0,1:T(8,128)(2,1)}, u32[]{:S(2)}) copy-start(bf16[512,5,128]{2,0,1:T(8,128)(2,1)} %param.7) | copy-start | bytes 1966084
  27.5 9.4 %collective-permute-start.3 = (bf16[512,128]{1,0:T(8,128)(2,1)S(1)}, bf16[512,128]{1,0:T(8,128)(2,1)S(1)}, u32[]{:S(2)}, u32[]{:S(2)}) collective-permute-start(bf16[512,128]{1,0:T(8,128)(2,1)S(1)} %get-tuple-element.24), channel_id=1, source_target_pairs={{0,12},{1,13},{2,14},{3,15},{4,0},{5,1},{6,2},{7,3},{8,4},{9,5},{1... | collective-permute-start | bytes 393224 | tf_op jit(solution)/shard_map/queries_z/ppermute | solution.py:33
  29.7 13.8 %collective-permute-start.4 = (bf16[512,128]{1,0:T(8,128)(2,1)S(1)}, bf16[512,128]{1,0:T(8,128)(2,1)S(1)}, u32[]{:S(2)}, u32[]{:S(2)}) collective-permute-start(bf16[512,128]{1,0:T(8,128)(2,1)S(1)} %get-tuple-element.25), channel_id=1, source_target_pairs={{0,8},{1,9},{2,10},{3,11},{4,12},{5,13},{6,14},{7,15},{8,0},{9,1},... | collective-permute-start | bytes 393224 | tf_op jit(solution)/shard_map/queries_z/ppermute | solution.py:33
  31.6 15.7 %collective-permute-start.5 = (bf16[512,128]{1,0:T(8,128)(2,1)S(1)}, bf16[512,128]{1,0:T(8,128)(2,1)S(1)}, u32[]{:S(2)}, u32[]{:S(2)}) collective-permute-start(bf16[512,128]{1,0:T(8,128)(2,1)S(1)} %get-tuple-element.26), channel_id=1, source_target_pairs={{0,4},{1,5},{2,6},{3,7},{4,8},{5,9},{6,10},{7,11},{8,12},{9,13},{1... | collective-permute-start | bytes 393224 | tf_op jit(solution)/shard_map/queries_z/ppermute | solution.py:33
  33.8 22.2 %collective-permute-start.6 = (bf16[2,2,512,128]{3,2,1,0:T(8,128)(2,1)}, bf16[2,2,512,128]{3,2,1,0:T(8,128)(2,1)S(1)}, u32[]{:S(2)}, u32[]{:S(2)}) collective-permute-start(bf16[2,2,512,128]{3,2,1,0:T(8,128)(2,1)} %get-tuple-element.30), channel_id=1, source_target_pairs={{0,16},{1,17},{2,18},{3,19},{4,20},{5,21},{6,22},{7,23},{8,24},{9,... | collective-permute-start | bytes 1572872 | tf_op jit(solution)/shard_map/keys_values_x/ppermute | solution.py:33
  36.9 10.3 %copy-start.18 = (bf16[512,128]{1,0:T(8,128)(2,1)}, bf16[512,128]{1,0:T(8,128)(2,1)S(1)}, u32[]{:S(2)}) copy-start(bf16[512,128]{1,0:T(8,128)(2,1)S(1)} %collective-permute-done.3.q1) | copy-start | bytes 393220
  37.0 19.1 %collective-permute-start.7 = (bf16[2,2,512,128]{3,2,1,0:T(8,128)(2,1)}, bf16[2,2,512,128]{3,2,1,0:T(8,128)(2,1)S(1)}, u32[]{:S(2)}, u32[]{:S(2)}) collective-permute-start(bf16[2,2,512,128]{3,2,1,0:T(8,128)(2,1)} %get-tuple-element.31), channel_id=1, source_target_pairs={{16,0},{17,1},{18,2},{19,3},{20,4},{21,5},{22,6},{23,7},{24,8},{25... | collective-permute-start | bytes 1572872 | tf_op jit(solution)/shard_map/keys_values_x/ppermute | solution.py:33
  43.5 85.1 %collective-permute-start.23 = (bf16[640,1280]{1,0:T(8,128)(2,1)S(1)}, bf16[640,1280]{1,0:T(8,128)(2,1)S(1)}, u32[]{:S(2)}, u32[]{:S(2)}) collective-permute-start(bf16[640,1280]{1,0:T(8,128)(2,1)S(1)} %get-tuple-element.37), channel_id=1, source_target_pairs={{0,1},{1,0},{2,3},{3,2},{4,5},{5,4},{6,7},{7,6},{8,9},{9,8},{10,11... | collective-permute-start | bytes 4915208 | tf_op jit(solution)/shard_map/weights_core/ppermute | solution.py:33
  49.3 87.6 %collective-permute-start.20 = (bf16[640,1280]{1,0:T(8,128)(2,1)S(1)}, bf16[640,1280]{1,0:T(8,128)(2,1)S(1)}, u32[]{:S(2)}, u32[]{:S(2)}) collective-permute-start(bf16[640,1280]{1,0:T(8,128)(2,1)S(1)} %get-tuple-element.39), channel_id=1, source_target_pairs={{0,1},{1,0},{2,3},{3,2},{4,5},{5,4},{6,7},{7,6},{8,9},{9,8},{10,11... | collective-permute-start | bytes 4915208 | tf_op jit(solution)/shard_map/weights_core/ppermute | solution.py:33
  57.6 12.7 %copy-start.5 = (bf16[2,512,128]{2,1,0:T(8,128)(2,1)S(1)}, bf16[2,512,128]{2,1,0:T(8,128)(2,1)}, u32[]{:S(2)}) copy-start(bf16[2,512,128]{2,1,0:T(8,128)(2,1)} %slice_bitcast_fusion.own.kv0) | copy-start | bytes 786436
  66.6 7.0 %collective-permute-start.8 = (bf16[512,128]{1,0:T(8,128)(2,1)}, bf16[512,128]{1,0:T(8,128)(2,1)S(1)}, u32[]{:S(2)}, u32[]{:S(2)}) collective-permute-start(bf16[512,128]{1,0:T(8,128)(2,1)} %get-tuple-element.33), channel_id=1, source_target_pairs={{0,12},{1,13},{2,14},{3,15},{4,0},{5,1},{6,2},{7,3},{8,4},{9,5},{1... | collective-permute-start | bytes 393224 | tf_op jit(solution)/shard_map/attended_z/ppermute | solution.py:33
  70.3 14.4 %collective-permute-start.12 = (bf16[2,512,128]{2,1,0:T(8,128)(2,1)S(1)}, bf16[2,512,128]{2,1,0:T(8,128)(2,1)S(1)}, u32[]{:S(2)}, u32[]{:S(2)}) collective-permute-start(bf16[2,512,128]{2,1,0:T(8,128)(2,1)S(1)} %copy-done.5), channel_id=1, source_target_pairs={{0,12},{1,13},{2,14},{3,15},{4,0},{5,1},{6,2},{7,3},{8,4},{9,5},{1... | collective-permute-start | bytes 786440 | tf_op jit(solution)/shard_map/rest_z/ppermute | solution.py:33
  70.5 6.2 %collective-permute-start.9 = (bf16[512,128]{1,0:T(8,128)(2,1)}, bf16[512,128]{1,0:T(8,128)(2,1)S(1)}, u32[]{:S(2)}, u32[]{:S(2)}) collective-permute-start(bf16[512,128]{1,0:T(8,128)(2,1)} %get-tuple-element.34), channel_id=1, source_target_pairs={{0,8},{1,9},{2,10},{3,11},{4,12},{5,13},{6,14},{7,15},{8,0},{9,1},... | collective-permute-start | bytes 393224 | tf_op jit(solution)/shard_map/attended_z/ppermute | solution.py:33
  73.6 6.2 %collective-permute-start.10 = (bf16[512,128]{1,0:T(8,128)(2,1)}, bf16[512,128]{1,0:T(8,128)(2,1)S(1)}, u32[]{:S(2)}, u32[]{:S(2)}) collective-permute-start(bf16[512,128]{1,0:T(8,128)(2,1)} %get-tuple-element.35), channel_id=1, source_target_pairs={{0,4},{1,5},{2,6},{3,7},{4,8},{5,9},{6,10},{7,11},{8,12},{9,13},{1... | collective-permute-start | bytes 393224 | tf_op jit(solution)/shard_map/attended_z/ppermute | solution.py:33
  76.7 9.6 %collective-permute-start.13 = (bf16[2,512,128]{2,1,0:T(8,128)(2,1)S(1)}, bf16[2,512,128]{2,1,0:T(8,128)(2,1)S(1)}, u32[]{:S(2)}, u32[]{:S(2)}) collective-permute-start(bf16[2,512,128]{2,1,0:T(8,128)(2,1)S(1)} %copy-done.5), channel_id=1, source_target_pairs={{0,8},{1,9},{2,10},{3,11},{4,12},{5,13},{6,14},{7,15},{8,0},{9,1},... | collective-permute-start | bytes 786440 | tf_op jit(solution)/shard_map/rest_z/ppermute | solution.py:33
  79.8 13.5 %collective-permute-start.14 = (bf16[2,512,128]{2,1,0:T(8,128)(2,1)S(1)}, bf16[2,512,128]{2,1,0:T(8,128)(2,1)S(1)}, u32[]{:S(2)}, u32[]{:S(2)}) collective-permute-start(bf16[2,512,128]{2,1,0:T(8,128)(2,1)S(1)} %copy-done.5), channel_id=1, source_target_pairs={{0,4},{1,5},{2,6},{3,7},{4,8},{5,9},{6,10},{7,11},{8,12},{9,13},{1... | collective-permute-start | bytes 786440 | tf_op jit(solution)/shard_map/rest_z/ppermute | solution.py:33
  84.8 35.0 %copy-start.2 = (bf16[4,512,128]{2,1,0:T(8,128)(2,1)}, bf16[4,512,128]{2,1,0:T(8,128)(2,1)S(1)}, u32[]{:S(2)}) copy-start(bf16[4,512,128]{2,1,0:T(8,128)(2,1)S(1)} %pad_maximum_fusion.1.m0) | copy-start | bytes 1572868
  84.8 8.5 %copy-start.8 = (bf16[2,512,128]{2,1,0:T(8,128)(2,1)}, bf16[2,512,128]{2,1,0:T(8,128)(2,1)S(1)}, u32[]{:S(2)}) copy-start(bf16[2,512,128]{2,1,0:T(8,128)(2,1)S(1)} %collective-permute-done.12.one.kv1) | copy-start | bytes 786436
  84.8 14.0 %collective-permute-start.11 = (bf16[4,512,128]{2,1,0:T(8,128)(2,1)S(1)}, bf16[4,512,128]{2,1,0:T(8,128)(2,1)}, u32[]{:S(2)}, u32[]{:S(2)}) collective-permute-start(bf16[4,512,128]{2,1,0:T(8,128)(2,1)S(1)} %pad_maximum_fusion.1.m0), channel_id=1, source_target_pairs={{0,2},{1,3},{2,0},{3,1},{4,6},{5,7},{6,4},{7,5},{8,10},{9,11},{10,... | collective-permute-start | bytes 1572872 | tf_op jit(solution)/shard_map/main_y/ppermute | solution.py:33
  86.4 6.9 %copy-start.9 = (bf16[2,512,128]{2,1,0:T(8,128)(2,1)}, bf16[2,512,128]{2,1,0:T(8,128)(2,1)S(1)}, u32[]{:S(2)}) copy-start(bf16[2,512,128]{2,1,0:T(8,128)(2,1)S(1)} %collective-permute-done.13.two.kv2) | copy-start | bytes 786436
  96.1 18.6 %collective-permute-start.15 = (bf16[2,2,512,128]{3,2,1,0:T(8,128)(2,1)}, bf16[2,2,512,128]{3,2,1,0:T(8,128)(2,1)}, u32[]{:S(2)}, u32[]{:S(2)}) collective-permute-start(bf16[2,2,512,128]{3,2,1,0:T(8,128)(2,1)} %rest_pick.1), channel_id=1, source_target_pairs={{0,16},{1,17},{2,18},{3,19},{4,20},{5,21},{6,22},{7,23},{16,32},{1... | collective-permute-start | bytes 1572872 | tf_op jit(solution)/shard_map/rest_x/ppermute | solution.py:33
  98.0 30.6 %collective-permute-start.21 = (bf16[4,512,128]{2,1,0:T(8,128)(2,1)S(1)}, bf16[4,512,128]{2,1,0:T(8,128)(2,1)S(1)}, u32[]{:S(2)}, u32[]{:S(2)}) collective-permute-start(bf16[4,512,128]{2,1,0:T(8,128)(2,1)S(1)} %pad_maximum_fusion.1.m0), channel_id=1, source_target_pairs={{0,1},{1,0},{2,3},{3,2},{4,5},{5,4},{6,7},{7,6},{8,9},{9,8},{10,11... | collective-permute-start | bytes 1572872 | tf_op jit(solution)/shard_map/main_core/ppermute | solution.py:33
  98.8 38.2 %collective-permute-start.18 = (bf16[4,512,128]{2,1,0:T(8,128)(2,1)}, bf16[4,512,128]{2,1,0:T(8,128)(2,1)}, u32[]{:S(2)}, u32[]{:S(2)}) collective-permute-start(bf16[4,512,128]{2,1,0:T(8,128)(2,1)} %collective-permute-done.11.m0), channel_id=1, source_target_pairs={{0,1},{1,0},{2,3},{3,2},{4,5},{5,4},{6,7},{7,6},{8,9},{9,8},{10,11... | collective-permute-start | bytes 1572872 | tf_op jit(solution)/shard_map/main_far_core/ppermute | solution.py:33
  119.7 2.8 %collective-permute-start.22 = (bf16[512,128]{1,0:T(8,128)(2,1)}, bf16[512,128]{1,0:T(8,128)(2,1)S(1)}, u32[]{:S(2)}, u32[]{:S(2)}) collective-permute-start(bf16[512,128]{1,0:T(8,128)(2,1)} %rest_attention.1.r0), channel_id=1, source_target_pairs={{0,1},{1,0},{2,3},{3,2},{4,5},{5,4},{6,7},{7,6},{8,9},{9,8},{10,11... | collective-permute-start | bytes 393224 | tf_op jit(solution)/shard_map/rest_core/ppermute | solution.py:33
  122.5 6.2 %copy-start.13 = (bf16[512,128]{1,0:T(8,128)(2,1)}, bf16[512,128]{1,0:T(8,128)(2,1)S(1)}, u32[]{:S(2)}) copy-start(bf16[512,128]{1,0:T(8,128)(2,1)S(1)} %collective-permute-done.22.r1) | copy-start | bytes 393220
  122.5 4.9 %collective-permute-start.16 = (bf16[512,128]{1,0:T(8,128)(2,1)}, bf16[512,128]{1,0:T(8,128)(2,1)S(1)}, u32[]{:S(2)}, u32[]{:S(2)}) collective-permute-start(bf16[512,128]{1,0:T(8,128)(2,1)} %rest_attention.1.r0), channel_id=1, source_target_pairs={{0,2},{1,3},{2,0},{3,1},{4,6},{5,7},{6,4},{7,5},{8,10},{9,11},{10,... | collective-permute-start | bytes 393224 | tf_op jit(solution)/shard_map/rest_y/ppermute | solution.py:33
  127.4 9.5 %copy-start.11 = (bf16[512,128]{1,0:T(8,128)(2,1)}, bf16[512,128]{1,0:T(8,128)(2,1)S(1)}, u32[]{:S(2)}) copy-start(bf16[512,128]{1,0:T(8,128)(2,1)S(1)} %collective-permute-done.16.r0) | copy-start | bytes 393220
  127.4 9.5 %collective-permute-start.19 = (bf16[512,128]{1,0:T(8,128)(2,1)S(1)}, bf16[512,128]{1,0:T(8,128)(2,1)S(1)}, u32[]{:S(2)}, u32[]{:S(2)}) collective-permute-start(bf16[512,128]{1,0:T(8,128)(2,1)S(1)} %collective-permute-done.16.r0), channel_id=1, source_target_pairs={{0,1},{1,0},{2,3},{3,2},{4,5},{5,4},{6,7},{7,6},{8,9},{9,8},{10,11... | collective-permute-start | bytes 393224 | tf_op jit(solution)/shard_map/rest_far_core/ppermute | solution.py:33
  (13 other events, 21.4 us)

commit v2 on v1

v2 whole, which is shorter than its diff:
```python
import functools

import jax
import jax.numpy as jnp
from jax import lax
from jax.experimental import pallas as pl
from jax.experimental.pallas import tpu as pltpu
from jax.sharding import PartitionSpec as P

TILE = 128
SLAB = 8
ROW = 4
NEG = -1e30
LOG2E = 1.4426950408889634
AXES = ("seq", "head")
VMEM_LIMIT = 16 * 1024 * 1024


def route(rows, target):
    pairs = []
    for row in range(rows):
        for z in range(ROW):
            for yl in range(2):
                for c in range(2):
                    to = target(row, z, yl, c)
                    if to is not None:
                        dst = ((to[0] * ROW + to[1]) * 2 + to[2]) * 2 + to[3]
                        pairs.append((((row * ROW + z) * 2 + yl) * 2 + c, dst))
    return pairs


def send(block, rows, target):
    return lax.ppermute(block, AXES, route(rows, target))


def along_z(blocks, rows):
    plus, two, minus = (
        send(blocks[j - 1], rows, lambda r, z, yl, c, j=j: (r, (z + j) % ROW, yl, c)) for j in (1, 2, 3)
    )
    return [minus, two, plus]


def after(first, *then):
    return list(lax.optimization_barrier((tuple(first), tuple(then)))[1])


def places_kernel(where_ref, mask_ref, out):
    count = mask_ref.shape[0]
    start = where_ref[3]
    pick = lax.broadcasted_iota(jnp.int32, (4 * SLAB, count), 1) - lax.broadcasted_iota(jnp.int32, (4 * SLAB, count), 0)
    pick = jnp.where(pick == start, 1.0, 0.0)
    rows = jnp.dot(pick, (mask_ref[...] > 0).astype(jnp.float32), preferred_element_type=jnp.float32)
    near = lax.dot_general(rows, pick, (((1,), (1,)), ((), ())), preferred_element_type=jnp.float32)
    live = jnp.where(near > 0.5, 1, 0)
    shape = live.shape
    down = lax.broadcasted_iota(jnp.int32, shape, 0)
    across = lax.broadcasted_iota(jnp.int32, shape, 1)
    same_slab = (down // SLAB) == (across // SLAB)
    inside = jnp.where(same_slab, live, 0)
    lane = across[:1]
    degree = (jnp.sum(inside, axis=0, keepdims=True), jnp.sum(inside, axis=1, keepdims=True))
    edge_row = degree[0] == 4

    def beside(reference):
        return (
            jnp.sum(jnp.where(down == reference, live, 0), axis=0, keepdims=True),
            jnp.sum(jnp.where(across == reference, live, 0), axis=1, keepdims=True),
        )

    first = jnp.min(jnp.where(edge_row & (lane // SLAB == 1), lane, 4 * SLAB), axis=1, keepdims=True)
    one = beside(first)
    second = jnp.min(jnp.where(edge_row & (lane // SLAB == 2) & (one[0] > 0), lane, 4 * SLAB), axis=1, keepdims=True)
    two = beside(second)
    column = []
    for at, index in ((0, lane), (1, down[:, :1])):
        side = jnp.where(index < 3 * SLAB, one[at], two[at]) > 0
        middle = jnp.where(degree[at] == 4, 0, 1)
        column.append(jnp.where(side, middle, 3 - middle))
    twin = same_slab & (column[0] == column[1]) & (down < across)
    place = column[0] * 2 + jnp.sum(jnp.where(twin, 1, 0), axis=0, keepdims=True)
    place = jnp.where(degree[0] == 0, lane % SLAB, place)
    out[...] = jnp.clip(place, 0, SLAB - 1)


ANYWHERE = pl.BlockSpec(memory_space=pltpu.VMEM)
SCALARS = pl.BlockSpec(memory_space=pltpu.SMEM)


def call(kernel, outs, scratch, operands, scalars, flops=1024):
    return pl.pallas_call(
        kernel,
        out_shape=outs,
        in_specs=[SCALARS] * scalars + [ANYWHERE] * (len(operands) - scalars),
        out_specs=jax.tree.map(lambda _: ANYWHERE, outs),
        scratch_shapes=scratch,
        compiler_params=pltpu.CompilerParams(vmem_limit_bytes=VMEM_LIMIT),
        cost_estimate=pl.CostEstimate(flops=flops, bytes_accessed=1024, transcendentals=0),
    )(*operands)


def pick_kernel(where_ref, own, one, two, three, up, down):
    z = where_ref[0]
    for at in range(ROW):

        @pl.when(z == at)
        def _():
            ring = (own, one, two, three)
            for out, blocks in ((up, (2, 3)), (down, (0, 1))):
                for at_out, block in enumerate(blocks):
                    out[at_out] = ring[(block - at) % ROW][:2]


def pick_one_kernel(where_ref, own, one, two, three, out):
    z = where_ref[0]
    for at in range(ROW):

        @pl.when(z == at)
        def _():
            ring = (own, one, two, three)
            base = 2 if at < 2 else 0
            out[0] = ring[(base - at) % ROW][...]
            out[1] = ring[(base + 1 - at) % ROW][...]


def spot(index):
    return pl.ds(pl.multiple_of(index * TILE, TILE), TILE)


def spread(where_ref, place_ref, ring, targets):
    z = where_ref[0]
    for j in range(ROW):
        block = lax.rem(z + j, ROW)
        for i in range(4):
            at = spot((block // 2) * SLAB + place_ref[0, SLAB + block * 4 + i])
            for target, piece in zip(targets, ring[j]):
                target[at, :] = piece[i * TILE : (i + 1) * TILE, :]


def softmax_rows(q, parts, valid, scale):
    scores = [
        lax.dot_general(q, keys, (((1,), (1,)), ((), ())), preferred_element_type=jnp.float32) for keys, _ in parts
    ]
    tops = [jnp.max(s, axis=-1, keepdims=True) for s in scores]
    tops[-1] = jnp.where(valid, tops[-1], NEG)
    top = functools.reduce(jnp.maximum, tops)
    total, summed = 0.0, 0.0
    for at, (s, (_, values)) in enumerate(zip(scores, parts)):
        weights = jnp.exp2((s - top) * (scale * LOG2E))
        part_total = jnp.sum(weights, axis=-1, keepdims=True)
        part_sum = jnp.dot(weights.astype(jnp.bfloat16), values, preferred_element_type=jnp.float32)
        if at == len(parts) - 1:
            part_total = jnp.where(valid, part_total, 0.0)
            part_sum = jnp.where(valid, part_sum, 0.0)
        total, summed = total + part_total, summed + part_sum
    return summed / total


WINDOW = ((0, 512), (0, 768), (256, 1024), (512, 1024))


def piece_scores(q, keys):
    return lax.dot_general(q, keys, (((1,), (1,)), ((), ())), preferred_element_type=jnp.float32)


def near_kernel(where_ref, place_ref, kvq0, kvq1, kvq2, kvq3, qs, acc, stats, ks, vs):
    factor = ks.shape[-1] ** -0.5 * LOG2E
    ring = [(kvq.at[0], kvq.at[1], kvq.at[2]) for kvq in (kvq0, kvq1, kvq2, kvq3)]
    spread(where_ref, place_ref, ring, (ks, vs, qs))
    lane = lax.broadcasted_iota(jnp.int32, (256, 128), 1)
    for s in range(2):
        for column, (low, high) in enumerate(WINDOW):
            rows = slice(s * 1024 + column * 256, s * 1024 + column * 256 + 256)
            q = qs[rows, :]
            pieces = [slice(t * 1024 + low, t * 1024 + high) for t in range(2)]
            scores = [piece_scores(q, ks[piece, :]) for piece in pieces]
            top = functools.reduce(jnp.maximum, [jnp.max(p, axis=-1, keepdims=True) for p in scores])
            total, summed = 0.0, 0.0
            for piece, score in zip(pieces, scores):
                weights = jnp.exp2((score - top) * factor)
                total = total + jnp.sum(weights, axis=-1, keepdims=True)
                summed = summed + jnp.dot(
                    weights.astype(jnp.bfloat16), vs[piece, :], preferred_element_type=jnp.float32
                )
            acc[rows, :] = summed
            stats[rows, :] = jnp.where(lane == 0, top, total)


def halo_kernel(where_ref, place_ref, qs, acc, stats, up, down, o0, o1, o2, o3, ks, vs, os):
    factor = qs.shape[-1] ** -0.5 * LOG2E
    for side, first, slab in ((up, 0, 0), (down, 24, 1)):
        for b in range(2):
            for i in range(4):
                at = spot(slab * SLAB + place_ref[0, first + b * 4 + i])
                rows = slice(i * TILE, (i + 1) * TILE)
                ks[at, :] = side[b, 0, rows, :]
                vs[at, :] = side[b, 1, rows, :]
    for s in range(2):
        valid = where_ref[1 + s] > 0
        for column, (low, high) in enumerate(WINDOW):
            rows = slice(s * 1024 + column * 256, s * 1024 + column * 256 + 256)
            piece = slice(s * 1024 + low, s * 1024 + high)
            score = piece_scores(qs[rows, :], ks[piece, :])
            before = stats[rows, :]
            top_before, total_before = before[:, 0:1], before[:, 1:2]
            top = jnp.maximum(top_before, jnp.where(valid, jnp.max(score, axis=-1, keepdims=True), NEG))
            weights = jnp.exp2((score - top) * factor)
            total = jnp.where(valid, jnp.sum(weights, axis=-1, keepdims=True), 0.0)
            summed = jnp.dot(weights.astype(jnp.bfloat16), vs[piece, :], preferred_element_type=jnp.float32)
            summed = jnp.where(valid, summed, 0.0)
            shrink = jnp.exp2((top_before - top) * factor)
            total = total + total_before * shrink
            os[rows, :] = ((summed + acc[rows, :] * shrink) / total).astype(jnp.bfloat16)
    z = where_ref[0]
    for j, out in enumerate((o0, o1, o2, o3)):
        block = lax.rem(z + j, ROW)
        for i in range(4):
            at = spot((block // 2) * SLAB + place_ref[0, SLAB + block * 4 + i])
            out[i * TILE : (i + 1) * TILE, :] = os[at, :]


def rest_kernel(where_ref, place_ref, kv0, kv1, kv2, kv3, q, halo, out, ks, vs):
    scale = q.shape[-1] ** -0.5
    z = where_ref[0]
    ring = [(kv.at[0], kv.at[1]) for kv in (kv0, kv1, kv2, kv3)]
    spread(where_ref, place_ref, ring, (ks.at[0:2048], vs.at[0:2048]))
    first = jnp.where(z < 2, 0, 24)
    valid = jnp.where(z < 2, where_ref[1], where_ref[2]) > 0
    for b in range(2):
        for i in range(4):
            at = spot(2 * SLAB + place_ref[0, first + b * 4 + i])
            rows = slice(i * TILE, (i + 1) * TILE)
            ks[at, :] = halo[b, 0, rows, :]
            vs[at, :] = halo[b, 1, rows, :]

    @pl.loop(0, 4)
    def _(i):
        column = place_ref[0, SLAB + z * 4 + i] // 2
        low = jnp.maximum(column - 1, 0) * 256
        here = spot(i)
        edge = (column == 0) | (column == 3)

        def work(width):
            parts = []
            for t in range(3):
                at = pl.ds(pl.multiple_of(t * 1024 + low, 256), width)
                parts.append((ks[at, :], vs[at, :]))
            out[here, :] = softmax_rows(q[here, :], parts, valid, scale).astype(jnp.bfloat16)

        @pl.when(edge)
        def _():
            work(512)

        @pl.when(jnp.logical_not(edge))
        def _():
            work(768)


def place_heads(z, ring, wide, base):
    for j in range(ROW):
        head = lax.rem(z + j, ROW)
        at = pl.multiple_of(base + head * TILE, TILE)
        wide[:, pl.ds(at, TILE)] = ring[j]
    wide[:, base + ROW * TILE : base + (ROW + 1) * TILE] = ring[ROW]


def project_kernel(where_ref, m0, w0, m1, w1, out, wide):
    z = where_ref[0]
    place_heads(z, m0, wide, 0)
    place_heads(z, m1, wide, 640)

    @pl.loop(0, out.shape[1] // 256)
    def _(n):
        at = pl.ds(pl.multiple_of(n * 256, 256), 256)
        out[:, at] = jnp.dot(wide[:, :640], w0[:, at], preferred_element_type=jnp.float32) + jnp.dot(
            wide[:, 640:], w1[:, at], preferred_element_type=jnp.float32
        )


def finish_kernel(where_ref, m0, w0, m1, w1, before, out, wide):
    z = where_ref[0]
    place_heads(z, m0, wide, 0)
    place_heads(z, m1, wide, 640)

    @pl.loop(0, out.shape[1] // 256)
    def _(n):
        at = pl.ds(pl.multiple_of(n * 256, 256), 256)
        part = jnp.dot(wide[:, :640], w0[:, at], preferred_element_type=jnp.float32) + jnp.dot(
            wide[:, 640:], w1[:, at], preferred_element_type=jnp.float32
        )
        out[:, at] = (part + before[:, at]).astype(out.dtype)


def columns_kernel(where_ref, weight, out):
    out[...] = weight[0]


def local(queries, key_rows, value_rows, out_weight, tile_mask):
    tok, heads, size = queries.shape
    rows = lax.axis_size("seq") // ROW
    seq, head = lax.axis_index("seq"), lax.axis_index("head")
    row, z = seq // ROW, seq % ROW
    yl, c = head // 2, head % 2
    bf = jnp.bfloat16
    wide_cols = out_weight.shape[-1] // 2
    cols = wide_cols // 2
    row_tok = ROW * tok
    block = jax.ShapeDtypeStruct((tok, size), bf)
    halo = jax.ShapeDtypeStruct((2, 2, tok, size), bf)

    def ring_slices(array):
        return [lax.dynamic_index_in_dim(array, (z + j) % ROW, 0, keepdims=False) for j in range(ROW)]

    def sibling(piece):
        return send(piece, rows, lambda r, z, yl, c: (r, z, yl, 1 - c))

    def y_pair(piece):
        return send(piece, rows, lambda r, z, yl, c: (r, z, 1 - yl, c))

    with jax.named_scope("lay_out"):
        kvq = jnp.stack([key_rows, value_rows, queries]).transpose(2, 0, 1, 3)
        own, *out = [lax.dynamic_index_in_dim(kvq, (z + j) % ROW, 0, keepdims=False) for j in range(ROW)]
        kv_rest, q_rest = kvq[ROW, :2], kvq[ROW, 2]
    with jax.named_scope("head_z"):
        ring = along_z(out, rows)

    with jax.named_scope("weights_y"):
        lead = send(out[0][0, :16], rows, lambda r, z, yl, c: (r, (z + 1) % ROW, yl, c))
        (out_weight,) = after([lead], out_weight)
        where = jnp.stack([z, row > 0, row < rows - 1, row * 2 * SLAB - SLAB, yl]).astype(jnp.int32)
        theirs = pl.pallas_call(
            columns_kernel,
            out_shape=jax.ShapeDtypeStruct((heads * size, wide_cols), bf),
            grid_spec=pltpu.PrefetchScalarGridSpec(
                num_scalar_prefetch=1,
                grid=(heads,),
                in_specs=[pl.BlockSpec((1, size, wide_cols), lambda h, where: (h, 0, 1 - where[4]))],
                out_specs=pl.BlockSpec((size, wide_cols), lambda h, where: (h, 0)),
            ),
            compiler_params=pltpu.CompilerParams(vmem_limit_bytes=VMEM_LIMIT),
            cost_estimate=pl.CostEstimate(flops=2 * 10**10, bytes_accessed=1024, transcendentals=0),
        )(where, out_weight)

        def y_step(r, z, yl, c):
            yh, x = r // ROW, r % ROW
            y = (yh * 2 + yl + (1 if c == 0 else -1)) % 4
            return ((y // 2) * ROW + x, z, y % 2, c)

        w_far = send(theirs, rows, y_step)

    with jax.named_scope("pick"):
        to_next, to_prev = call(pick_kernel, (halo, halo), [], [where, own, *ring], 1)
    with jax.named_scope("head_x"):
        from_prev = send(to_next, rows, lambda r, z, yl, c: (r + 1, z, yl, c) if r + 1 < rows else None)
        from_next = send(to_prev, rows, lambda r, z, yl, c: (r - 1, z, yl, c) if r > 0 else None)
    with jax.named_scope("places"):
        (tile_mask,) = after([to_next], tile_mask)
        place = call(
            places_kernel, jax.ShapeDtypeStruct((1, 4 * SLAB), jnp.int32), [], [where, tile_mask], 1, flops=10**10
        )
    with jax.named_scope("rest_z"):
        (kv_rest,) = after([place], kv_rest)
        rest_in = along_z([kv_rest] * 3, rows)
    with jax.named_scope("near_attention"):
        qs, acc, stats = call(
            near_kernel,
            (
                jax.ShapeDtypeStruct((row_tok, size), bf),
                jax.ShapeDtypeStruct((row_tok, size), jnp.float32),
                jax.ShapeDtypeStruct((row_tok, size), jnp.float32),
            ),
            [pltpu.VMEM((row_tok, size), bf), pltpu.VMEM((row_tok, size), bf)],
            [where, place, own, *ring],
            2,
            flops=10**10,
        )
    with jax.named_scope("rest_pick"):
        to_rest = call(pick_one_kernel, halo, [], [where, kv_rest, *rest_in], 1)
    with jax.named_scope("rest_x"):

        def rest_step(r, z, yl, c):
            to = r + 1 if z < 2 else r - 1
            return (to, z, yl, c) if 0 <= to < rows else None

        rest_halo = send(to_rest, rows, rest_step)
    with jax.named_scope("halo_attention"):
        (from_prev,) = after([to_rest], from_prev)
        o_own, *o_out = call(
            halo_kernel,
            (block,) * 4,
            [pltpu.VMEM((row_tok, size), bf)] * 3,
            [where, place, qs, acc, stats, from_prev, from_next],
            2,
            flops=10**10,
        )
    with jax.named_scope("attended_z"):
        o_in = along_z(o_out, rows)
    with jax.named_scope("rest_attention"):
        (rest_halo,) = after([o_own], rest_halo)
        o_rest = call(
            rest_kernel,
            block,
            [pltpu.VMEM((6 * tok, size), bf), pltpu.VMEM((6 * tok, size), bf)],
            [where, place, kv_rest, *rest_in, q_rest, rest_halo],
            2,
            flops=10**10,
        )
    mine = jnp.stack([o_own, *o_in, o_rest])
    with jax.named_scope("attended_y"):
        far = y_pair(mine)
    with jax.named_scope("attended_core"):
        mine_sib = sibling(mine)
    with jax.named_scope("weights_core"):

        def halves(array, base):
            mine = lax.dynamic_slice_in_dim(array, base + c * cols, cols, 1)
            other = lax.dynamic_slice_in_dim(array, base + (1 - c) * cols, cols, 1)
            return mine, other

        flat, w_far = after([mine], out_weight.reshape(heads * size, 2 * wide_cols), w_far)
        w_own, w_own_other = halves(flat, yl * wide_cols)
        w_y, w_y_other = halves(w_far, 0)
        w_sib = sibling(jnp.stack([w_own_other, w_y_other]))
    wide = pltpu.VMEM((tok, 2 * heads * size), bf)
    with jax.named_scope("project"):
        near = call(
            project_kernel,
            jax.ShapeDtypeStruct((tok, cols), jnp.float32),
            [wide],
            [where, mine, w_own, mine_sib, w_sib[0]],
            1,
            flops=10**10,
        )
    with jax.named_scope("far_core"):
        (far,) = after([near], far)
        far_sib = sibling(far)
    with jax.named_scope("finish"):
        return call(
            finish_kernel,
            jax.ShapeDtypeStruct((tok, cols), bf),
            [wide],
            [where, far, w_y, far_sib, w_sib[1], near],
            1,
        )


def solution(mesh):
    placed = (
        P("seq", "head", None),
        P("seq", "head", None),
        P("seq", "head", None),
        P("head", None, None),
        P(),
    )
    return jax.shard_map(local, mesh=mesh, in_specs=placed, out_specs=P("seq", "head"), check_vma=False)
```

time: 146 us -> 105 us (0.72)
  local copies, waits for them, and re-layouts: 22.8 us -> 7.74 us
  starting transfers between devices: 43.5 us -> 32.6 us
  Pallas kernels: 32.5 us -> 23.4 us
  other arithmetic: 10.4 us -> 6.94 us
  waiting for transfers between devices: 36 us -> 32.6 us
    pallas_call x6 -> x7, Pallas kernels: 32.5 us -> 20 us  [call(): pl.pallas_call(kernel, out_shape=outs, in_specs=[SCALARS] * scalars + [AN...]
    ppermute x24 -> x17, starting transfers between devices: 43.5 us -> 32.6 us  [send(): return lax.ppermute(block, AXES, route(rows, target))]
    dynamic_slice x3 -> x1, local copies, waits for them, and re-layouts: 8.66 us -> 2.14 us  [halves(): mine = lax.dynamic_slice_in_dim(array, base + c * cols, cols, 1)]
    unnamed x42 -> x12, local copies, waits for them, and re-layouts: 6.67 us -> 2.94 us
    pallas_call x0 -> x1, other arithmetic: none -> 3.54 us  [call(): pl.pallas_call(kernel, out_shape=outs, in_specs=[SCALARS] * scalars + [AN...]
    ppermute x24 -> x17, waiting for transfers between devices: 36 us -> 32.6 us  [send(): return lax.ppermute(block, AXES, route(rows, target))]
    pallas_call x0 -> x1, Pallas kernels: none -> 3.38 us  [local(): pl.pallas_call(columns_kernel, out_shape=jax.ShapeDtypeStruct((heads * si...]
    transpose x1, other arithmetic: 0.12 us -> 3.1 us  [local(): kvq = jnp.stack([key_rows, value_rows, queries]).transpose(2, 0, 1, 3)]
  transfers between devices with their start and end apart: 24 -> 17, of which waited for: 8 -> 11; matrix products, arithmetic and copies ran while one was open for 16% -> 6% of each run, Pallas kernels for 17% -> 18%
where the time goes in v2:
time: 105 us; the launch traced here: 104 us
  starting transfers between devices  32.6 us (31%)
  waiting for transfers between devices  32.6 us (31%)
  Pallas kernels  23.4 us (22%)
  local copies, waits for them, and re-layouts  7.74 us (7%)
  other arithmetic  6.94 us (7%)
    ppermute x17, waiting for transfers between devices, send(): return lax.ppermute(block, AXES, route(rows, target))  32.6 us
    ppermute x17, starting transfers between devices, send(): return lax.ppermute(block, AXES, route(rows, target))  32.6 us
    pallas_call x7, Pallas kernels, call(): pl.pallas_call(kernel, out_shape=outs, in_specs=[SCALARS] * scalars + [AN...  20 us
    pallas_call x1, other arithmetic, call(): pl.pallas_call(kernel, out_shape=outs, in_specs=[SCALARS] * scalars + [AN...  3.54 us
    pallas_call x1, Pallas kernels, local(): pl.pallas_call(columns_kernel, out_shape=jax.ShapeDtypeStruct((heads * si...  3.38 us
    transpose x1, other arithmetic, local(): kvq = jnp.stack([key_rows, value_rows, queries]).transpose(2, 0, 1, 3)  3.1 us
    unnamed x12, local copies, waits for them, and re-layouts  2.94 us
    dynamic_slice x1, local copies, waits for them, and re-layouts, halves(): mine = lax.dynamic_slice_in_dim(array, base + c * cols, cols, 1)  2.14 us
  transfers between devices with their start and end apart: 17, of which 11 were waited for; matrix products, arithmetic and copies ran while one was open for 6% of the time, Pallas kernels for 18%

profile of v2, /device:TPU:17, one launch (start us, length us, event | category | flops | bytes accessed | tf_op | source)
XLA Modules:
  0.0 103.6 jit_solution(11814633670954769590)
XLA Ops:
  0.0 3.1 %fusion = (bf16[5,3,512,128]{3,2,1,0:T(8,128)(2,1)}, bf16[3,512,5,128]{3,1,0,2:T(8,128)(2,1)S(1)}) fusion(bf16[1,512,5,128]{3,1,0,2:T(8,128)(2,1)} %bitcast.44, bf16[1,512,5,128]{3,1,0,2:T(8,128)(2,1)} %bitcast.45, bf16[1,512,5,128]{3,1,0,2:T(8,128)(2,1)} %bitcast.46), kind=kLoop, calls=%fused_computation.19 | loop fusion | flops 1966080 | bytes 5898240 | tf_op jit(solution)/shard_map/lay_out/transpose | solution.py:320
  3.2 3.8 %collective-permute-start = (bf16[3,512,128]{2,1,0:T(8,128)(2,1)S(1)}, bf16[3,512,128]{2,1,0:T(8,128)(2,1)S(1)}, u32[]{:S(2)}, u32[]{:S(2)}) collective-permute-start(bf16[3,512,128]{2,1,0:T(8,128)(2,1)S(1)} %get-tuple-element.47), channel_id=1, source_target_pairs={{0,12},{1,13},{2,14},{3,15},{4,0},{5,1},{6,2},{7,3},{8,4},{9,5},{1... | collective-permute-start | bytes 1179656 | tf_op jit(solution)/shard_map/head_z/ppermute | solution.py:33
  7.8 2.9 %copy-done = bf16[5,128,5120]{2,1,0:T(8,128)(2,1)S(1)} copy-done((bf16[5,128,5120]{2,1,0:T(8,128)(2,1)S(1)}, bf16[5,128,5120]{2,1,0:T(8,128)(2,1)}, u32[]{:S(2)}) %copy-start) | copy-done | bytes 6553624
  10.7 3.4 %weights_y.1 = bf16[640,2560]{1,0:T(8,128)(2,1)} custom-call(s32[5]{0:T(128)S(1)} %stack.70.where_ref, bf16[5,128,5120]{2,1,0:T(8,128)(2,1)S(1)} %copy-done), custom_call_target="tpu_custom_call" | custom-call | flops 20000000000 | bytes 1024 | tf_op jit(solution)/shard_map/weights_y/pallas_call | solution.py:330
  14.2 1.0 slice_bitcast_fusion.2.own
  15.2 7.9 %collective-permute-done.one.kvq1 = bf16[3,512,128]{2,1,0:T(8,128)(2,1)S(1)} collective-permute-done((bf16[3,512,128]{2,1,0:T(8,128)(2,1)S(1)}, bf16[3,512,128]{2,1,0:T(8,128)(2,1)S(1)}, u32[]{:S(2)}, u32[]{:S(2)}) %collective-permute-start) | collective-permute-done | bytes 393248 | tf_op jit(solution)/shard_map/head_z/ppermute | solution.py:33
  23.1 4.3 %collective-permute-done.2.three.kvq3 = bf16[3,512,128]{2,1,0:T(8,128)(2,1)S(1)} collective-permute-done((bf16[3,512,128]{2,1,0:T(8,128)(2,1)S(1)}, bf16[3,512,128]{2,1,0:T(8,128)(2,1)S(1)}, u32[]{:S(2)}, u32[]{:S(2)}) %collective-permute-start.2) | collective-permute-done | bytes 393248 | tf_op jit(solution)/shard_map/head_z/ppermute | solution.py:33
  28.0 1.2 %places.1.place_ref = s32[1,32]{1,0:T(1,128)S(1)} custom-call(s32[5]{0:T(128)S(1)} %stack.70.where_ref, s32[128,128]{1,0:T(8,128)S(1)} %copy-done.1), custom_call_target="tpu_custom_call" | custom-call | flops 10000000000 | bytes 1024 | tf_op jit(solution)/shard_map/places/pallas_call | solution.py:90
  29.4 0.9 slice_bitcast_fusion.3
  30.3 0.8 collective-permute-start.4
  31.1 0.8 collective-permute-start.5
  31.9 3.1 %collective-permute-start.6 = (bf16[2,2,512,128]{3,2,1,0:T(8,128)(2,1)S(1)}, bf16[2,2,512,128]{3,2,1,0:T(8,128)(2,1)S(1)}, u32[]{:S(2)}, u32[]{:S(2)}) collective-permute-start(bf16[2,2,512,128]{3,2,1,0:T(8,128)(2,1)S(1)} %get-tuple-element.21), channel_id=1, source_target_pairs={{0,16},{1,17},{2,18},{3,19},{4,20},{5,21},{6,22},{7,23},{8,24},{9,... | collective-permute-start | bytes 1572872 | tf_op jit(solution)/shard_map/head_x/ppermute | solution.py:33
  35.0 1.4 %collective-permute-done.3.one = bf16[2,512,128]{2,1,0:T(8,128)(2,1)S(1)} collective-permute-done((bf16[2,512,128]{2,1,0:T(8,128)(2,1)S(1)}, bf16[2,512,128]{2,1,0:T(8,128)(2,1)S(1)}, u32[]{:S(2)}, u32[]{:S(2)}) %collective-permute-start.3) | collective-permute-done | bytes 262176 | tf_op jit(solution)/shard_map/rest_z/ppermute | solution.py:33
  36.4 4.4 %collective-permute-start.7 = (bf16[2,2,512,128]{3,2,1,0:T(8,128)(2,1)S(1)}, bf16[2,2,512,128]{3,2,1,0:T(8,128)(2,1)S(1)}, u32[]{:S(2)}, u32[]{:S(2)}) collective-permute-start(bf16[2,2,512,128]{3,2,1,0:T(8,128)(2,1)S(1)} %get-tuple-element.28), channel_id=1, source_target_pairs={{16,0},{17,1},{18,2},{19,3},{20,4},{21,5},{22,6},{23,7},{24,8},{25... | collective-permute-start | bytes 1572872 | tf_op jit(solution)/shard_map/head_x/ppermute | solution.py:33
  40.8 5.1 %near_attention.1 = (bf16[2048,128]{1,0:T(8,128)(2,1)S(1)}, f32[2048,128]{1,0:T(8,128)S(1)}, f32[2048,128]{1,0:T(8,128)S(1)}) custom-call(s32[5]{0:T(128)S(1)} %stack.70.where_ref, s32[1,32]{1,0:T(1,128)S(1)} %places.1.place_ref, bf16[3,512,128]{2,1,0:T(8,128)(2,1)S(1)} %get-tuple-element.48.own.kvq0, ...), custom_call_target="tpu_custom_call" | custom-call | flops 10000000000 | bytes 1024 | tf_op jit(solution)/shard_map/near_attention/pallas_call | solution.py:90
  46.5 2.9 %collective-permute-start.11 = (bf16[2,2,512,128]{3,2,1,0:T(8,128)(2,1)S(1)}, bf16[2,2,512,128]{3,2,1,0:T(8,128)(2,1)S(1)}, u32[]{:S(2)}, u32[]{:S(2)}) collective-permute-start(bf16[2,2,512,128]{3,2,1,0:T(8,128)(2,1)S(1)} %rest_pick.1), channel_id=1, source_target_pairs={{0,16},{1,17},{2,18},{3,19},{4,20},{5,21},{6,22},{7,23},{16,32},{1... | collective-permute-start | bytes 1572872 | tf_op jit(solution)/shard_map/rest_x/ppermute | solution.py:33
  49.5 4.3 %halo_attention.1 = (bf16[512,128]{1,0:T(8,128)(2,1)S(1)}, bf16[512,128]{1,0:T(8,128)(2,1)S(1)}, bf16[512,128]{1,0:T(8,128)(2,1)S(1)}, bf16[512,128]{1,0:T(8,128)(2,1)S(1)}) custom-call(s32[5]{0:T(128)S(1)} %stack.70.where_ref, s32[1,32]{1,0:T(1,128)S(1)} %places.1.place_ref, bf16[2048,128]{1,0:T(8,128)(2,1)S(1)} %get-tuple-element.23.qs, ...), custom_call_target="tpu_custom_call" | custom-call | flops 10000000000 | bytes 1024 | tf_op jit(solution)/shard_map/halo_attention/pallas_call | solution.py:90
  53.9 3.4 %collective-permute-start.8 = (bf16[512,128]{1,0:T(8,128)(2,1)S(1)}, bf16[512,128]{1,0:T(8,128)(2,1)S(1)}, u32[]{:S(2)}, u32[]{:S(2)}) collective-permute-start(bf16[512,128]{1,0:T(8,128)(2,1)S(1)} %get-tuple-element.30), channel_id=1, source_target_pairs={{0,12},{1,13},{2,14},{3,15},{4,0},{5,1},{6,2},{7,3},{8,4},{9,5},{1... | collective-permute-start | bytes 393224 | tf_op jit(solution)/shard_map/attended_z/ppermute | solution.py:33
  57.2 1.0 collective-permute-start.9
  58.2 0.8 collective-permute-start.10
  59.2 3.6 %collective-permute-done.9 = bf16[512,128]{1,0:T(8,128)(2,1)S(1)} collective-permute-done((bf16[512,128]{1,0:T(8,128)(2,1)S(1)}, bf16[512,128]{1,0:T(8,128)(2,1)S(1)}, u32[]{:S(2)}, u32[]{:S(2)}) %collective-permute-start.9) | collective-permute-done | bytes 131104 | tf_op jit(solution)/shard_map/attended_z/ppermute | solution.py:33
  62.9 1.4 %collective-permute-done.10 = bf16[512,128]{1,0:T(8,128)(2,1)S(1)} collective-permute-done((bf16[512,128]{1,0:T(8,128)(2,1)S(1)}, bf16[512,128]{1,0:T(8,128)(2,1)S(1)}, u32[]{:S(2)}, u32[]{:S(2)}) %collective-permute-start.10) | collective-permute-done | bytes 131104 | tf_op jit(solution)/shard_map/attended_z/ppermute | solution.py:33
  64.3 3.5 %rest_attention.1.m0 = bf16[5,512,128]{2,1,0:T(8,128)(2,1)S(1)} fusion(bf16[5,512,128]{2,1,0:T(8,128)(2,1)S(1)} %bitcast_dynamic-update-slice_fusion.1, s32[5]{0:T(128)S(1)} %stack.70.where_ref, s32[1,32]{1,0:T(1,128)S(1)} %places.1.place_ref, bf16[2,512,128]{2,1,0:T(8,128)(2,1)S(1)} %slice_bitcast_fusion.2.own, ...), kind=kCustom, calls=%fused_computation.12 | custom fusion | flops 10000000000 | bytes 1836032 | tf_op jit(solution)/shard_map/rest_attention/pallas_call | solution.py:90
  67.8 2.1 %constant_dynamic-slice_fusion = (bf16[640,1280]{1,0:T(8,128)(2,1)S(1)}, bf16[1,640,1280]{2,1,0:T(8,128)(2,1)S(1)}) fusion(bf16[640,2560]{1,0:T(8,128)(2,1)} %collective-permute-done.12, s32[]{:T(128)S(6)} %select_n.74, s32[]{:T(128)S(6)} %select_n.73), kind=kLoop, calls=%fused_computation.17 | loop fusion | bytes 6553608 | tf_op jit(solution)/shard_map/weights_core/dynamic_slice | solution.py:415
  70.7 9.3 %collective-permute-start.14 = (bf16[2,640,1280]{2,1,0:T(8,128)(2,1)S(1)}, bf16[2,640,1280]{2,1,0:T(8,128)(2,1)S(1)}, u32[]{:S(2)}, u32[]{:S(2)}) collective-permute-start(bf16[2,640,1280]{2,1,0:T(8,128)(2,1)S(1)} %pad_maximum_fusion), channel_id=1, source_target_pairs={{0,1},{1,0},{2,3},{3,2},{4,5},{5,4},{6,7},{7,6},{8,9},{9,8},{10,11... | collective-permute-start | bytes 9830408 | tf_op jit(solution)/shard_map/weights_core/ppermute | solution.py:33
  80.1 5.4 %collective-permute-done.14 = bf16[2,640,1280]{2,1,0:T(8,128)(2,1)S(1)} collective-permute-done((bf16[2,640,1280]{2,1,0:T(8,128)(2,1)S(1)}, bf16[2,640,1280]{2,1,0:T(8,128)(2,1)S(1)}, u32[]{:S(2)}, u32[]{:S(2)}) %collective-permute-start.14) | collective-permute-done | bytes 3276832 | tf_op jit(solution)/shard_map/weights_core/ppermute | solution.py:33
  85.7 0.7 collective-permute-done.13.m1
  86.4 3.6 %project.1.before = f32[512,1280]{1,0:T(8,128)S(1)} custom-call(s32[5]{0:T(128)S(1)} %stack.70.where_ref, bf16[5,512,128]{2,1,0:T(8,128)(2,1)S(1)} %rest_attention.1.m0, bf16[640,1280]{1,0:T(8,128)(2,1)S(1)} %get-tuple-element.38.w0, bf16[5,512,128]{2,1,0:T(8,128)(2,1)S(1)} %collective-permute-done.13.m1, bf16[640,1280]{1,0:T(8,128)(2,1)S(1)} %get-tuple-element.40.w1), custom_call_target="tpu_custom_call" | custom-call | flops 10000000000 | bytes 1024 | tf_op jit(solution)/shard_map/project/pallas_call | solution.py:90
  90.0 6.0 %collective-permute-done.15.m0 = bf16[5,512,128]{2,1,0:T(8,128)(2,1)S(1)} collective-permute-done((bf16[5,512,128]{2,1,0:T(8,128)(2,1)S(1)}, bf16[5,512,128]{2,1,0:T(8,128)(2,1)S(1)}, u32[]{:S(2)}, u32[]{:S(2)}) %collective-permute-start.15) | collective-permute-done | bytes 655392 | tf_op jit(solution)/shard_map/attended_y/ppermute | solution.py:33
  96.0 1.3 %collective-permute-start.16 = (bf16[5,512,128]{2,1,0:T(8,128)(2,1)S(1)}, bf16[5,512,128]{2,1,0:T(8,128)(2,1)S(1)}, u32[]{:S(2)}, u32[]{:S(2)}) collective-permute-start(bf16[5,512,128]{2,1,0:T(8,128)(2,1)S(1)} %collective-permute-done.15.m0), channel_id=1, source_target_pairs={{0,1},{1,0},{2,3},{3,2},{4,5},{5,4},{6,7},{7,6},{8,9},{9,8},{10,11... | collective-permute-start | bytes 1966088 | tf_op jit(solution)/shard_map/far_core/ppermute | solution.py:33
  97.2 1.7 %collective-permute-done.16.m1 = bf16[5,512,128]{2,1,0:T(8,128)(2,1)S(1)} collective-permute-done((bf16[5,512,128]{2,1,0:T(8,128)(2,1)S(1)}, bf16[5,512,128]{2,1,0:T(8,128)(2,1)S(1)}, u32[]{:S(2)}, u32[]{:S(2)}) %collective-permute-start.16) | collective-permute-done | bytes 655392 | tf_op jit(solution)/shard_map/far_core/ppermute | solution.py:33
  98.9 4.7 %finish.1 = bf16[512,1280]{1,0:T(8,128)(2,1)} custom-call(s32[5]{0:T(128)S(1)} %stack.70.where_ref, bf16[5,512,128]{2,1,0:T(8,128)(2,1)S(1)} %collective-permute-done.15.m0, bf16[640,1280]{1,0:T(8,128)(2,1)S(1)} %get-tuple-element.41.w0, bf16[5,512,128]{2,1,0:T(8,128)(2,1)S(1)} %collective-permute-done.16.m1, bf16[640,1280]{1,0:T(8,128)(2,1)S(1)} %get-tuple-element.39.w1, ...), custom_call_target="tpu_custom_call" | custom-call | flops 1024 | bytes 1024 | tf_op jit(solution)/shard_map/finish/pallas_call | solution.py:90
  (33 shorter events, 3.7 us)
Async XLA Ops:
  3.2 19.9 %collective-permute-start = (bf16[3,512,128]{2,1,0:T(8,128)(2,1)S(1)}, bf16[3,512,128]{2,1,0:T(8,128)(2,1)S(1)}, u32[]{:S(2)}, u32[]{:S(2)}) collective-permute-start(bf16[3,512,128]{2,1,0:T(8,128)(2,1)S(1)} %get-tuple-element.47), channel_id=1, source_target_pairs={{0,12},{1,13},{2,14},{3,15},{4,0},{5,1},{6,2},{7,3},{8,4},{9,5},{1... | collective-permute-start | bytes 1179656 | tf_op jit(solution)/shard_map/head_z/ppermute | solution.py:33
  7.1 16.1 %collective-permute-start.1 = (bf16[3,512,128]{2,1,0:T(8,128)(2,1)S(1)}, bf16[3,512,128]{2,1,0:T(8,128)(2,1)S(1)}, u32[]{:S(2)}, u32[]{:S(2)}) collective-permute-start(bf16[3,512,128]{2,1,0:T(8,128)(2,1)S(1)} %get-tuple-element.46), channel_id=1, source_target_pairs={{0,8},{1,9},{2,10},{3,11},{4,12},{5,13},{6,14},{7,15},{8,0},{9,1},... | collective-permute-start | bytes 1179656 | tf_op jit(solution)/shard_map/head_z/ppermute | solution.py:33
  7.1 20.3 %collective-permute-start.2 = (bf16[3,512,128]{2,1,0:T(8,128)(2,1)S(1)}, bf16[3,512,128]{2,1,0:T(8,128)(2,1)S(1)}, u32[]{:S(2)}, u32[]{:S(2)}) collective-permute-start(bf16[3,512,128]{2,1,0:T(8,128)(2,1)S(1)} %get-tuple-element.45), channel_id=1, source_target_pairs={{0,4},{1,5},{2,6},{3,7},{4,8},{5,9},{6,10},{7,11},{8,12},{9,13},{1... | collective-permute-start | bytes 1179656 | tf_op jit(solution)/shard_map/head_z/ppermute | solution.py:33
  7.8 2.9 %copy-start = (bf16[5,128,5120]{2,1,0:T(8,128)(2,1)S(1)}, bf16[5,128,5120]{2,1,0:T(8,128)(2,1)}, u32[]{:S(2)}) copy-start(bf16[5,128,5120]{2,1,0:T(8,128)(2,1)} %weight) | copy-start | bytes 19660804
  14.1 13.9 %copy-start.1 = (s32[128,128]{1,0:T(8,128)S(1)}, s32[128,128]{1,0:T(8,128)}, u32[]{:S(2)}) copy-start(s32[128,128]{1,0:T(8,128)} %mask_ref) | copy-start | bytes 196612
  14.1 53.8 %collective-permute-start.12 = (bf16[640,2560]{1,0:T(8,128)(2,1)}, bf16[640,2560]{1,0:T(8,128)(2,1)}, u32[]{:S(2)}, u32[]{:S(2)}) collective-permute-start(bf16[640,2560]{1,0:T(8,128)(2,1)} %weights_y.1), channel_id=1, source_target_pairs={{0,2},{1,67},{2,64},{3,1},{4,6},{5,71},{6,68},{7,5},{8,10},{9,75},... | collective-permute-start | bytes 9830408 | tf_op jit(solution)/shard_map/weights_y/ppermute | solution.py:33
  29.3 7.2 %collective-permute-start.3 = (bf16[2,512,128]{2,1,0:T(8,128)(2,1)S(1)}, bf16[2,512,128]{2,1,0:T(8,128)(2,1)S(1)}, u32[]{:S(2)}, u32[]{:S(2)}) collective-permute-start(bf16[2,512,128]{2,1,0:T(8,128)(2,1)S(1)} %slice_bitcast_fusion.2.own), channel_id=1, source_target_pairs={{0,12},{1,13},{2,14},{3,15},{4,0},{5,1},{6,2},{7,3},{8,4},{9,5},{1... | collective-permute-start | bytes 786440 | tf_op jit(solution)/shard_map/rest_z/ppermute | solution.py:33
  30.3 15.6 %collective-permute-start.4 = (bf16[2,512,128]{2,1,0:T(8,128)(2,1)S(1)}, bf16[2,512,128]{2,1,0:T(8,128)(2,1)S(1)}, u32[]{:S(2)}, u32[]{:S(2)}) collective-permute-start(bf16[2,512,128]{2,1,0:T(8,128)(2,1)S(1)} %slice_bitcast_fusion.2.own), channel_id=1, source_target_pairs={{0,8},{1,9},{2,10},{3,11},{4,12},{5,13},{6,14},{7,15},{8,0},{9,1},... | collective-permute-start | bytes 786440 | tf_op jit(solution)/shard_map/rest_z/ppermute | solution.py:33
  31.1 14.8 %collective-permute-start.5 = (bf16[2,512,128]{2,1,0:T(8,128)(2,1)S(1)}, bf16[2,512,128]{2,1,0:T(8,128)(2,1)S(1)}, u32[]{:S(2)}, u32[]{:S(2)}) collective-permute-start(bf16[2,512,128]{2,1,0:T(8,128)(2,1)S(1)} %slice_bitcast_fusion.2.own), channel_id=1, source_target_pairs={{0,4},{1,5},{2,6},{3,7},{4,8},{5,9},{6,10},{7,11},{8,12},{9,13},{1... | collective-permute-start | bytes 786440 | tf_op jit(solution)/shard_map/rest_z/ppermute | solution.py:33
  31.9 17.6 %collective-permute-start.6 = (bf16[2,2,512,128]{3,2,1,0:T(8,128)(2,1)S(1)}, bf16[2,2,512,128]{3,2,1,0:T(8,128)(2,1)S(1)}, u32[]{:S(2)}, u32[]{:S(2)}) collective-permute-start(bf16[2,2,512,128]{3,2,1,0:T(8,128)(2,1)S(1)} %get-tuple-element.21), channel_id=1, source_target_pairs={{0,16},{1,17},{2,18},{3,19},{4,20},{5,21},{6,22},{7,23},{8,24},{9,... | collective-permute-start | bytes 1572872 | tf_op jit(solution)/shard_map/head_x/ppermute | solution.py:33
  36.4 13.1 %collective-permute-start.7 = (bf16[2,2,512,128]{3,2,1,0:T(8,128)(2,1)S(1)}, bf16[2,2,512,128]{3,2,1,0:T(8,128)(2,1)S(1)}, u32[]{:S(2)}, u32[]{:S(2)}) collective-permute-start(bf16[2,2,512,128]{3,2,1,0:T(8,128)(2,1)S(1)} %get-tuple-element.28), channel_id=1, source_target_pairs={{16,0},{17,1},{18,2},{19,3},{20,4},{21,5},{22,6},{23,7},{24,8},{25... | collective-permute-start | bytes 1572872 | tf_op jit(solution)/shard_map/head_x/ppermute | solution.py:33
  46.5 17.7 %collective-permute-start.11 = (bf16[2,2,512,128]{3,2,1,0:T(8,128)(2,1)S(1)}, bf16[2,2,512,128]{3,2,1,0:T(8,128)(2,1)S(1)}, u32[]{:S(2)}, u32[]{:S(2)}) collective-permute-start(bf16[2,2,512,128]{3,2,1,0:T(8,128)(2,1)S(1)} %rest_pick.1), channel_id=1, source_target_pairs={{0,16},{1,17},{2,18},{3,19},{4,20},{5,21},{6,22},{7,23},{16,32},{1... | collective-permute-start | bytes 1572872 | tf_op jit(solution)/shard_map/rest_x/ppermute | solution.py:33
  49.5 20.4 %slice-start = ((s8[6553600]{0:T(1024)(128)(4,1)}), s8[4194304]{0:T(1024)(128)(4,1)S(1)}, s32[]{:S(2)}) async-start(s8[6553600]{0:T(1024)(128)(4,1)} %bitcast.41), calls=%async_computation | async-start | bytes 8388608
  53.9 5.3 %collective-permute-start.8 = (bf16[512,128]{1,0:T(8,128)(2,1)S(1)}, bf16[512,128]{1,0:T(8,128)(2,1)S(1)}, u32[]{:S(2)}, u32[]{:S(2)}) collective-permute-start(bf16[512,128]{1,0:T(8,128)(2,1)S(1)} %get-tuple-element.30), channel_id=1, source_target_pairs={{0,12},{1,13},{2,14},{3,15},{4,0},{5,1},{6,2},{7,3},{8,4},{9,5},{1... | collective-permute-start | bytes 393224 | tf_op jit(solution)/shard_map/attended_z/ppermute | solution.py:33
  57.2 5.6 %collective-permute-start.9 = (bf16[512,128]{1,0:T(8,128)(2,1)S(1)}, bf16[512,128]{1,0:T(8,128)(2,1)S(1)}, u32[]{:S(2)}, u32[]{:S(2)}) collective-permute-start(bf16[512,128]{1,0:T(8,128)(2,1)S(1)} %get-tuple-element.31), channel_id=1, source_target_pairs={{0,8},{1,9},{2,10},{3,11},{4,12},{5,13},{6,14},{7,15},{8,0},{9,1},... | collective-permute-start | bytes 393224 | tf_op jit(solution)/shard_map/attended_z/ppermute | solution.py:33
  58.2 6.0 %collective-permute-start.10 = (bf16[512,128]{1,0:T(8,128)(2,1)S(1)}, bf16[512,128]{1,0:T(8,128)(2,1)S(1)}, u32[]{:S(2)}, u32[]{:S(2)}) collective-permute-start(bf16[512,128]{1,0:T(8,128)(2,1)S(1)} %get-tuple-element.32), channel_id=1, source_target_pairs={{0,4},{1,5},{2,6},{3,7},{4,8},{5,9},{6,10},{7,11},{8,12},{9,13},{1... | collective-permute-start | bytes 393224 | tf_op jit(solution)/shard_map/attended_z/ppermute | solution.py:33
  64.3 5.7 %slice-start.1 = ((s8[6553600]{0:T(1024)(128)(4,1)}), s8[2359296]{0:T(1024)(128)(4,1)S(1)}, s32[]{:S(2)}) async-start(s8[6553600]{0:T(1024)(128)(4,1)} %bitcast.41), calls=%async_computation.1 | async-start | bytes 4718592
  70.7 14.8 %collective-permute-start.14 = (bf16[2,640,1280]{2,1,0:T(8,128)(2,1)S(1)}, bf16[2,640,1280]{2,1,0:T(8,128)(2,1)S(1)}, u32[]{:S(2)}, u32[]{:S(2)}) collective-permute-start(bf16[2,640,1280]{2,1,0:T(8,128)(2,1)S(1)} %pad_maximum_fusion), channel_id=1, source_target_pairs={{0,1},{1,0},{2,3},{3,2},{4,5},{5,4},{6,7},{7,6},{8,9},{9,8},{10,11... | collective-permute-start | bytes 9830408 | tf_op jit(solution)/shard_map/weights_core/ppermute | solution.py:33
  80.0 6.4 %collective-permute-start.13 = (bf16[5,512,128]{2,1,0:T(8,128)(2,1)S(1)}, bf16[5,512,128]{2,1,0:T(8,128)(2,1)S(1)}, u32[]{:S(2)}, u32[]{:S(2)}) collective-permute-start(bf16[5,512,128]{2,1,0:T(8,128)(2,1)S(1)} %rest_attention.1.m0), channel_id=1, source_target_pairs={{0,1},{1,0},{2,3},{3,2},{4,5},{5,4},{6,7},{7,6},{8,9},{9,8},{10,11... | collective-permute-start | bytes 1966088 | tf_op jit(solution)/shard_map/attended_core/ppermute | solution.py:33
  80.1 15.9 %collective-permute-start.15 = (bf16[5,512,128]{2,1,0:T(8,128)(2,1)S(1)}, bf16[5,512,128]{2,1,0:T(8,128)(2,1)S(1)}, u32[]{:S(2)}, u32[]{:S(2)}) collective-permute-start(bf16[5,512,128]{2,1,0:T(8,128)(2,1)S(1)} %rest_attention.1.m0), channel_id=1, source_target_pairs={{0,2},{1,3},{2,0},{3,1},{4,6},{5,7},{6,4},{7,5},{8,10},{9,11},{10,... | collective-permute-start | bytes 1966088 | tf_op jit(solution)/shard_map/attended_y/ppermute | solution.py:33
  96.0 3.0 %collective-permute-start.16 = (bf16[5,512,128]{2,1,0:T(8,128)(2,1)S(1)}, bf16[5,512,128]{2,1,0:T(8,128)(2,1)S(1)}, u32[]{:S(2)}, u32[]{:S(2)}) collective-permute-start(bf16[5,512,128]{2,1,0:T(8,128)(2,1)S(1)} %collective-permute-done.15.m0), channel_id=1, source_target_pairs={{0,1},{1,0},{2,3},{3,2},{4,5},{5,4},{6,7},{7,6},{8,9},{9,8},{10,11... | collective-permute-start | bytes 1966088 | tf_op jit(solution)/shard_map/far_core/ppermute | solution.py:33

commit v3 on v2

--- a/solution.py
+++ b/solution.py
@@ -40,11 +40,12 @@
     return [minus, two, plus]
 
 
-def after(first, *then):
-    return list(lax.optimization_barrier((tuple(first), tuple(then)))[1])
-
-
-def places_kernel(where_ref, mask_ref, out):
+def together(*arrays):
+    return lax.optimization_barrier(arrays)
+
+
+def places_kernel(where_ref, mask_ref, rest_ref, out, rest_out):
+    rest_out[...] = rest_ref[...]
     count = mask_ref.shape[0]
     start = where_ref[3]
     pick = lax.broadcasted_iota(jnp.int32, (4 * SLAB, count), 1) - lax.broadcasted_iota(jnp.int32, (4 * SLAB, count), 0)
@@ -86,16 +87,22 @@
 SCALARS = pl.BlockSpec(memory_space=pltpu.SMEM)
 
 
-def call(kernel, outs, scratch, operands, scalars, flops=1024):
+def call(kernel, outs, scratch, operands, scalars, flops=1024, later=(), far=0):
+    held = len(operands) - scalars - far
+
+    def body(*refs):
+        at = len(operands)
+        kernel(*refs[:at], *refs[at + len(later) :])
+
     return pl.pallas_call(
-        kernel,
+        body,
         out_shape=outs,
-        in_specs=[SCALARS] * scalars + [ANYWHERE] * (len(operands) - scalars),
+        in_specs=[SCALARS] * scalars + [ANYWHERE] * held + [pl.BlockSpec(memory_space=pl.ANY)] * (far + len(later)),
         out_specs=jax.tree.map(lambda _: ANYWHERE, outs),
         scratch_shapes=scratch,
         compiler_params=pltpu.CompilerParams(vmem_limit_bytes=VMEM_LIMIT),
         cost_estimate=pl.CostEstimate(flops=flops, bytes_accessed=1024, transcendentals=0),
-    )(*operands)
+    )(*operands, *later)
 
 
 def pick_kernel(where_ref, own, one, two, three, up, down):
@@ -290,8 +297,38 @@
         out[:, at] = (part + before[:, at]).astype(out.dtype)
 
 
-def columns_kernel(where_ref, weight, out):
-    out[...] = weight[0]
+def fetch(copies):
+    for copy in copies:
+        copy.start()
+    for copy in copies:
+        copy.wait()
+
+
+def theirs_kernel(where_ref, weight, out, sem):
+    heads, _, width = weight.shape
+    at = pl.ds(pl.multiple_of((1 - where_ref[4]) * (width // 2), TILE), width // 2)
+    fetch([pltpu.make_async_copy(weight.at[h, :, at], out.at[spot(h), :], sem.at[h]) for h in range(heads)])
+
+
+def own_halves_kernel(where_ref, weight, mine, other, sem):
+    heads, _, width = weight.shape
+    cols, c = width // 4, where_ref[5]
+    copies = []
+    for k, (out, core) in enumerate(((mine, c), (other, 1 - c))):
+        at = pl.ds(pl.multiple_of((where_ref[4] * 2 + core) * cols, TILE), cols)
+        copies += [
+            pltpu.make_async_copy(weight.at[h, :, at], out.at[spot(h), :], sem.at[k * heads + h]) for h in range(heads)
+        ]
+    fetch(copies)
+
+
+def far_halves_kernel(where_ref, weight, mine, other, sem):
+    cols, c = weight.shape[1] // 2, where_ref[5]
+    copies = []
+    for k, (out, core) in enumerate(((mine, c), (other, 1 - c))):
+        at = pl.ds(pl.multiple_of(core * cols, TILE), cols)
+        copies.append(pltpu.make_async_copy(weight.at[:, at], out, sem.at[k]))
+    fetch(copies)
 
 
 def local(queries, key_rows, value_rows, out_weight, tile_mask):
@@ -324,21 +361,17 @@
         ring = along_z(out, rows)
 
     with jax.named_scope("weights_y"):
-        lead = send(out[0][0, :16], rows, lambda r, z, yl, c: (r, (z + 1) % ROW, yl, c))
-        (out_weight,) = after([lead], out_weight)
-        where = jnp.stack([z, row > 0, row < rows - 1, row * 2 * SLAB - SLAB, yl]).astype(jnp.int32)
-        theirs = pl.pallas_call(
-            columns_kernel,
-            out_shape=jax.ShapeDtypeStruct((heads * size, wide_cols), bf),
-            grid_spec=pltpu.PrefetchScalarGridSpec(
-                num_scalar_prefetch=1,
-                grid=(heads,),
-                in_specs=[pl.BlockSpec((1, size, wide_cols), lambda h, where: (h, 0, 1 - where[4]))],
-                out_specs=pl.BlockSpec((size, wide_cols), lambda h, where: (h, 0)),
-            ),
-            compiler_params=pltpu.CompilerParams(vmem_limit_bytes=VMEM_LIMIT),
-            cost_estimate=pl.CostEstimate(flops=2 * 10**10, bytes_accessed=1024, transcendentals=0),
-        )(where, out_weight)
+        where = jnp.stack([z, row > 0, row < rows - 1, row * 2 * SLAB - SLAB, yl, c]).astype(jnp.int32)
+        theirs = call(
+            theirs_kernel,
+            jax.ShapeDtypeStruct((heads * size, wide_cols), bf),
+            [pltpu.SemaphoreType.DMA((heads,))],
+            [where, out_weight],
+            1,
+            later=out[:1],
+            far=1,
+            flops=8000000000,
+        )
 
         def y_step(r, z, yl, c):
             yh, x = r // ROW, r % ROW
@@ -353,13 +386,26 @@
         from_prev = send(to_next, rows, lambda r, z, yl, c: (r + 1, z, yl, c) if r + 1 < rows else None)
         from_next = send(to_prev, rows, lambda r, z, yl, c: (r - 1, z, yl, c) if r > 0 else None)
     with jax.named_scope("places"):
-        (tile_mask,) = after([to_next], tile_mask)
-        place = call(
-            places_kernel, jax.ShapeDtypeStruct((1, 4 * SLAB), jnp.int32), [], [where, tile_mask], 1, flops=10**10
+        place, kv_rest = call(
+            places_kernel,
+            (jax.ShapeDtypeStruct((1, 4 * SLAB), jnp.int32), jax.ShapeDtypeStruct((2, tok, size), bf)),
+            [],
+            [where, tile_mask, kv_rest],
+            1,
+            later=[to_next],
+            flops=8000000000,
         )
     with jax.named_scope("rest_z"):
-        (kv_rest,) = after([place], kv_rest)
         rest_in = along_z([kv_rest] * 3, rows)
+    with jax.named_scope("rest_pick"):
+        to_rest = call(pick_one_kernel, halo, [], [where, kv_rest, *rest_in], 1)
+    with jax.named_scope("rest_x"):
+
+        def rest_step(r, z, yl, c):
+            to = r + 1 if z < 2 else r - 1
+            return (to, z, yl, c) if 0 <= to < rows else None
+
+        rest_halo = send(to_rest, rows, rest_step)
     with jax.named_scope("near_attention"):
         qs, acc, stats = call(
             near_kernel,
@@ -371,74 +417,78 @@
             [pltpu.VMEM((row_tok, size), bf), pltpu.VMEM((row_tok, size), bf)],
             [where, place, own, *ring],
             2,
-            flops=10**10,
-        )
-    with jax.named_scope("rest_pick"):
-        to_rest = call(pick_one_kernel, halo, [], [where, kv_rest, *rest_in], 1)
-    with jax.named_scope("rest_x"):
-
-        def rest_step(r, z, yl, c):
-            to = r + 1 if z < 2 else r - 1
-            return (to, z, yl, c) if 0 <= to < rows else None
-
-        rest_halo = send(to_rest, rows, rest_step)
+            flops=8000000000,
+        )
     with jax.named_scope("halo_attention"):
-        (from_prev,) = after([to_rest], from_prev)
         o_own, *o_out = call(
             halo_kernel,
             (block,) * 4,
             [pltpu.VMEM((row_tok, size), bf)] * 3,
             [where, place, qs, acc, stats, from_prev, from_next],
             2,
-            flops=10**10,
+            later=[to_rest],
+            flops=1000000000,
         )
     with jax.named_scope("attended_z"):
         o_in = along_z(o_out, rows)
+    half = jax.ShapeDtypeStruct((heads * size, cols), bf)
+    with jax.named_scope("weights_core"):
+        w_own, w_own_other = call(
+            own_halves_kernel,
+            (half, half),
+            [pltpu.SemaphoreType.DMA((2 * heads,))],
+            [where, out_weight],
+            1,
+            later=[o_own],
+            far=1,
+        )
+        w_sib = sibling(w_own_other)
     with jax.named_scope("rest_attention"):
-        (rest_halo,) = after([o_own], rest_halo)
         o_rest = call(
             rest_kernel,
             block,
             [pltpu.VMEM((6 * tok, size), bf), pltpu.VMEM((6 * tok, size), bf)],
             [where, place, kv_rest, *rest_in, q_rest, rest_halo],
             2,
-            flops=10**10,
-        )
+            later=[o_own],
+            flops=3000000000,
+        )
+    with jax.named_scope("weights_far_core"):
+        w_y, w_y_other = call(
+            far_halves_kernel,
+            (half, half),
+            [pltpu.SemaphoreType.DMA((2,))],
+            [where, w_far],
+            1,
+            later=[o_rest],
+            far=1,
+            flops=1000000000,
+        )
+        w_y_sib = sibling(w_y_other)
     mine = jnp.stack([o_own, *o_in, o_rest])
     with jax.named_scope("attended_y"):
         far = y_pair(mine)
     with jax.named_scope("attended_core"):
         mine_sib = sibling(mine)
-    with jax.named_scope("weights_core"):
-
-        def halves(array, base):
-            mine = lax.dynamic_slice_in_dim(array, base + c * cols, cols, 1)
-            other = lax.dynamic_slice_in_dim(array, base + (1 - c) * cols, cols, 1)
-            return mine, other
-
-        flat, w_far = after([mine], out_weight.reshape(heads * size, 2 * wide_cols), w_far)
-        w_own, w_own_other = halves(flat, yl * wide_cols)
-        w_y, w_y_other = halves(w_far, 0)
-        w_sib = sibling(jnp.stack([w_own_other, w_y_other]))
     wide = pltpu.VMEM((tok, 2 * heads * size), bf)
     with jax.named_scope("project"):
         near = call(
             project_kernel,
             jax.ShapeDtypeStruct((tok, cols), jnp.float32),
             [wide],
-            [where, mine, w_own, mine_sib, w_sib[0]],
+            [where, mine, w_own, mine_sib, w_sib],
             1,
-            flops=10**10,
+            flops=10000000000,
         )
     with jax.named_scope("far_core"):
-        (far,) = after([near], far)
+        near, far = together(near, far)
         far_sib = sibling(far)
     with jax.named_scope("finish"):
         return call(
             finish_kernel,
             jax.ShapeDtypeStruct((tok, cols), bf),
             [wide],
-            [where, far, w_y, far_sib, w_sib[1], near],
+            [where, far, w_y, far_sib, w_y_sib, near],
             1,
         )
 

time: 105 us -> 100 us (0.952)
  other arithmetic: 6.94 us -> 3.04 us
  starting transfers between devices: 32.6 us -> 29.4 us
  Pallas kernels: 23.4 us -> 26.1 us
  local copies, waits for them, and re-layouts: 7.74 us -> 5.04 us
  waiting for transfers between devices: 32.6 us -> 34.9 us
    pallas_call x1 -> x0, other arithmetic: 3.54 us -> none  [call(): pl.pallas_call(kernel, out_shape=outs, in_specs=[SCALARS] * scalars + [AN...]
    ppermute x17 -> x18, starting transfers between devices: 32.6 us -> 29.4 us  [send(): return lax.ppermute(block, AXES, route(rows, target))]
    transpose x1 -> x0, other arithmetic: 3.1 us -> none  [local(): kvq = jnp.stack([key_rows, value_rows, queries]).transpose(2, 0, 1, 3)]
    another operation x1, other arithmetic: 0.3 us -> 3.04 us  [local(): kvq = jnp.stack([key_rows, value_rows, queries]).transpose(2, 0, 1, 3)]
    pallas_call x8 -> x11, Pallas kernels: 23.4 us -> 26.1 us  [call(): pl.pallas_call(body, out_shape=outs, in_specs=[SCALARS] * scalars + [ANYW...]
    ppermute x17 -> x18, waiting for transfers between devices: 32.6 us -> 34.9 us  [send(): return lax.ppermute(block, AXES, route(rows, target))]
    dynamic_slice x1 -> x0, local copies, waits for them, and re-layouts: 2.14 us -> none  [halves(): mine = lax.dynamic_slice_in_dim(array, base + c * cols, cols, 1)]
  transfers between devices with their start and end apart: 17 -> 18, of which waited for: 11 -> 7; matrix products, arithmetic and copies ran while one was open for 6% -> 2% of each run, Pallas kernels for 18% -> 22%
where the time goes in v3:
time: 100 us; the launch traced here: 98.7 us
  waiting for transfers between devices  34.9 us (35%)
  starting transfers between devices  29.4 us (29%)
  Pallas kernels  26.1 us (26%)
  local copies, waits for them, and re-layouts  5.04 us (5%)
  other arithmetic  3.04 us (3%)
    ppermute x18, waiting for transfers between devices, send(): return lax.ppermute(block, AXES, route(rows, target))  34.9 us
    ppermute x18, starting transfers between devices, send(): return lax.ppermute(block, AXES, route(rows, target))  29.4 us
    pallas_call x11, Pallas kernels, call(): pl.pallas_call(body, out_shape=outs, in_specs=[SCALARS] * scalars + [ANYW...  26.1 us
    another operation x1, other arithmetic, local(): kvq = jnp.stack([key_rows, value_rows, queries]).transpose(2, 0, 1, 3)  3.04 us
    unnamed x12, local copies, waits for them, and re-layouts  2.95 us
  transfers between devices with their start and end apart: 18, of which 7 were waited for; matrix products, arithmetic and copies ran while one was open for 2% of the time, Pallas kernels for 22%

profile of v3, /device:TPU:17, one launch (start us, length us, event | category | flops | bytes accessed | tf_op | source)
XLA Modules:
  0.0 98.7 jit_solution(16010259958258927129)
XLA Ops:
  0.0 3.0 %pad_maximum_fusion = (bf16[3,512,5,128]{3,1,0,2:T(8,128)(2,1)S(1)}, bf16[5,3,512,128]{3,2,1,0:T(8,128)(2,1)}) fusion(bf16[1,512,5,128]{3,1,0,2:T(8,128)(2,1)} %bitcast.35, bf16[1,512,5,128]{3,1,0,2:T(8,128)(2,1)} %bitcast.36, bf16[1,512,5,128]{3,1,0,2:T(8,128)(2,1)} %bitcast.37), kind=kLoop, calls=%fused_computation | loop fusion | flops 1966080 | bytes 5898240 | tf_op jit(solution)/shard_map/lay_out/stack | solution.py:357
  3.2 3.8 %collective-permute-start = (bf16[3,512,128]{2,1,0:T(8,128)(2,1)S(1)}, bf16[3,512,128]{2,1,0:T(8,128)(2,1)S(1)}, u32[]{:S(2)}, u32[]{:S(2)}) collective-permute-start(bf16[3,512,128]{2,1,0:T(8,128)(2,1)S(1)} %get-tuple-element.41), channel_id=1, source_target_pairs={{0,12},{1,13},{2,14},{3,15},{4,0},{5,1},{6,2},{7,3},{8,4},{9,5},{1... | collective-permute-start | bytes 1179656 | tf_op jit(solution)/shard_map/head_z/ppermute | solution.py:33
  7.8 2.9 %copy-done = bf16[5,128,5120]{2,1,0:T(8,128)(2,1)S(1)} copy-done((bf16[5,128,5120]{2,1,0:T(8,128)(2,1)S(1)}, bf16[5,128,5120]{2,1,0:T(8,128)(2,1)}, u32[]{:S(2)}) %copy-start) | copy-done | bytes 6553624
  10.6 0.9 weights_y.1
  11.8 1.0 slice_bitcast_fusion.refs_2_
  12.7 10.3 %collective-permute-done.refs_2_.refs_3_ = bf16[3,512,128]{2,1,0:T(8,128)(2,1)S(1)} collective-permute-done((bf16[3,512,128]{2,1,0:T(8,128)(2,1)S(1)}, bf16[3,512,128]{2,1,0:T(8,128)(2,1)S(1)}, u32[]{:S(2)}, u32[]{:S(2)}) %collective-permute-start) | collective-permute-done | bytes 393248 | tf_op jit(solution)/shard_map/head_z/ppermute | solution.py:33
  23.0 4.3 %collective-permute-done.2.refs_4_.refs_5_ = bf16[3,512,128]{2,1,0:T(8,128)(2,1)S(1)} collective-permute-done((bf16[3,512,128]{2,1,0:T(8,128)(2,1)S(1)}, bf16[3,512,128]{2,1,0:T(8,128)(2,1)S(1)}, u32[]{:S(2)}, u32[]{:S(2)}) %collective-permute-start.2) | collective-permute-done | bytes 393248 | tf_op jit(solution)/shard_map/head_z/ppermute | solution.py:33
  28.0 1.2 %places.1 = (s32[1,32]{1,0:T(1,128)S(1)}, bf16[2,512,128]{2,1,0:T(8,128)(2,1)S(1)}) custom-call(s32[6]{0:T(128)S(1)} %stack.65.refs_0_, s32[128,128]{1,0:T(8,128)S(1)} %copy-done.1, bf16[2,512,128]{2,1,0:T(8,128)(2,1)S(1)} %slice_bitcast_fusion.refs_2_, bf16[2,2,512,128]{3,2,1,0:T(8,128)(2,1)S(1)} %get-tuple-element.22.refs_3_), custom_call_target="tpu_custom_call" | custom-call | flops 8000000000 | bytes 1024 | tf_op jit(solution)/shard_map/places/pallas_call | solution.py:97
  29.3 0.9 slice_bitcast_fusion.1.refs_6_
  30.2 3.1 %collective-permute-start.3 = (bf16[2,2,512,128]{3,2,1,0:T(8,128)(2,1)S(1)}, bf16[2,2,512,128]{3,2,1,0:T(8,128)(2,1)S(1)}, u32[]{:S(2)}, u32[]{:S(2)}) collective-permute-start(bf16[2,2,512,128]{3,2,1,0:T(8,128)(2,1)S(1)} %get-tuple-element.22.refs_3_), channel_id=1, source_target_pairs={{0,16},{1,17},{2,18},{3,19},{4,20},{5,21},{6,22},{7,23},{8,24},{9,... | collective-permute-start | bytes 1572872 | tf_op jit(solution)/shard_map/head_x/ppermute | solution.py:33
  34.1 0.9 collective-permute-start.7
  34.9 1.3 %collective-permute-done.5.refs_2_.refs_3_ = bf16[2,512,128]{2,1,0:T(8,128)(2,1)S(1)} collective-permute-done((bf16[2,512,128]{2,1,0:T(8,128)(2,1)S(1)}, bf16[2,512,128]{2,1,0:T(8,128)(2,1)S(1)}, u32[]{:S(2)}, u32[]{:S(2)}) %collective-permute-start.5) | collective-permute-done | bytes 262176 | tf_op jit(solution)/shard_map/rest_z/ppermute | solution.py:33
  36.3 4.5 %collective-permute-start.4 = (bf16[2,2,512,128]{3,2,1,0:T(8,128)(2,1)S(1)}, bf16[2,2,512,128]{3,2,1,0:T(8,128)(2,1)S(1)}, u32[]{:S(2)}, u32[]{:S(2)}) collective-permute-start(bf16[2,2,512,128]{3,2,1,0:T(8,128)(2,1)S(1)} %get-tuple-element.27), channel_id=1, source_target_pairs={{16,0},{17,1},{18,2},{19,3},{20,4},{21,5},{22,6},{23,7},{24,8},{25... | collective-permute-start | bytes 1572872 | tf_op jit(solution)/shard_map/head_x/ppermute | solution.py:33
  40.7 5.1 %near_attention.1 = (bf16[2048,128]{1,0:T(8,128)(2,1)S(1)}, f32[2048,128]{1,0:T(8,128)S(1)}, f32[2048,128]{1,0:T(8,128)S(1)}) custom-call(s32[6]{0:T(128)S(1)} %stack.65.refs_0_, s32[1,32]{1,0:T(1,128)S(1)} %get-tuple-element.23.refs_1_, bf16[3,512,128]{2,1,0:T(8,128)(2,1)S(1)} %get-tuple-element.42.refs_1_.refs_2_, ...), custom_call_target="tpu_custom_call" | custom-call | flops 8000000000 | bytes 1024 | tf_op jit(solution)/shard_map/near_attention/pallas_call | solution.py:97
  45.8 2.9 %collective-permute-done.7.refs_4_.refs_5_ = bf16[2,512,128]{2,1,0:T(8,128)(2,1)S(1)} collective-permute-done((bf16[2,512,128]{2,1,0:T(8,128)(2,1)S(1)}, bf16[2,512,128]{2,1,0:T(8,128)(2,1)S(1)}, u32[]{:S(2)}, u32[]{:S(2)}) %collective-permute-start.7) | collective-permute-done | bytes 262176 | tf_op jit(solution)/shard_map/rest_z/ppermute | solution.py:33
  49.4 3.1 %collective-permute-start.11 = (bf16[2,2,512,128]{3,2,1,0:T(8,128)(2,1)S(1)}, bf16[2,2,512,128]{3,2,1,0:T(8,128)(2,1)S(1)}, u32[]{:S(2)}, u32[]{:S(2)}) collective-permute-start(bf16[2,2,512,128]{3,2,1,0:T(8,128)(2,1)S(1)} %rest_pick.1.refs_7_), channel_id=1, source_target_pairs={{0,16},{1,17},{2,18},{3,19},{4,20},{5,21},{6,22},{7,23},{16,32},{1... | collective-permute-start | bytes 1572872 | tf_op jit(solution)/shard_map/rest_x/ppermute | solution.py:33
  52.5 4.3 %halo_attention.1 = (bf16[512,128]{1,0:T(8,128)(2,1)S(1)}, bf16[512,128]{1,0:T(8,128)(2,1)S(1)}, bf16[512,128]{1,0:T(8,128)(2,1)S(1)}, bf16[512,128]{1,0:T(8,128)(2,1)S(1)}) custom-call(s32[6]{0:T(128)S(1)} %stack.65.refs_0_, s32[1,32]{1,0:T(1,128)S(1)} %get-tuple-element.23.refs_1_, bf16[2048,128]{1,0:T(8,128)(2,1)S(1)} %get-tuple-element.24.refs_2_, ...), custom_call_target="tpu_custom_call" | custom-call | flops 1000000000 | bytes 1024 | tf_op jit(solution)/shard_map/halo_attention/pallas_call | solution.py:97
  56.8 2.2 %collective-permute-start.8 = (bf16[512,128]{1,0:T(8,128)(2,1)S(1)}, bf16[512,128]{1,0:T(8,128)(2,1)S(1)}, u32[]{:S(2)}, u32[]{:S(2)}) collective-permute-start(bf16[512,128]{1,0:T(8,128)(2,1)S(1)} %get-tuple-element.30), channel_id=1, source_target_pairs={{0,12},{1,13},{2,14},{3,15},{4,0},{5,1},{6,2},{7,3},{8,4},{9,5},{1... | collective-permute-start | bytes 393224 | tf_op jit(solution)/shard_map/attended_z/ppermute | solution.py:33
  59.0 1.5 %collective-permute-start.9 = (bf16[512,128]{1,0:T(8,128)(2,1)S(1)}, bf16[512,128]{1,0:T(8,128)(2,1)S(1)}, u32[]{:S(2)}, u32[]{:S(2)}) collective-permute-start(bf16[512,128]{1,0:T(8,128)(2,1)S(1)} %get-tuple-element.31), channel_id=1, source_target_pairs={{0,8},{1,9},{2,10},{3,11},{4,12},{5,13},{6,14},{7,15},{8,0},{9,1},... | collective-permute-start | bytes 393224 | tf_op jit(solution)/shard_map/attended_z/ppermute | solution.py:33
  60.5 0.8 collective-permute-start.10
  61.3 0.9 weights_core.1
  62.2 4.0 %collective-permute-start.13 = (bf16[640,1280]{1,0:T(8,128)(2,1)S(1)}, bf16[640,1280]{1,0:T(8,128)(2,1)S(1)}, u32[]{:S(2)}, u32[]{:S(2)}) collective-permute-start(bf16[640,1280]{1,0:T(8,128)(2,1)S(1)} %get-tuple-element.34), channel_id=1, source_target_pairs={{0,1},{1,0},{2,3},{3,2},{4,5},{5,4},{6,7},{7,6},{8,9},{9,8},{10,11... | collective-permute-start | bytes 4915208 | tf_op jit(solution)/shard_map/weights_core/ppermute | solution.py:33
  66.3 1.6 %collective-permute-done.11.refs_7_ = bf16[2,2,512,128]{3,2,1,0:T(8,128)(2,1)S(1)} collective-permute-done((bf16[2,2,512,128]{3,2,1,0:T(8,128)(2,1)S(1)}, bf16[2,2,512,128]{3,2,1,0:T(8,128)(2,1)S(1)}, u32[]{:S(2)}, u32[]{:S(2)}) %collective-permute-start.11) | collective-permute-done | bytes 524320 | tf_op jit(solution)/shard_map/rest_x/ppermute | solution.py:33
  67.9 3.4 %rest_attention.1.refs_2_ = bf16[512,128]{1,0:T(8,128)(2,1)S(1)} custom-call(s32[6]{0:T(128)S(1)} %stack.65.refs_0_, s32[1,32]{1,0:T(1,128)S(1)} %get-tuple-element.23.refs_1_, bf16[2,512,128]{2,1,0:T(8,128)(2,1)S(1)} %get-tuple-element.28.refs_1_.refs_2_, bf16[2,512,128]{2,1,0:T(8,128)(2,1)S(1)} %collective-permute-done.5.refs_2_.refs_3_, ...), custom_call_target="tpu_custom_call" | custom-call | flops 3000000000 | bytes 1024 | tf_op jit(solution)/shard_map/rest_attention/pallas_call | solution.py:97
  71.3 1.5 %collective-permute-start.12 = (bf16[5,512,128]{2,1,0:T(8,128)(2,1)S(1)}, bf16[5,512,128]{2,1,0:T(8,128)(2,1)S(1)}, u32[]{:S(2)}, u32[]{:S(2)}) collective-permute-start(bf16[5,512,128]{2,1,0:T(8,128)(2,1)S(1)} %bitcast_dynamic-update-slice_fusion.refs_1_), channel_id=1, source_target_pairs={{0,1},{1,0},{2,3},{3,2},{4,5},{5,4},{6,7},{7,6},{8,9},{9,8},{10,11... | collective-permute-start | bytes 1966088 | tf_op jit(solution)/shard_map/attended_core/ppermute | solution.py:33
  72.8 0.8 weights_far_core.1
  73.6 1.5 %collective-permute-start.17 = (bf16[640,1280]{1,0:T(8,128)(2,1)S(1)}, bf16[640,1280]{1,0:T(8,128)(2,1)S(1)}, u32[]{:S(2)}, u32[]{:S(2)}) collective-permute-start(bf16[640,1280]{1,0:T(8,128)(2,1)S(1)} %get-tuple-element.37), channel_id=1, source_target_pairs={{0,1},{1,0},{2,3},{3,2},{4,5},{5,4},{6,7},{7,6},{8,9},{9,8},{10,11... | collective-permute-start | bytes 4915208 | tf_op jit(solution)/shard_map/weights_far_core/ppermute | solution.py:33
  75.1 3.6 %project.1.refs_5_ = f32[512,1280]{1,0:T(8,128)S(1)} custom-call(s32[6]{0:T(128)S(1)} %stack.65.refs_0_, bf16[5,512,128]{2,1,0:T(8,128)(2,1)S(1)} %bitcast_dynamic-update-slice_fusion.refs_1_, bf16[640,1280]{1,0:T(8,128)(2,1)S(1)} %get-tuple-element.33.refs_2_, bf16[5,512,128]{2,1,0:T(8,128)(2,1)S(1)} %collective-permute-done.12.refs_3_, ...), custom_call_target="tpu_custom_call" | custom-call | flops 10000000000 | bytes 1024 | tf_op jit(solution)/shard_map/project/pallas_call | solution.py:97
  78.7 12.7 %collective-permute-done.14.refs_1_ = bf16[5,512,128]{2,1,0:T(8,128)(2,1)S(1)} collective-permute-done((bf16[5,512,128]{2,1,0:T(8,128)(2,1)S(1)}, bf16[5,512,128]{2,1,0:T(8,128)(2,1)S(1)}, u32[]{:S(2)}, u32[]{:S(2)}) %collective-permute-start.14) | collective-permute-done | bytes 655392 | tf_op jit(solution)/shard_map/attended_y/ppermute | solution.py:33
  91.4 0.9 collective-permute-start.16
  92.3 1.7 %collective-permute-done.16.refs_3_ = bf16[5,512,128]{2,1,0:T(8,128)(2,1)S(1)} collective-permute-done((bf16[5,512,128]{2,1,0:T(8,128)(2,1)S(1)}, bf16[5,512,128]{2,1,0:T(8,128)(2,1)S(1)}, u32[]{:S(2)}, u32[]{:S(2)}) %collective-permute-start.16) | collective-permute-done | bytes 655392 | tf_op jit(solution)/shard_map/far_core/ppermute | solution.py:33
  94.0 4.7 %finish.1 = bf16[512,1280]{1,0:T(8,128)(2,1)} custom-call(s32[6]{0:T(128)S(1)} %stack.65.refs_0_, bf16[5,512,128]{2,1,0:T(8,128)(2,1)S(1)} %collective-permute-done.14.refs_1_, bf16[640,1280]{1,0:T(8,128)(2,1)S(1)} %get-tuple-element.36.refs_2_, bf16[5,512,128]{2,1,0:T(8,128)(2,1)S(1)} %collective-permute-done.16.refs_3_, ...), custom_call_target="tpu_custom_call" | custom-call | flops 1024 | bytes 1024 | tf_op jit(solution)/shard_map/finish/pallas_call | solution.py:97
  (34 shorter events, 3.3 us)
Async XLA Ops:
  3.2 19.9 %collective-permute-start = (bf16[3,512,128]{2,1,0:T(8,128)(2,1)S(1)}, bf16[3,512,128]{2,1,0:T(8,128)(2,1)S(1)}, u32[]{:S(2)}, u32[]{:S(2)}) collective-permute-start(bf16[3,512,128]{2,1,0:T(8,128)(2,1)S(1)} %get-tuple-element.41), channel_id=1, source_target_pairs={{0,12},{1,13},{2,14},{3,15},{4,0},{5,1},{6,2},{7,3},{8,4},{9,5},{1... | collective-permute-start | bytes 1179656 | tf_op jit(solution)/shard_map/head_z/ppermute | solution.py:33
  7.0 16.1 %collective-permute-start.1 = (bf16[3,512,128]{2,1,0:T(8,128)(2,1)S(1)}, bf16[3,512,128]{2,1,0:T(8,128)(2,1)S(1)}, u32[]{:S(2)}, u32[]{:S(2)}) collective-permute-start(bf16[3,512,128]{2,1,0:T(8,128)(2,1)S(1)} %get-tuple-element.40), channel_id=1, source_target_pairs={{0,8},{1,9},{2,10},{3,11},{4,12},{5,13},{6,14},{7,15},{8,0},{9,1},... | collective-permute-start | bytes 1179656 | tf_op jit(solution)/shard_map/head_z/ppermute | solution.py:33
  7.0 20.3 %collective-permute-start.2 = (bf16[3,512,128]{2,1,0:T(8,128)(2,1)S(1)}, bf16[3,512,128]{2,1,0:T(8,128)(2,1)S(1)}, u32[]{:S(2)}, u32[]{:S(2)}) collective-permute-start(bf16[3,512,128]{2,1,0:T(8,128)(2,1)S(1)} %get-tuple-element.39.refs_2_), channel_id=1, source_target_pairs={{0,4},{1,5},{2,6},{3,7},{4,8},{5,9},{6,10},{7,11},{8,12},{9,13},{1... | collective-permute-start | bytes 1179656 | tf_op jit(solution)/shard_map/head_z/ppermute | solution.py:33
  7.8 2.9 %copy-start = (bf16[5,128,5120]{2,1,0:T(8,128)(2,1)S(1)}, bf16[5,128,5120]{2,1,0:T(8,128)(2,1)}, u32[]{:S(2)}) copy-start(bf16[5,128,5120]{2,1,0:T(8,128)(2,1)} %refs_1_.5) | copy-start | bytes 19660804
  11.5 16.4 %copy-start.1 = (s32[128,128]{1,0:T(8,128)S(1)}, s32[128,128]{1,0:T(8,128)}, u32[]{:S(2)}) copy-start(s32[128,128]{1,0:T(8,128)} %refs_1_.3) | copy-start | bytes 196612
  11.5 61.3 %collective-permute-start.15 = (bf16[640,2560]{1,0:T(8,128)(2,1)S(1)}, bf16[640,2560]{1,0:T(8,128)(2,1)S(1)}, u32[]{:S(2)}, u32[]{:S(2)}) collective-permute-start(bf16[640,2560]{1,0:T(8,128)(2,1)S(1)} %weights_y.1), channel_id=1, source_target_pairs={{0,2},{1,67},{2,64},{3,1},{4,6},{5,71},{6,68},{7,5},{8,10},{9,75},... | collective-permute-start | bytes 9830408 | tf_op jit(solution)/shard_map/weights_y/ppermute | solution.py:33
  28.0 33.3 %slice-start = ((s8[6553600]{0:T(1024)(128)(4,1)}), s8[4194304]{0:T(1024)(128)(4,1)S(1)}, s32[]{:S(2)}) async-start(s8[6553600]{0:T(1024)(128)(4,1)} %bitcast.33), calls=%async_computation | async-start | bytes 8388608
  29.2 7.1 %collective-permute-start.5 = (bf16[2,512,128]{2,1,0:T(8,128)(2,1)S(1)}, bf16[2,512,128]{2,1,0:T(8,128)(2,1)S(1)}, u32[]{:S(2)}, u32[]{:S(2)}) collective-permute-start(bf16[2,512,128]{2,1,0:T(8,128)(2,1)S(1)} %get-tuple-element.28.refs_1_.refs_2_), channel_id=1, source_target_pairs={{0,12},{1,13},{2,14},{3,15},{4,0},{5,1},{6,2},{7,3},{8,4},{9,5},{1... | collective-permute-start | bytes 786440 | tf_op jit(solution)/shard_map/rest_z/ppermute | solution.py:33
  30.2 22.3 %collective-permute-start.3 = (bf16[2,2,512,128]{3,2,1,0:T(8,128)(2,1)S(1)}, bf16[2,2,512,128]{3,2,1,0:T(8,128)(2,1)S(1)}, u32[]{:S(2)}, u32[]{:S(2)}) collective-permute-start(bf16[2,2,512,128]{3,2,1,0:T(8,128)(2,1)S(1)} %get-tuple-element.22.refs_3_), channel_id=1, source_target_pairs={{0,16},{1,17},{2,18},{3,19},{4,20},{5,21},{6,22},{7,23},{8,24},{9,... | collective-permute-start | bytes 1572872 | tf_op jit(solution)/shard_map/head_x/ppermute | solution.py:33
  33.3 12.5 %collective-permute-start.6 = (bf16[2,512,128]{2,1,0:T(8,128)(2,1)S(1)}, bf16[2,512,128]{2,1,0:T(8,128)(2,1)S(1)}, u32[]{:S(2)}, u32[]{:S(2)}) collective-permute-start(bf16[2,512,128]{2,1,0:T(8,128)(2,1)S(1)} %get-tuple-element.28.refs_1_.refs_2_), channel_id=1, source_target_pairs={{0,8},{1,9},{2,10},{3,11},{4,12},{5,13},{6,14},{7,15},{8,0},{9,1},... | collective-permute-start | bytes 786440 | tf_op jit(solution)/shard_map/rest_z/ppermute | solution.py:33
  34.1 14.7 %collective-permute-start.7 = (bf16[2,512,128]{2,1,0:T(8,128)(2,1)S(1)}, bf16[2,512,128]{2,1,0:T(8,128)(2,1)S(1)}, u32[]{:S(2)}, u32[]{:S(2)}) collective-permute-start(bf16[2,512,128]{2,1,0:T(8,128)(2,1)S(1)} %get-tuple-element.28.refs_1_.refs_2_), channel_id=1, source_target_pairs={{0,4},{1,5},{2,6},{3,7},{4,8},{5,9},{6,10},{7,11},{8,12},{9,13},{1... | collective-permute-start | bytes 786440 | tf_op jit(solution)/shard_map/rest_z/ppermute | solution.py:33
  36.3 16.2 %collective-permute-start.4 = (bf16[2,2,512,128]{3,2,1,0:T(8,128)(2,1)S(1)}, bf16[2,2,512,128]{3,2,1,0:T(8,128)(2,1)S(1)}, u32[]{:S(2)}, u32[]{:S(2)}) collective-permute-start(bf16[2,2,512,128]{3,2,1,0:T(8,128)(2,1)S(1)} %get-tuple-element.27), channel_id=1, source_target_pairs={{16,0},{17,1},{18,2},{19,3},{20,4},{21,5},{22,6},{23,7},{24,8},{25... | collective-permute-start | bytes 1572872 | tf_op jit(solution)/shard_map/head_x/ppermute | solution.py:33
  40.7 20.5 %slice-start.1 = ((s8[6553600]{0:T(1024)(128)(4,1)}), s8[2359296]{0:T(1024)(128)(4,1)S(1)}, s32[]{:S(2)}) async-start(s8[6553600]{0:T(1024)(128)(4,1)} %bitcast.33), calls=%async_computation.1 | async-start | bytes 4718592
  49.4 18.6 %collective-permute-start.11 = (bf16[2,2,512,128]{3,2,1,0:T(8,128)(2,1)S(1)}, bf16[2,2,512,128]{3,2,1,0:T(8,128)(2,1)S(1)}, u32[]{:S(2)}, u32[]{:S(2)}) collective-permute-start(bf16[2,2,512,128]{3,2,1,0:T(8,128)(2,1)S(1)} %rest_pick.1.refs_7_), channel_id=1, source_target_pairs={{0,16},{1,17},{2,18},{3,19},{4,20},{5,21},{6,22},{7,23},{16,32},{1... | collective-permute-start | bytes 1572872 | tf_op jit(solution)/shard_map/rest_x/ppermute | solution.py:33
  56.8 5.4 %collective-permute-start.8 = (bf16[512,128]{1,0:T(8,128)(2,1)S(1)}, bf16[512,128]{1,0:T(8,128)(2,1)S(1)}, u32[]{:S(2)}, u32[]{:S(2)}) collective-permute-start(bf16[512,128]{1,0:T(8,128)(2,1)S(1)} %get-tuple-element.30), channel_id=1, source_target_pairs={{0,12},{1,13},{2,14},{3,15},{4,0},{5,1},{6,2},{7,3},{8,4},{9,5},{1... | collective-permute-start | bytes 393224 | tf_op jit(solution)/shard_map/attended_z/ppermute | solution.py:33
  59.0 7.2 %collective-permute-start.9 = (bf16[512,128]{1,0:T(8,128)(2,1)S(1)}, bf16[512,128]{1,0:T(8,128)(2,1)S(1)}, u32[]{:S(2)}, u32[]{:S(2)}) collective-permute-start(bf16[512,128]{1,0:T(8,128)(2,1)S(1)} %get-tuple-element.31), channel_id=1, source_target_pairs={{0,8},{1,9},{2,10},{3,11},{4,12},{5,13},{6,14},{7,15},{8,0},{9,1},... | collective-permute-start | bytes 393224 | tf_op jit(solution)/shard_map/attended_z/ppermute | solution.py:33
  60.5 5.8 %collective-permute-start.10 = (bf16[512,128]{1,0:T(8,128)(2,1)S(1)}, bf16[512,128]{1,0:T(8,128)(2,1)S(1)}, u32[]{:S(2)}, u32[]{:S(2)}) collective-permute-start(bf16[512,128]{1,0:T(8,128)(2,1)S(1)} %get-tuple-element.32), channel_id=1, source_target_pairs={{0,4},{1,5},{2,6},{3,7},{4,8},{5,9},{6,10},{7,11},{8,12},{9,13},{1... | collective-permute-start | bytes 393224 | tf_op jit(solution)/shard_map/attended_z/ppermute | solution.py:33
  62.2 12.9 %collective-permute-start.13 = (bf16[640,1280]{1,0:T(8,128)(2,1)S(1)}, bf16[640,1280]{1,0:T(8,128)(2,1)S(1)}, u32[]{:S(2)}, u32[]{:S(2)}) collective-permute-start(bf16[640,1280]{1,0:T(8,128)(2,1)S(1)} %get-tuple-element.34), channel_id=1, source_target_pairs={{0,1},{1,0},{2,3},{3,2},{4,5},{5,4},{6,7},{7,6},{8,9},{9,8},{10,11... | collective-permute-start | bytes 4915208 | tf_op jit(solution)/shard_map/weights_core/ppermute | solution.py:33
  71.3 3.8 %collective-permute-start.12 = (bf16[5,512,128]{2,1,0:T(8,128)(2,1)S(1)}, bf16[5,512,128]{2,1,0:T(8,128)(2,1)S(1)}, u32[]{:S(2)}, u32[]{:S(2)}) collective-permute-start(bf16[5,512,128]{2,1,0:T(8,128)(2,1)S(1)} %bitcast_dynamic-update-slice_fusion.refs_1_), channel_id=1, source_target_pairs={{0,1},{1,0},{2,3},{3,2},{4,5},{5,4},{6,7},{7,6},{8,9},{9,8},{10,11... | collective-permute-start | bytes 1966088 | tf_op jit(solution)/shard_map/attended_core/ppermute | solution.py:33
  73.6 20.4 %collective-permute-start.17 = (bf16[640,1280]{1,0:T(8,128)(2,1)S(1)}, bf16[640,1280]{1,0:T(8,128)(2,1)S(1)}, u32[]{:S(2)}, u32[]{:S(2)}) collective-permute-start(bf16[640,1280]{1,0:T(8,128)(2,1)S(1)} %get-tuple-element.37), channel_id=1, source_target_pairs={{0,1},{1,0},{2,3},{3,2},{4,5},{5,4},{6,7},{7,6},{8,9},{9,8},{10,11... | collective-permute-start | bytes 4915208 | tf_op jit(solution)/shard_map/weights_far_core/ppermute | solution.py:33
  75.1 16.3 %collective-permute-start.14 = (bf16[5,512,128]{2,1,0:T(8,128)(2,1)S(1)}, bf16[5,512,128]{2,1,0:T(8,128)(2,1)S(1)}, u32[]{:S(2)}, u32[]{:S(2)}) collective-permute-start(bf16[5,512,128]{2,1,0:T(8,128)(2,1)S(1)} %bitcast_dynamic-update-slice_fusion.refs_1_), channel_id=1, source_target_pairs={{0,2},{1,3},{2,0},{3,1},{4,6},{5,7},{6,4},{7,5},{8,10},{9,11},{10,... | collective-permute-start | bytes 1966088 | tf_op jit(solution)/shard_map/attended_y/ppermute | solution.py:33
  91.4 2.6 %collective-permute-start.16 = (bf16[5,512,128]{2,1,0:T(8,128)(2,1)S(1)}, bf16[5,512,128]{2,1,0:T(8,128)(2,1)S(1)}, u32[]{:S(2)}, u32[]{:S(2)}) collective-permute-start(bf16[5,512,128]{2,1,0:T(8,128)(2,1)S(1)} %collective-permute-done.14.refs_1_), channel_id=1, source_target_pairs={{0,1},{1,0},{2,3},{3,2},{4,5},{5,4},{6,7},{7,6},{8,9},{9,8},{10,11... | collective-permute-start | bytes 1966088 | tf_op jit(solution)/shard_map/far_core/ppermute | solution.py:33

commit v4 on v3

--- a/solution.py
+++ b/solution.py
@@ -87,7 +87,7 @@
 SCALARS = pl.BlockSpec(memory_space=pltpu.SMEM)
 
 
-def call(kernel, outs, scratch, operands, scalars, flops=1024, later=(), far=0):
+def call(kernel, outs, scratch, operands, scalars, flops=1024, later=(), far=0, out_spec=ANYWHERE):
     held = len(operands) - scalars - far
 
     def body(*refs):
@@ -98,7 +98,7 @@
         body,
         out_shape=outs,
         in_specs=[SCALARS] * scalars + [ANYWHERE] * held + [pl.BlockSpec(memory_space=pl.ANY)] * (far + len(later)),
-        out_specs=jax.tree.map(lambda _: ANYWHERE, outs),
+        out_specs=jax.tree.map(lambda _: out_spec, outs),
         scratch_shapes=scratch,
         compiler_params=pltpu.CompilerParams(vmem_limit_bytes=VMEM_LIMIT),
         cost_estimate=pl.CostEstimate(flops=flops, bytes_accessed=1024, transcendentals=0),
@@ -270,31 +270,36 @@
     wide[:, base + ROW * TILE : base + (ROW + 1) * TILE] = ring[ROW]
 
 
+STRIP = 256
+
+
+def strips(width):
+    return [slice(n, n + STRIP) for n in range(0, width, STRIP)]
+
+
 def project_kernel(where_ref, m0, w0, m1, w1, out, wide):
     z = where_ref[0]
     place_heads(z, m0, wide, 0)
     place_heads(z, m1, wide, 640)
-
-    @pl.loop(0, out.shape[1] // 256)
-    def _(n):
-        at = pl.ds(pl.multiple_of(n * 256, 256), 256)
+    for at in strips(out.shape[1]):
         out[:, at] = jnp.dot(wide[:, :640], w0[:, at], preferred_element_type=jnp.float32) + jnp.dot(
             wide[:, 640:], w1[:, at], preferred_element_type=jnp.float32
         )
 
 
-def finish_kernel(where_ref, m0, w0, m1, w1, before, out, wide):
+def finish_kernel(where_ref, m0, w0, m1, w1, before, out, wide, rounded, sem):
     z = where_ref[0]
     place_heads(z, m0, wide, 0)
     place_heads(z, m1, wide, 640)
-
-    @pl.loop(0, out.shape[1] // 256)
-    def _(n):
-        at = pl.ds(pl.multiple_of(n * 256, 256), 256)
-        part = jnp.dot(wide[:, :640], w0[:, at], preferred_element_type=jnp.float32) + jnp.dot(
-            wide[:, 640:], w1[:, at], preferred_element_type=jnp.float32
-        )
-        out[:, at] = (part + before[:, at]).astype(out.dtype)
+    copies = []
+    for n, at in enumerate(strips(out.shape[1])):
+        part = before[:, at] + jnp.dot(wide[:, :640], w0[:, at], preferred_element_type=jnp.float32)
+        part = part + jnp.dot(wide[:, 640:], w1[:, at], preferred_element_type=jnp.float32)
+        rounded[:, at] = part.astype(rounded.dtype)
+        copies.append(pltpu.make_async_copy(rounded.at[:, at], out.at[:, at], sem.at[n]))
+        copies[-1].start()
+    for copy in copies:
+        copy.wait()
 
 
 def fetch(copies):
@@ -487,9 +492,10 @@
         return call(
             finish_kernel,
             jax.ShapeDtypeStruct((tok, cols), bf),
-            [wide],
+            [wide, pltpu.VMEM((tok, cols), bf), pltpu.SemaphoreType.DMA((cols // STRIP,))],
             [where, far, w_y, far_sib, w_y_sib, near],
             1,
+            out_spec=pl.BlockSpec(memory_space=pl.ANY),
         )
 
 

time: 100 us -> 99.3 us (level)
  Pallas kernels: 26.1 us -> 24.8 us
    pallas_call x11, Pallas kernels: 26.1 us -> 24.8 us  [call(): pl.pallas_call(body, out_shape=outs, in_specs=[SCALARS] * scalars + [ANYW...]
where the time goes in v4:
time: 99.3 us; the launch traced here: 97.8 us
  waiting for transfers between devices  35.5 us (36%)
  starting transfers between devices  29.1 us (29%)
  Pallas kernels  24.8 us (25%)
  local copies, waits for them, and re-layouts  5.04 us (5%)
  other arithmetic  3.04 us (3%)
    ppermute x18, waiting for transfers between devices, send(): return lax.ppermute(block, AXES, route(rows, target))  35.5 us
    ppermute x18, starting transfers between devices, send(): return lax.ppermute(block, AXES, route(rows, target))  29.1 us
    pallas_call x11, Pallas kernels, call(): pl.pallas_call(body, out_shape=outs, in_specs=[SCALARS] * scalars + [ANYW...  24.8 us
    another operation x1, other arithmetic, local(): kvq = jnp.stack([key_rows, value_rows, queries]).transpose(2, 0, 1, 3)  3.04 us
    unnamed x12, local copies, waits for them, and re-layouts  2.95 us
  transfers between devices with their start and end apart: 18, of which 7 were waited for; matrix products, arithmetic and copies ran while one was open for 2% of the time, Pallas kernels for 22%

profile of v4, /device:TPU:17, one launch (start us, length us, event | category | flops | bytes accessed | tf_op | source)
XLA Modules:
  0.0 97.8 jit_solution(7882398379169461767)
XLA Ops:
  0.0 3.0 %pad_maximum_fusion = (bf16[3,512,5,128]{3,1,0,2:T(8,128)(2,1)S(1)}, bf16[5,3,512,128]{3,2,1,0:T(8,128)(2,1)}) fusion(bf16[1,512,5,128]{3,1,0,2:T(8,128)(2,1)} %bitcast.35, bf16[1,512,5,128]{3,1,0,2:T(8,128)(2,1)} %bitcast.36, bf16[1,512,5,128]{3,1,0,2:T(8,128)(2,1)} %bitcast.37), kind=kLoop, calls=%fused_computation | loop fusion | flops 1966080 | bytes 5898240 | tf_op jit(solution)/shard_map/lay_out/stack | solution.py:362
  3.2 3.8 %collective-permute-start = (bf16[3,512,128]{2,1,0:T(8,128)(2,1)S(1)}, bf16[3,512,128]{2,1,0:T(8,128)(2,1)S(1)}, u32[]{:S(2)}, u32[]{:S(2)}) collective-permute-start(bf16[3,512,128]{2,1,0:T(8,128)(2,1)S(1)} %get-tuple-element.41), channel_id=1, source_target_pairs={{0,12},{1,13},{2,14},{3,15},{4,0},{5,1},{6,2},{7,3},{8,4},{9,5},{1... | collective-permute-start | bytes 1179656 | tf_op jit(solution)/shard_map/head_z/ppermute | solution.py:33
  7.8 2.9 %copy-done = bf16[5,128,5120]{2,1,0:T(8,128)(2,1)S(1)} copy-done((bf16[5,128,5120]{2,1,0:T(8,128)(2,1)S(1)}, bf16[5,128,5120]{2,1,0:T(8,128)(2,1)}, u32[]{:S(2)}) %copy-start) | copy-done | bytes 6553624
  10.6 0.9 weights_y.1
  11.8 1.0 slice_bitcast_fusion.refs_2_
  12.7 10.3 %collective-permute-done.refs_2_.refs_3_ = bf16[3,512,128]{2,1,0:T(8,128)(2,1)S(1)} collective-permute-done((bf16[3,512,128]{2,1,0:T(8,128)(2,1)S(1)}, bf16[3,512,128]{2,1,0:T(8,128)(2,1)S(1)}, u32[]{:S(2)}, u32[]{:S(2)}) %collective-permute-start) | collective-permute-done | bytes 393248 | tf_op jit(solution)/shard_map/head_z/ppermute | solution.py:33
  23.0 4.3 %collective-permute-done.2.refs_4_.refs_5_ = bf16[3,512,128]{2,1,0:T(8,128)(2,1)S(1)} collective-permute-done((bf16[3,512,128]{2,1,0:T(8,128)(2,1)S(1)}, bf16[3,512,128]{2,1,0:T(8,128)(2,1)S(1)}, u32[]{:S(2)}, u32[]{:S(2)}) %collective-permute-start.2) | collective-permute-done | bytes 393248 | tf_op jit(solution)/shard_map/head_z/ppermute | solution.py:33
  28.0 1.2 %places.1 = (s32[1,32]{1,0:T(1,128)S(1)}, bf16[2,512,128]{2,1,0:T(8,128)(2,1)S(1)}) custom-call(s32[6]{0:T(128)S(1)} %stack.65.refs_0_, s32[128,128]{1,0:T(8,128)S(1)} %copy-done.1, bf16[2,512,128]{2,1,0:T(8,128)(2,1)S(1)} %slice_bitcast_fusion.refs_2_, bf16[2,2,512,128]{3,2,1,0:T(8,128)(2,1)S(1)} %get-tuple-element.22.refs_3_), custom_call_target="tpu_custom_call" | custom-call | flops 8000000000 | bytes 1024 | tf_op jit(solution)/shard_map/places/pallas_call | solution.py:97
  29.3 0.9 slice_bitcast_fusion.1.refs_6_
  30.2 3.1 %collective-permute-start.3 = (bf16[2,2,512,128]{3,2,1,0:T(8,128)(2,1)S(1)}, bf16[2,2,512,128]{3,2,1,0:T(8,128)(2,1)S(1)}, u32[]{:S(2)}, u32[]{:S(2)}) collective-permute-start(bf16[2,2,512,128]{3,2,1,0:T(8,128)(2,1)S(1)} %get-tuple-element.22.refs_3_), channel_id=1, source_target_pairs={{0,16},{1,17},{2,18},{3,19},{4,20},{5,21},{6,22},{7,23},{8,24},{9,... | collective-permute-start | bytes 1572872 | tf_op jit(solution)/shard_map/head_x/ppermute | solution.py:33
  34.1 0.9 collective-permute-start.7
  34.9 1.3 %collective-permute-done.5.refs_2_.refs_3_ = bf16[2,512,128]{2,1,0:T(8,128)(2,1)S(1)} collective-permute-done((bf16[2,512,128]{2,1,0:T(8,128)(2,1)S(1)}, bf16[2,512,128]{2,1,0:T(8,128)(2,1)S(1)}, u32[]{:S(2)}, u32[]{:S(2)}) %collective-permute-start.5) | collective-permute-done | bytes 262176 | tf_op jit(solution)/shard_map/rest_z/ppermute | solution.py:33
  36.3 4.5 %collective-permute-start.4 = (bf16[2,2,512,128]{3,2,1,0:T(8,128)(2,1)S(1)}, bf16[2,2,512,128]{3,2,1,0:T(8,128)(2,1)S(1)}, u32[]{:S(2)}, u32[]{:S(2)}) collective-permute-start(bf16[2,2,512,128]{3,2,1,0:T(8,128)(2,1)S(1)} %get-tuple-element.27), channel_id=1, source_target_pairs={{16,0},{17,1},{18,2},{19,3},{20,4},{21,5},{22,6},{23,7},{24,8},{25... | collective-permute-start | bytes 1572872 | tf_op jit(solution)/shard_map/head_x/ppermute | solution.py:33
  40.7 5.1 %near_attention.1 = (bf16[2048,128]{1,0:T(8,128)(2,1)S(1)}, f32[2048,128]{1,0:T(8,128)S(1)}, f32[2048,128]{1,0:T(8,128)S(1)}) custom-call(s32[6]{0:T(128)S(1)} %stack.65.refs_0_, s32[1,32]{1,0:T(1,128)S(1)} %get-tuple-element.23.refs_1_, bf16[3,512,128]{2,1,0:T(8,128)(2,1)S(1)} %get-tuple-element.42.refs_1_.refs_2_, ...), custom_call_target="tpu_custom_call" | custom-call | flops 8000000000 | bytes 1024 | tf_op jit(solution)/shard_map/near_attention/pallas_call | solution.py:97
  45.8 2.9 %collective-permute-done.7.refs_4_.refs_5_ = bf16[2,512,128]{2,1,0:T(8,128)(2,1)S(1)} collective-permute-done((bf16[2,512,128]{2,1,0:T(8,128)(2,1)S(1)}, bf16[2,512,128]{2,1,0:T(8,128)(2,1)S(1)}, u32[]{:S(2)}, u32[]{:S(2)}) %collective-permute-start.7) | collective-permute-done | bytes 262176 | tf_op jit(solution)/shard_map/rest_z/ppermute | solution.py:33
  49.4 3.1 %collective-permute-start.11 = (bf16[2,2,512,128]{3,2,1,0:T(8,128)(2,1)S(1)}, bf16[2,2,512,128]{3,2,1,0:T(8,128)(2,1)S(1)}, u32[]{:S(2)}, u32[]{:S(2)}) collective-permute-start(bf16[2,2,512,128]{3,2,1,0:T(8,128)(2,1)S(1)} %rest_pick.1.refs_7_), channel_id=1, source_target_pairs={{0,16},{1,17},{2,18},{3,19},{4,20},{5,21},{6,22},{7,23},{16,32},{1... | collective-permute-start | bytes 1572872 | tf_op jit(solution)/shard_map/rest_x/ppermute | solution.py:33
  52.5 4.3 %halo_attention.1 = (bf16[512,128]{1,0:T(8,128)(2,1)S(1)}, bf16[512,128]{1,0:T(8,128)(2,1)S(1)}, bf16[512,128]{1,0:T(8,128)(2,1)S(1)}, bf16[512,128]{1,0:T(8,128)(2,1)S(1)}) custom-call(s32[6]{0:T(128)S(1)} %stack.65.refs_0_, s32[1,32]{1,0:T(1,128)S(1)} %get-tuple-element.23.refs_1_, bf16[2048,128]{1,0:T(8,128)(2,1)S(1)} %get-tuple-element.24.refs_2_, ...), custom_call_target="tpu_custom_call" | custom-call | flops 1000000000 | bytes 1024 | tf_op jit(solution)/shard_map/halo_attention/pallas_call | solution.py:97
  56.8 2.2 %collective-permute-start.8 = (bf16[512,128]{1,0:T(8,128)(2,1)S(1)}, bf16[512,128]{1,0:T(8,128)(2,1)S(1)}, u32[]{:S(2)}, u32[]{:S(2)}) collective-permute-start(bf16[512,128]{1,0:T(8,128)(2,1)S(1)} %get-tuple-element.30), channel_id=1, source_target_pairs={{0,12},{1,13},{2,14},{3,15},{4,0},{5,1},{6,2},{7,3},{8,4},{9,5},{1... | collective-permute-start | bytes 393224 | tf_op jit(solution)/shard_map/attended_z/ppermute | solution.py:33
  59.0 1.5 %collective-permute-start.9 = (bf16[512,128]{1,0:T(8,128)(2,1)S(1)}, bf16[512,128]{1,0:T(8,128)(2,1)S(1)}, u32[]{:S(2)}, u32[]{:S(2)}) collective-permute-start(bf16[512,128]{1,0:T(8,128)(2,1)S(1)} %get-tuple-element.31), channel_id=1, source_target_pairs={{0,8},{1,9},{2,10},{3,11},{4,12},{5,13},{6,14},{7,15},{8,0},{9,1},... | collective-permute-start | bytes 393224 | tf_op jit(solution)/shard_map/attended_z/ppermute | solution.py:33
  60.5 0.8 collective-permute-start.10
  61.3 0.9 weights_core.1
  62.2 4.0 %collective-permute-start.13 = (bf16[640,1280]{1,0:T(8,128)(2,1)S(1)}, bf16[640,1280]{1,0:T(8,128)(2,1)S(1)}, u32[]{:S(2)}, u32[]{:S(2)}) collective-permute-start(bf16[640,1280]{1,0:T(8,128)(2,1)S(1)} %get-tuple-element.34), channel_id=1, source_target_pairs={{0,1},{1,0},{2,3},{3,2},{4,5},{5,4},{6,7},{7,6},{8,9},{9,8},{10,11... | collective-permute-start | bytes 4915208 | tf_op jit(solution)/shard_map/weights_core/ppermute | solution.py:33
  66.3 1.6 %collective-permute-done.11.refs_7_ = bf16[2,2,512,128]{3,2,1,0:T(8,128)(2,1)S(1)} collective-permute-done((bf16[2,2,512,128]{3,2,1,0:T(8,128)(2,1)S(1)}, bf16[2,2,512,128]{3,2,1,0:T(8,128)(2,1)S(1)}, u32[]{:S(2)}, u32[]{:S(2)}) %collective-permute-start.11) | collective-permute-done | bytes 524320 | tf_op jit(solution)/shard_map/rest_x/ppermute | solution.py:33
  67.9 3.8 %rest_attention.1.refs_2_ = bf16[512,128]{1,0:T(8,128)(2,1)S(1)} custom-call(s32[6]{0:T(128)S(1)} %stack.65.refs_0_, s32[1,32]{1,0:T(1,128)S(1)} %get-tuple-element.23.refs_1_, bf16[2,512,128]{2,1,0:T(8,128)(2,1)S(1)} %get-tuple-element.28.refs_1_.refs_2_, bf16[2,512,128]{2,1,0:T(8,128)(2,1)S(1)} %collective-permute-done.5.refs_2_.refs_3_, ...), custom_call_target="tpu_custom_call" | custom-call | flops 3000000000 | bytes 1024 | tf_op jit(solution)/shard_map/rest_attention/pallas_call | solution.py:97
  71.7 1.5 %collective-permute-start.12 = (bf16[5,512,128]{2,1,0:T(8,128)(2,1)S(1)}, bf16[5,512,128]{2,1,0:T(8,128)(2,1)S(1)}, u32[]{:S(2)}, u32[]{:S(2)}) collective-permute-start(bf16[5,512,128]{2,1,0:T(8,128)(2,1)S(1)} %bitcast_dynamic-update-slice_fusion.refs_1_), channel_id=1, source_target_pairs={{0,1},{1,0},{2,3},{3,2},{4,5},{5,4},{6,7},{7,6},{8,9},{9,8},{10,11... | collective-permute-start | bytes 1966088 | tf_op jit(solution)/shard_map/attended_core/ppermute | solution.py:33
  73.2 0.8 weights_far_core.1
  74.0 1.1 %collective-permute-start.17 = (bf16[640,1280]{1,0:T(8,128)(2,1)S(1)}, bf16[640,1280]{1,0:T(8,128)(2,1)S(1)}, u32[]{:S(2)}, u32[]{:S(2)}) collective-permute-start(bf16[640,1280]{1,0:T(8,128)(2,1)S(1)} %get-tuple-element.37), channel_id=1, source_target_pairs={{0,1},{1,0},{2,3},{3,2},{4,5},{5,4},{6,7},{7,6},{8,9},{9,8},{10,11... | collective-permute-start | bytes 4915208 | tf_op jit(solution)/shard_map/weights_far_core/ppermute | solution.py:33
  75.2 2.9 %project.1.refs_5_ = f32[512,1280]{1,0:T(8,128)S(1)} custom-call(s32[6]{0:T(128)S(1)} %stack.65.refs_0_, bf16[5,512,128]{2,1,0:T(8,128)(2,1)S(1)} %bitcast_dynamic-update-slice_fusion.refs_1_, bf16[640,1280]{1,0:T(8,128)(2,1)S(1)} %get-tuple-element.33.refs_2_, bf16[5,512,128]{2,1,0:T(8,128)(2,1)S(1)} %collective-permute-done.12.refs_3_, ...), custom_call_target="tpu_custom_call" | custom-call | flops 10000000000 | bytes 1024 | tf_op jit(solution)/shard_map/project/pallas_call | solution.py:97
  78.1 13.3 %collective-permute-done.14.refs_1_ = bf16[5,512,128]{2,1,0:T(8,128)(2,1)S(1)} collective-permute-done((bf16[5,512,128]{2,1,0:T(8,128)(2,1)S(1)}, bf16[5,512,128]{2,1,0:T(8,128)(2,1)S(1)}, u32[]{:S(2)}, u32[]{:S(2)}) %collective-permute-start.14) | collective-permute-done | bytes 655392 | tf_op jit(solution)/shard_map/attended_y/ppermute | solution.py:33
  91.4 0.9 collective-permute-start.16
  92.3 1.7 %collective-permute-done.16.refs_3_ = bf16[5,512,128]{2,1,0:T(8,128)(2,1)S(1)} collective-permute-done((bf16[5,512,128]{2,1,0:T(8,128)(2,1)S(1)}, bf16[5,512,128]{2,1,0:T(8,128)(2,1)S(1)}, u32[]{:S(2)}, u32[]{:S(2)}) %collective-permute-start.16) | collective-permute-done | bytes 655392 | tf_op jit(solution)/shard_map/far_core/ppermute | solution.py:33
  94.0 3.7 %finish.1 = bf16[512,1280]{1,0:T(8,128)(2,1)} custom-call(s32[6]{0:T(128)S(1)} %stack.65.refs_0_, bf16[5,512,128]{2,1,0:T(8,128)(2,1)S(1)} %collective-permute-done.14.refs_1_, bf16[640,1280]{1,0:T(8,128)(2,1)S(1)} %get-tuple-element.36.refs_2_, bf16[5,512,128]{2,1,0:T(8,128)(2,1)S(1)} %collective-permute-done.16.refs_3_, ...), custom_call_target="tpu_custom_call" | custom-call | flops 1024 | bytes 1024 | tf_op jit(solution)/shard_map/finish/pallas_call | solution.py:97
  (34 shorter events, 3.4 us)
Async XLA Ops:
  3.2 19.9 %collective-permute-start = (bf16[3,512,128]{2,1,0:T(8,128)(2,1)S(1)}, bf16[3,512,128]{2,1,0:T(8,128)(2,1)S(1)}, u32[]{:S(2)}, u32[]{:S(2)}) collective-permute-start(bf16[3,512,128]{2,1,0:T(8,128)(2,1)S(1)} %get-tuple-element.41), channel_id=1, source_target_pairs={{0,12},{1,13},{2,14},{3,15},{4,0},{5,1},{6,2},{7,3},{8,4},{9,5},{1... | collective-permute-start | bytes 1179656 | tf_op jit(solution)/shard_map/head_z/ppermute | solution.py:33
  7.0 16.1 %collective-permute-start.1 = (bf16[3,512,128]{2,1,0:T(8,128)(2,1)S(1)}, bf16[3,512,128]{2,1,0:T(8,128)(2,1)S(1)}, u32[]{:S(2)}, u32[]{:S(2)}) collective-permute-start(bf16[3,512,128]{2,1,0:T(8,128)(2,1)S(1)} %get-tuple-element.40), channel_id=1, source_target_pairs={{0,8},{1,9},{2,10},{3,11},{4,12},{5,13},{6,14},{7,15},{8,0},{9,1},... | collective-permute-start | bytes 1179656 | tf_op jit(solution)/shard_map/head_z/ppermute | solution.py:33
  7.0 20.3 %collective-permute-start.2 = (bf16[3,512,128]{2,1,0:T(8,128)(2,1)S(1)}, bf16[3,512,128]{2,1,0:T(8,128)(2,1)S(1)}, u32[]{:S(2)}, u32[]{:S(2)}) collective-permute-start(bf16[3,512,128]{2,1,0:T(8,128)(2,1)S(1)} %get-tuple-element.39.refs_2_), channel_id=1, source_target_pairs={{0,4},{1,5},{2,6},{3,7},{4,8},{5,9},{6,10},{7,11},{8,12},{9,13},{1... | collective-permute-start | bytes 1179656 | tf_op jit(solution)/shard_map/head_z/ppermute | solution.py:33
  7.8 2.9 %copy-start = (bf16[5,128,5120]{2,1,0:T(8,128)(2,1)S(1)}, bf16[5,128,5120]{2,1,0:T(8,128)(2,1)}, u32[]{:S(2)}) copy-start(bf16[5,128,5120]{2,1,0:T(8,128)(2,1)} %refs_1_.5) | copy-start | bytes 19660804
  11.5 16.4 %copy-start.1 = (s32[128,128]{1,0:T(8,128)S(1)}, s32[128,128]{1,0:T(8,128)}, u32[]{:S(2)}) copy-start(s32[128,128]{1,0:T(8,128)} %refs_1_.3) | copy-start | bytes 196612
  11.5 61.7 %collective-permute-start.15 = (bf16[640,2560]{1,0:T(8,128)(2,1)S(1)}, bf16[640,2560]{1,0:T(8,128)(2,1)S(1)}, u32[]{:S(2)}, u32[]{:S(2)}) collective-permute-start(bf16[640,2560]{1,0:T(8,128)(2,1)S(1)} %weights_y.1), channel_id=1, source_target_pairs={{0,2},{1,67},{2,64},{3,1},{4,6},{5,71},{6,68},{7,5},{8,10},{9,75},... | collective-permute-start | bytes 9830408 | tf_op jit(solution)/shard_map/weights_y/ppermute | solution.py:33
  28.0 33.3 %slice-start = ((s8[6553600]{0:T(1024)(128)(4,1)}), s8[4194304]{0:T(1024)(128)(4,1)S(1)}, s32[]{:S(2)}) async-start(s8[6553600]{0:T(1024)(128)(4,1)} %bitcast.33), calls=%async_computation | async-start | bytes 8388608
  29.2 7.1 %collective-permute-start.5 = (bf16[2,512,128]{2,1,0:T(8,128)(2,1)S(1)}, bf16[2,512,128]{2,1,0:T(8,128)(2,1)S(1)}, u32[]{:S(2)}, u32[]{:S(2)}) collective-permute-start(bf16[2,512,128]{2,1,0:T(8,128)(2,1)S(1)} %get-tuple-element.28.refs_1_.refs_2_), channel_id=1, source_target_pairs={{0,12},{1,13},{2,14},{3,15},{4,0},{5,1},{6,2},{7,3},{8,4},{9,5},{1... | collective-permute-start | bytes 786440 | tf_op jit(solution)/shard_map/rest_z/ppermute | solution.py:33
  30.2 22.3 %collective-permute-start.3 = (bf16[2,2,512,128]{3,2,1,0:T(8,128)(2,1)S(1)}, bf16[2,2,512,128]{3,2,1,0:T(8,128)(2,1)S(1)}, u32[]{:S(2)}, u32[]{:S(2)}) collective-permute-start(bf16[2,2,512,128]{3,2,1,0:T(8,128)(2,1)S(1)} %get-tuple-element.22.refs_3_), channel_id=1, source_target_pairs={{0,16},{1,17},{2,18},{3,19},{4,20},{5,21},{6,22},{7,23},{8,24},{9,... | collective-permute-start | bytes 1572872 | tf_op jit(solution)/shard_map/head_x/ppermute | solution.py:33
  33.3 12.5 %collective-permute-start.6 = (bf16[2,512,128]{2,1,0:T(8,128)(2,1)S(1)}, bf16[2,512,128]{2,1,0:T(8,128)(2,1)S(1)}, u32[]{:S(2)}, u32[]{:S(2)}) collective-permute-start(bf16[2,512,128]{2,1,0:T(8,128)(2,1)S(1)} %get-tuple-element.28.refs_1_.refs_2_), channel_id=1, source_target_pairs={{0,8},{1,9},{2,10},{3,11},{4,12},{5,13},{6,14},{7,15},{8,0},{9,1},... | collective-permute-start | bytes 786440 | tf_op jit(solution)/shard_map/rest_z/ppermute | solution.py:33
  34.1 14.7 %collective-permute-start.7 = (bf16[2,512,128]{2,1,0:T(8,128)(2,1)S(1)}, bf16[2,512,128]{2,1,0:T(8,128)(2,1)S(1)}, u32[]{:S(2)}, u32[]{:S(2)}) collective-permute-start(bf16[2,512,128]{2,1,0:T(8,128)(2,1)S(1)} %get-tuple-element.28.refs_1_.refs_2_), channel_id=1, source_target_pairs={{0,4},{1,5},{2,6},{3,7},{4,8},{5,9},{6,10},{7,11},{8,12},{9,13},{1... | collective-permute-start | bytes 786440 | tf_op jit(solution)/shard_map/rest_z/ppermute | solution.py:33
  36.3 16.2 %collective-permute-start.4 = (bf16[2,2,512,128]{3,2,1,0:T(8,128)(2,1)S(1)}, bf16[2,2,512,128]{3,2,1,0:T(8,128)(2,1)S(1)}, u32[]{:S(2)}, u32[]{:S(2)}) collective-permute-start(bf16[2,2,512,128]{3,2,1,0:T(8,128)(2,1)S(1)} %get-tuple-element.27), channel_id=1, source_target_pairs={{16,0},{17,1},{18,2},{19,3},{20,4},{21,5},{22,6},{23,7},{24,8},{25... | collective-permute-start | bytes 1572872 | tf_op jit(solution)/shard_map/head_x/ppermute | solution.py:33
  40.7 20.5 %slice-start.1 = ((s8[6553600]{0:T(1024)(128)(4,1)}), s8[2359296]{0:T(1024)(128)(4,1)S(1)}, s32[]{:S(2)}) async-start(s8[6553600]{0:T(1024)(128)(4,1)} %bitcast.33), calls=%async_computation.1 | async-start | bytes 4718592
  49.4 18.6 %collective-permute-start.11 = (bf16[2,2,512,128]{3,2,1,0:T(8,128)(2,1)S(1)}, bf16[2,2,512,128]{3,2,1,0:T(8,128)(2,1)S(1)}, u32[]{:S(2)}, u32[]{:S(2)}) collective-permute-start(bf16[2,2,512,128]{3,2,1,0:T(8,128)(2,1)S(1)} %rest_pick.1.refs_7_), channel_id=1, source_target_pairs={{0,16},{1,17},{2,18},{3,19},{4,20},{5,21},{6,22},{7,23},{16,32},{1... | collective-permute-start | bytes 1572872 | tf_op jit(solution)/shard_map/rest_x/ppermute | solution.py:33
  56.8 5.4 %collective-permute-start.8 = (bf16[512,128]{1,0:T(8,128)(2,1)S(1)}, bf16[512,128]{1,0:T(8,128)(2,1)S(1)}, u32[]{:S(2)}, u32[]{:S(2)}) collective-permute-start(bf16[512,128]{1,0:T(8,128)(2,1)S(1)} %get-tuple-element.30), channel_id=1, source_target_pairs={{0,12},{1,13},{2,14},{3,15},{4,0},{5,1},{6,2},{7,3},{8,4},{9,5},{1... | collective-permute-start | bytes 393224 | tf_op jit(solution)/shard_map/attended_z/ppermute | solution.py:33
  59.0 7.2 %collective-permute-start.9 = (bf16[512,128]{1,0:T(8,128)(2,1)S(1)}, bf16[512,128]{1,0:T(8,128)(2,1)S(1)}, u32[]{:S(2)}, u32[]{:S(2)}) collective-permute-start(bf16[512,128]{1,0:T(8,128)(2,1)S(1)} %get-tuple-element.31), channel_id=1, source_target_pairs={{0,8},{1,9},{2,10},{3,11},{4,12},{5,13},{6,14},{7,15},{8,0},{9,1},... | collective-permute-start | bytes 393224 | tf_op jit(solution)/shard_map/attended_z/ppermute | solution.py:33
  60.5 5.8 %collective-permute-start.10 = (bf16[512,128]{1,0:T(8,128)(2,1)S(1)}, bf16[512,128]{1,0:T(8,128)(2,1)S(1)}, u32[]{:S(2)}, u32[]{:S(2)}) collective-permute-start(bf16[512,128]{1,0:T(8,128)(2,1)S(1)} %get-tuple-element.32), channel_id=1, source_target_pairs={{0,4},{1,5},{2,6},{3,7},{4,8},{5,9},{6,10},{7,11},{8,12},{9,13},{1... | collective-permute-start | bytes 393224 | tf_op jit(solution)/shard_map/attended_z/ppermute | solution.py:33
  62.2 13.0 %collective-permute-start.13 = (bf16[640,1280]{1,0:T(8,128)(2,1)S(1)}, bf16[640,1280]{1,0:T(8,128)(2,1)S(1)}, u32[]{:S(2)}, u32[]{:S(2)}) collective-permute-start(bf16[640,1280]{1,0:T(8,128)(2,1)S(1)} %get-tuple-element.34), channel_id=1, source_target_pairs={{0,1},{1,0},{2,3},{3,2},{4,5},{5,4},{6,7},{7,6},{8,9},{9,8},{10,11... | collective-permute-start | bytes 4915208 | tf_op jit(solution)/shard_map/weights_core/ppermute | solution.py:33
  71.7 3.5 %collective-permute-start.12 = (bf16[5,512,128]{2,1,0:T(8,128)(2,1)S(1)}, bf16[5,512,128]{2,1,0:T(8,128)(2,1)S(1)}, u32[]{:S(2)}, u32[]{:S(2)}) collective-permute-start(bf16[5,512,128]{2,1,0:T(8,128)(2,1)S(1)} %bitcast_dynamic-update-slice_fusion.refs_1_), channel_id=1, source_target_pairs={{0,1},{1,0},{2,3},{3,2},{4,5},{5,4},{6,7},{7,6},{8,9},{9,8},{10,11... | collective-permute-start | bytes 1966088 | tf_op jit(solution)/shard_map/attended_core/ppermute | solution.py:33
  74.0 20.0 %collective-permute-start.17 = (bf16[640,1280]{1,0:T(8,128)(2,1)S(1)}, bf16[640,1280]{1,0:T(8,128)(2,1)S(1)}, u32[]{:S(2)}, u32[]{:S(2)}) collective-permute-start(bf16[640,1280]{1,0:T(8,128)(2,1)S(1)} %get-tuple-element.37), channel_id=1, source_target_pairs={{0,1},{1,0},{2,3},{3,2},{4,5},{5,4},{6,7},{7,6},{8,9},{9,8},{10,11... | collective-permute-start | bytes 4915208 | tf_op jit(solution)/shard_map/weights_far_core/ppermute | solution.py:33
  75.1 16.3 %collective-permute-start.14 = (bf16[5,512,128]{2,1,0:T(8,128)(2,1)S(1)}, bf16[5,512,128]{2,1,0:T(8,128)(2,1)S(1)}, u32[]{:S(2)}, u32[]{:S(2)}) collective-permute-start(bf16[5,512,128]{2,1,0:T(8,128)(2,1)S(1)} %bitcast_dynamic-update-slice_fusion.refs_1_), channel_id=1, source_target_pairs={{0,2},{1,3},{2,0},{3,1},{4,6},{5,7},{6,4},{7,5},{8,10},{9,11},{10,... | collective-permute-start | bytes 1966088 | tf_op jit(solution)/shard_map/attended_y/ppermute | solution.py:33
  91.4 2.6 %collective-permute-start.16 = (bf16[5,512,128]{2,1,0:T(8,128)(2,1)S(1)}, bf16[5,512,128]{2,1,0:T(8,128)(2,1)S(1)}, u32[]{:S(2)}, u32[]{:S(2)}) collective-permute-start(bf16[5,512,128]{2,1,0:T(8,128)(2,1)S(1)} %collective-permute-done.14.refs_1_), channel_id=1, source_target_pairs={{0,1},{1,0},{2,3},{3,2},{4,5},{5,4},{6,7},{7,6},{8,9},{9,8},{10,11... | collective-permute-start | bytes 1966088 | tf_op jit(solution)/shard_map/far_core/ppermute | solution.py:33

commit v5 on v4

--- a/solution.py
+++ b/solution.py
@@ -239,11 +239,10 @@
             ks[at, :] = halo[b, 0, rows, :]
             vs[at, :] = halo[b, 1, rows, :]
 
-    @pl.loop(0, 4)
-    def _(i):
+    for i in range(4):
         column = place_ref[0, SLAB + z * 4 + i] // 2
         low = jnp.maximum(column - 1, 0) * 256
-        here = spot(i)
+        here = slice(i * TILE, (i + 1) * TILE)
         edge = (column == 0) | (column == 3)
 
         def work(width):

time: 99.3 us -> 99 us (level)
  transfers between devices with their start and end apart: 18 -> 18, of which waited for: 7 -> 7; matrix products, arithmetic and copies ran while one was open for 2% -> 2% of each run, Pallas kernels for 22% -> 21%
where the time goes in v5:
time: 99 us; the launch traced here: 97.8 us
  waiting for transfers between devices  35.6 us (36%)
  starting transfers between devices  29.2 us (29%)
  Pallas kernels  24.5 us (25%)
  local copies, waits for them, and re-layouts  5.04 us (5%)
  other arithmetic  3.04 us (3%)
    ppermute x18, waiting for transfers between devices, send(): return lax.ppermute(block, AXES, route(rows, target))  35.6 us
    ppermute x18, starting transfers between devices, send(): return lax.ppermute(block, AXES, route(rows, target))  29.2 us
    pallas_call x11, Pallas kernels, call(): pl.pallas_call(body, out_shape=outs, in_specs=[SCALARS] * scalars + [ANYW...  24.5 us
    another operation x1, other arithmetic, local(): kvq = jnp.stack([key_rows, value_rows, queries]).transpose(2, 0, 1, 3)  3.04 us
    unnamed x12, local copies, waits for them, and re-layouts  2.95 us
  transfers between devices with their start and end apart: 18, of which 7 were waited for; matrix products, arithmetic and copies ran while one was open for 2% of the time, Pallas kernels for 21%

profile of v5, /device:TPU:17, one launch (start us, length us, event | category | flops | bytes accessed | tf_op | source)
XLA Modules:
  0.0 97.8 jit_solution(5686597060071483541)
XLA Ops:
  0.0 3.0 %pad_maximum_fusion = (bf16[3,512,5,128]{3,1,0,2:T(8,128)(2,1)S(1)}, bf16[5,3,512,128]{3,2,1,0:T(8,128)(2,1)}) fusion(bf16[1,512,5,128]{3,1,0,2:T(8,128)(2,1)} %bitcast.35, bf16[1,512,5,128]{3,1,0,2:T(8,128)(2,1)} %bitcast.36, bf16[1,512,5,128]{3,1,0,2:T(8,128)(2,1)} %bitcast.37), kind=kLoop, calls=%fused_computation | loop fusion | flops 1966080 | bytes 5898240 | tf_op jit(solution)/shard_map/lay_out/stack | solution.py:361
  3.2 3.8 %collective-permute-start = (bf16[3,512,128]{2,1,0:T(8,128)(2,1)S(1)}, bf16[3,512,128]{2,1,0:T(8,128)(2,1)S(1)}, u32[]{:S(2)}, u32[]{:S(2)}) collective-permute-start(bf16[3,512,128]{2,1,0:T(8,128)(2,1)S(1)} %get-tuple-element.41), channel_id=1, source_target_pairs={{0,12},{1,13},{2,14},{3,15},{4,0},{5,1},{6,2},{7,3},{8,4},{9,5},{1... | collective-permute-start | bytes 1179656 | tf_op jit(solution)/shard_map/head_z/ppermute | solution.py:33
  7.8 2.9 %copy-done = bf16[5,128,5120]{2,1,0:T(8,128)(2,1)S(1)} copy-done((bf16[5,128,5120]{2,1,0:T(8,128)(2,1)S(1)}, bf16[5,128,5120]{2,1,0:T(8,128)(2,1)}, u32[]{:S(2)}) %copy-start) | copy-done | bytes 6553624
  10.6 0.9 weights_y.1
  11.8 1.0 slice_bitcast_fusion.refs_2_
  12.7 10.3 %collective-permute-done.refs_2_.refs_3_ = bf16[3,512,128]{2,1,0:T(8,128)(2,1)S(1)} collective-permute-done((bf16[3,512,128]{2,1,0:T(8,128)(2,1)S(1)}, bf16[3,512,128]{2,1,0:T(8,128)(2,1)S(1)}, u32[]{:S(2)}, u32[]{:S(2)}) %collective-permute-start) | collective-permute-done | bytes 393248 | tf_op jit(solution)/shard_map/head_z/ppermute | solution.py:33
  23.0 4.3 %collective-permute-done.2.refs_4_.refs_5_ = bf16[3,512,128]{2,1,0:T(8,128)(2,1)S(1)} collective-permute-done((bf16[3,512,128]{2,1,0:T(8,128)(2,1)S(1)}, bf16[3,512,128]{2,1,0:T(8,128)(2,1)S(1)}, u32[]{:S(2)}, u32[]{:S(2)}) %collective-permute-start.2) | collective-permute-done | bytes 393248 | tf_op jit(solution)/shard_map/head_z/ppermute | solution.py:33
  28.0 1.2 %places.1 = (s32[1,32]{1,0:T(1,128)S(1)}, bf16[2,512,128]{2,1,0:T(8,128)(2,1)S(1)}) custom-call(s32[6]{0:T(128)S(1)} %stack.65.refs_0_, s32[128,128]{1,0:T(8,128)S(1)} %copy-done.1, bf16[2,512,128]{2,1,0:T(8,128)(2,1)S(1)} %slice_bitcast_fusion.refs_2_, bf16[2,2,512,128]{3,2,1,0:T(8,128)(2,1)S(1)} %get-tuple-element.22.refs_3_), custom_call_target="tpu_custom_call" | custom-call | flops 8000000000 | bytes 1024 | tf_op jit(solution)/shard_map/places/pallas_call | solution.py:97
  29.3 0.9 slice_bitcast_fusion.1.refs_6_
  30.2 3.1 %collective-permute-start.3 = (bf16[2,2,512,128]{3,2,1,0:T(8,128)(2,1)S(1)}, bf16[2,2,512,128]{3,2,1,0:T(8,128)(2,1)S(1)}, u32[]{:S(2)}, u32[]{:S(2)}) collective-permute-start(bf16[2,2,512,128]{3,2,1,0:T(8,128)(2,1)S(1)} %get-tuple-element.22.refs_3_), channel_id=1, source_target_pairs={{0,16},{1,17},{2,18},{3,19},{4,20},{5,21},{6,22},{7,23},{8,24},{9,... | collective-permute-start | bytes 1572872 | tf_op jit(solution)/shard_map/head_x/ppermute | solution.py:33
  34.1 0.9 collective-permute-start.7
  34.9 1.3 %collective-permute-done.5.refs_2_.refs_3_ = bf16[2,512,128]{2,1,0:T(8,128)(2,1)S(1)} collective-permute-done((bf16[2,512,128]{2,1,0:T(8,128)(2,1)S(1)}, bf16[2,512,128]{2,1,0:T(8,128)(2,1)S(1)}, u32[]{:S(2)}, u32[]{:S(2)}) %collective-permute-start.5) | collective-permute-done | bytes 262176 | tf_op jit(solution)/shard_map/rest_z/ppermute | solution.py:33
  36.3 4.5 %collective-permute-start.4 = (bf16[2,2,512,128]{3,2,1,0:T(8,128)(2,1)S(1)}, bf16[2,2,512,128]{3,2,1,0:T(8,128)(2,1)S(1)}, u32[]{:S(2)}, u32[]{:S(2)}) collective-permute-start(bf16[2,2,512,128]{3,2,1,0:T(8,128)(2,1)S(1)} %get-tuple-element.27), channel_id=1, source_target_pairs={{16,0},{17,1},{18,2},{19,3},{20,4},{21,5},{22,6},{23,7},{24,8},{25... | collective-permute-start | bytes 1572872 | tf_op jit(solution)/shard_map/head_x/ppermute | solution.py:33
  40.7 5.1 %near_attention.1 = (bf16[2048,128]{1,0:T(8,128)(2,1)S(1)}, f32[2048,128]{1,0:T(8,128)S(1)}, f32[2048,128]{1,0:T(8,128)S(1)}) custom-call(s32[6]{0:T(128)S(1)} %stack.65.refs_0_, s32[1,32]{1,0:T(1,128)S(1)} %get-tuple-element.23.refs_1_, bf16[3,512,128]{2,1,0:T(8,128)(2,1)S(1)} %get-tuple-element.42.refs_1_.refs_2_, ...), custom_call_target="tpu_custom_call" | custom-call | flops 8000000000 | bytes 1024 | tf_op jit(solution)/shard_map/near_attention/pallas_call | solution.py:97
  45.8 2.9 %collective-permute-done.7.refs_4_.refs_5_ = bf16[2,512,128]{2,1,0:T(8,128)(2,1)S(1)} collective-permute-done((bf16[2,512,128]{2,1,0:T(8,128)(2,1)S(1)}, bf16[2,512,128]{2,1,0:T(8,128)(2,1)S(1)}, u32[]{:S(2)}, u32[]{:S(2)}) %collective-permute-start.7) | collective-permute-done | bytes 262176 | tf_op jit(solution)/shard_map/rest_z/ppermute | solution.py:33
  49.4 3.1 %collective-permute-start.11 = (bf16[2,2,512,128]{3,2,1,0:T(8,128)(2,1)S(1)}, bf16[2,2,512,128]{3,2,1,0:T(8,128)(2,1)S(1)}, u32[]{:S(2)}, u32[]{:S(2)}) collective-permute-start(bf16[2,2,512,128]{3,2,1,0:T(8,128)(2,1)S(1)} %rest_pick.1.refs_7_), channel_id=1, source_target_pairs={{0,16},{1,17},{2,18},{3,19},{4,20},{5,21},{6,22},{7,23},{16,32},{1... | collective-permute-start | bytes 1572872 | tf_op jit(solution)/shard_map/rest_x/ppermute | solution.py:33
  52.5 4.3 %halo_attention.1 = (bf16[512,128]{1,0:T(8,128)(2,1)S(1)}, bf16[512,128]{1,0:T(8,128)(2,1)S(1)}, bf16[512,128]{1,0:T(8,128)(2,1)S(1)}, bf16[512,128]{1,0:T(8,128)(2,1)S(1)}) custom-call(s32[6]{0:T(128)S(1)} %stack.65.refs_0_, s32[1,32]{1,0:T(1,128)S(1)} %get-tuple-element.23.refs_1_, bf16[2048,128]{1,0:T(8,128)(2,1)S(1)} %get-tuple-element.24.refs_2_, ...), custom_call_target="tpu_custom_call" | custom-call | flops 1000000000 | bytes 1024 | tf_op jit(solution)/shard_map/halo_attention/pallas_call | solution.py:97
  56.8 2.2 %collective-permute-start.8 = (bf16[512,128]{1,0:T(8,128)(2,1)S(1)}, bf16[512,128]{1,0:T(8,128)(2,1)S(1)}, u32[]{:S(2)}, u32[]{:S(2)}) collective-permute-start(bf16[512,128]{1,0:T(8,128)(2,1)S(1)} %get-tuple-element.30), channel_id=1, source_target_pairs={{0,12},{1,13},{2,14},{3,15},{4,0},{5,1},{6,2},{7,3},{8,4},{9,5},{1... | collective-permute-start | bytes 393224 | tf_op jit(solution)/shard_map/attended_z/ppermute | solution.py:33
  59.0 1.5 %collective-permute-start.9 = (bf16[512,128]{1,0:T(8,128)(2,1)S(1)}, bf16[512,128]{1,0:T(8,128)(2,1)S(1)}, u32[]{:S(2)}, u32[]{:S(2)}) collective-permute-start(bf16[512,128]{1,0:T(8,128)(2,1)S(1)} %get-tuple-element.31), channel_id=1, source_target_pairs={{0,8},{1,9},{2,10},{3,11},{4,12},{5,13},{6,14},{7,15},{8,0},{9,1},... | collective-permute-start | bytes 393224 | tf_op jit(solution)/shard_map/attended_z/ppermute | solution.py:33
  60.5 0.8 collective-permute-start.10
  61.3 0.9 weights_core.1
  62.2 4.0 %collective-permute-start.13 = (bf16[640,1280]{1,0:T(8,128)(2,1)S(1)}, bf16[640,1280]{1,0:T(8,128)(2,1)S(1)}, u32[]{:S(2)}, u32[]{:S(2)}) collective-permute-start(bf16[640,1280]{1,0:T(8,128)(2,1)S(1)} %get-tuple-element.34), channel_id=1, source_target_pairs={{0,1},{1,0},{2,3},{3,2},{4,5},{5,4},{6,7},{7,6},{8,9},{9,8},{10,11... | collective-permute-start | bytes 4915208 | tf_op jit(solution)/shard_map/weights_core/ppermute | solution.py:33
  66.3 1.6 %collective-permute-done.11.refs_7_ = bf16[2,2,512,128]{3,2,1,0:T(8,128)(2,1)S(1)} collective-permute-done((bf16[2,2,512,128]{3,2,1,0:T(8,128)(2,1)S(1)}, bf16[2,2,512,128]{3,2,1,0:T(8,128)(2,1)S(1)}, u32[]{:S(2)}, u32[]{:S(2)}) %collective-permute-start.11) | collective-permute-done | bytes 524320 | tf_op jit(solution)/shard_map/rest_x/ppermute | solution.py:33
  67.9 3.5 %rest_attention.1.refs_2_ = bf16[512,128]{1,0:T(8,128)(2,1)S(1)} custom-call(s32[6]{0:T(128)S(1)} %stack.65.refs_0_, s32[1,32]{1,0:T(1,128)S(1)} %get-tuple-element.23.refs_1_, bf16[2,512,128]{2,1,0:T(8,128)(2,1)S(1)} %get-tuple-element.28.refs_1_.refs_2_, bf16[2,512,128]{2,1,0:T(8,128)(2,1)S(1)} %collective-permute-done.5.refs_2_.refs_3_, ...), custom_call_target="tpu_custom_call" | custom-call | flops 3000000000 | bytes 1024 | tf_op jit(solution)/shard_map/rest_attention/pallas_call | solution.py:97
  71.5 1.5 %collective-permute-start.12 = (bf16[5,512,128]{2,1,0:T(8,128)(2,1)S(1)}, bf16[5,512,128]{2,1,0:T(8,128)(2,1)S(1)}, u32[]{:S(2)}, u32[]{:S(2)}) collective-permute-start(bf16[5,512,128]{2,1,0:T(8,128)(2,1)S(1)} %bitcast_dynamic-update-slice_fusion.refs_1_), channel_id=1, source_target_pairs={{0,1},{1,0},{2,3},{3,2},{4,5},{5,4},{6,7},{7,6},{8,9},{9,8},{10,11... | collective-permute-start | bytes 1966088 | tf_op jit(solution)/shard_map/attended_core/ppermute | solution.py:33
  73.0 0.8 weights_far_core.1
  73.8 1.3 %collective-permute-start.17 = (bf16[640,1280]{1,0:T(8,128)(2,1)S(1)}, bf16[640,1280]{1,0:T(8,128)(2,1)S(1)}, u32[]{:S(2)}, u32[]{:S(2)}) collective-permute-start(bf16[640,1280]{1,0:T(8,128)(2,1)S(1)} %get-tuple-element.37), channel_id=1, source_target_pairs={{0,1},{1,0},{2,3},{3,2},{4,5},{5,4},{6,7},{7,6},{8,9},{9,8},{10,11... | collective-permute-start | bytes 4915208 | tf_op jit(solution)/shard_map/weights_far_core/ppermute | solution.py:33
  75.1 2.9 %project.1.refs_5_ = f32[512,1280]{1,0:T(8,128)S(1)} custom-call(s32[6]{0:T(128)S(1)} %stack.65.refs_0_, bf16[5,512,128]{2,1,0:T(8,128)(2,1)S(1)} %bitcast_dynamic-update-slice_fusion.refs_1_, bf16[640,1280]{1,0:T(8,128)(2,1)S(1)} %get-tuple-element.33.refs_2_, bf16[5,512,128]{2,1,0:T(8,128)(2,1)S(1)} %collective-permute-done.12.refs_3_, ...), custom_call_target="tpu_custom_call" | custom-call | flops 10000000000 | bytes 1024 | tf_op jit(solution)/shard_map/project/pallas_call | solution.py:97
  78.0 13.4 %collective-permute-done.14.refs_1_ = bf16[5,512,128]{2,1,0:T(8,128)(2,1)S(1)} collective-permute-done((bf16[5,512,128]{2,1,0:T(8,128)(2,1)S(1)}, bf16[5,512,128]{2,1,0:T(8,128)(2,1)S(1)}, u32[]{:S(2)}, u32[]{:S(2)}) %collective-permute-start.14) | collective-permute-done | bytes 655392 | tf_op jit(solution)/shard_map/attended_y/ppermute | solution.py:33
  91.4 0.9 collective-permute-start.16
  92.3 1.7 %collective-permute-done.16.refs_3_ = bf16[5,512,128]{2,1,0:T(8,128)(2,1)S(1)} collective-permute-done((bf16[5,512,128]{2,1,0:T(8,128)(2,1)S(1)}, bf16[5,512,128]{2,1,0:T(8,128)(2,1)S(1)}, u32[]{:S(2)}, u32[]{:S(2)}) %collective-permute-start.16) | collective-permute-done | bytes 655392 | tf_op jit(solution)/shard_map/far_core/ppermute | solution.py:33
  94.0 3.7 %finish.1 = bf16[512,1280]{1,0:T(8,128)(2,1)} custom-call(s32[6]{0:T(128)S(1)} %stack.65.refs_0_, bf16[5,512,128]{2,1,0:T(8,128)(2,1)S(1)} %collective-permute-done.14.refs_1_, bf16[640,1280]{1,0:T(8,128)(2,1)S(1)} %get-tuple-element.36.refs_2_, bf16[5,512,128]{2,1,0:T(8,128)(2,1)S(1)} %collective-permute-done.16.refs_3_, ...), custom_call_target="tpu_custom_call" | custom-call | flops 1024 | bytes 1024 | tf_op jit(solution)/shard_map/finish/pallas_call | solution.py:97
  (34 shorter events, 3.3 us)
Async XLA Ops:
  3.2 19.9 %collective-permute-start = (bf16[3,512,128]{2,1,0:T(8,128)(2,1)S(1)}, bf16[3,512,128]{2,1,0:T(8,128)(2,1)S(1)}, u32[]{:S(2)}, u32[]{:S(2)}) collective-permute-start(bf16[3,512,128]{2,1,0:T(8,128)(2,1)S(1)} %get-tuple-element.41), channel_id=1, source_target_pairs={{0,12},{1,13},{2,14},{3,15},{4,0},{5,1},{6,2},{7,3},{8,4},{9,5},{1... | collective-permute-start | bytes 1179656 | tf_op jit(solution)/shard_map/head_z/ppermute | solution.py:33
  7.0 16.1 %collective-permute-start.1 = (bf16[3,512,128]{2,1,0:T(8,128)(2,1)S(1)}, bf16[3,512,128]{2,1,0:T(8,128)(2,1)S(1)}, u32[]{:S(2)}, u32[]{:S(2)}) collective-permute-start(bf16[3,512,128]{2,1,0:T(8,128)(2,1)S(1)} %get-tuple-element.40), channel_id=1, source_target_pairs={{0,8},{1,9},{2,10},{3,11},{4,12},{5,13},{6,14},{7,15},{8,0},{9,1},... | collective-permute-start | bytes 1179656 | tf_op jit(solution)/shard_map/head_z/ppermute | solution.py:33
  7.0 20.3 %collective-permute-start.2 = (bf16[3,512,128]{2,1,0:T(8,128)(2,1)S(1)}, bf16[3,512,128]{2,1,0:T(8,128)(2,1)S(1)}, u32[]{:S(2)}, u32[]{:S(2)}) collective-permute-start(bf16[3,512,128]{2,1,0:T(8,128)(2,1)S(1)} %get-tuple-element.39.refs_2_), channel_id=1, source_target_pairs={{0,4},{1,5},{2,6},{3,7},{4,8},{5,9},{6,10},{7,11},{8,12},{9,13},{1... | collective-permute-start | bytes 1179656 | tf_op jit(solution)/shard_map/head_z/ppermute | solution.py:33
  7.8 2.9 %copy-start = (bf16[5,128,5120]{2,1,0:T(8,128)(2,1)S(1)}, bf16[5,128,5120]{2,1,0:T(8,128)(2,1)}, u32[]{:S(2)}) copy-start(bf16[5,128,5120]{2,1,0:T(8,128)(2,1)} %refs_1_.5) | copy-start | bytes 19660804
  11.5 16.4 %copy-start.1 = (s32[128,128]{1,0:T(8,128)S(1)}, s32[128,128]{1,0:T(8,128)}, u32[]{:S(2)}) copy-start(s32[128,128]{1,0:T(8,128)} %refs_1_.3) | copy-start | bytes 196612
  11.5 61.5 %collective-permute-start.15 = (bf16[640,2560]{1,0:T(8,128)(2,1)S(1)}, bf16[640,2560]{1,0:T(8,128)(2,1)S(1)}, u32[]{:S(2)}, u32[]{:S(2)}) collective-permute-start(bf16[640,2560]{1,0:T(8,128)(2,1)S(1)} %weights_y.1), channel_id=1, source_target_pairs={{0,2},{1,67},{2,64},{3,1},{4,6},{5,71},{6,68},{7,5},{8,10},{9,75},... | collective-permute-start | bytes 9830408 | tf_op jit(solution)/shard_map/weights_y/ppermute | solution.py:33
  28.0 33.3 %slice-start = ((s8[6553600]{0:T(1024)(128)(4,1)}), s8[4194304]{0:T(1024)(128)(4,1)S(1)}, s32[]{:S(2)}) async-start(s8[6553600]{0:T(1024)(128)(4,1)} %bitcast.33), calls=%async_computation | async-start | bytes 8388608
  29.2 7.1 %collective-permute-start.5 = (bf16[2,512,128]{2,1,0:T(8,128)(2,1)S(1)}, bf16[2,512,128]{2,1,0:T(8,128)(2,1)S(1)}, u32[]{:S(2)}, u32[]{:S(2)}) collective-permute-start(bf16[2,512,128]{2,1,0:T(8,128)(2,1)S(1)} %get-tuple-element.28.refs_1_.refs_2_), channel_id=1, source_target_pairs={{0,12},{1,13},{2,14},{3,15},{4,0},{5,1},{6,2},{7,3},{8,4},{9,5},{1... | collective-permute-start | bytes 786440 | tf_op jit(solution)/shard_map/rest_z/ppermute | solution.py:33
  30.2 22.3 %collective-permute-start.3 = (bf16[2,2,512,128]{3,2,1,0:T(8,128)(2,1)S(1)}, bf16[2,2,512,128]{3,2,1,0:T(8,128)(2,1)S(1)}, u32[]{:S(2)}, u32[]{:S(2)}) collective-permute-start(bf16[2,2,512,128]{3,2,1,0:T(8,128)(2,1)S(1)} %get-tuple-element.22.refs_3_), channel_id=1, source_target_pairs={{0,16},{1,17},{2,18},{3,19},{4,20},{5,21},{6,22},{7,23},{8,24},{9,... | collective-permute-start | bytes 1572872 | tf_op jit(solution)/shard_map/head_x/ppermute | solution.py:33
  33.3 12.5 %collective-permute-start.6 = (bf16[2,512,128]{2,1,0:T(8,128)(2,1)S(1)}, bf16[2,512,128]{2,1,0:T(8,128)(2,1)S(1)}, u32[]{:S(2)}, u32[]{:S(2)}) collective-permute-start(bf16[2,512,128]{2,1,0:T(8,128)(2,1)S(1)} %get-tuple-element.28.refs_1_.refs_2_), channel_id=1, source_target_pairs={{0,8},{1,9},{2,10},{3,11},{4,12},{5,13},{6,14},{7,15},{8,0},{9,1},... | collective-permute-start | bytes 786440 | tf_op jit(solution)/shard_map/rest_z/ppermute | solution.py:33
  34.1 14.7 %collective-permute-start.7 = (bf16[2,512,128]{2,1,0:T(8,128)(2,1)S(1)}, bf16[2,512,128]{2,1,0:T(8,128)(2,1)S(1)}, u32[]{:S(2)}, u32[]{:S(2)}) collective-permute-start(bf16[2,512,128]{2,1,0:T(8,128)(2,1)S(1)} %get-tuple-element.28.refs_1_.refs_2_), channel_id=1, source_target_pairs={{0,4},{1,5},{2,6},{3,7},{4,8},{5,9},{6,10},{7,11},{8,12},{9,13},{1... | collective-permute-start | bytes 786440 | tf_op jit(solution)/shard_map/rest_z/ppermute | solution.py:33
  36.3 16.2 %collective-permute-start.4 = (bf16[2,2,512,128]{3,2,1,0:T(8,128)(2,1)S(1)}, bf16[2,2,512,128]{3,2,1,0:T(8,128)(2,1)S(1)}, u32[]{:S(2)}, u32[]{:S(2)}) collective-permute-start(bf16[2,2,512,128]{3,2,1,0:T(8,128)(2,1)S(1)} %get-tuple-element.27), channel_id=1, source_target_pairs={{16,0},{17,1},{18,2},{19,3},{20,4},{21,5},{22,6},{23,7},{24,8},{25... | collective-permute-start | bytes 1572872 | tf_op jit(solution)/shard_map/head_x/ppermute | solution.py:33
  40.7 20.5 %slice-start.1 = ((s8[6553600]{0:T(1024)(128)(4,1)}), s8[2359296]{0:T(1024)(128)(4,1)S(1)}, s32[]{:S(2)}) async-start(s8[6553600]{0:T(1024)(128)(4,1)} %bitcast.33), calls=%async_computation.1 | async-start | bytes 4718592
  49.4 18.6 %collective-permute-start.11 = (bf16[2,2,512,128]{3,2,1,0:T(8,128)(2,1)S(1)}, bf16[2,2,512,128]{3,2,1,0:T(8,128)(2,1)S(1)}, u32[]{:S(2)}, u32[]{:S(2)}) collective-permute-start(bf16[2,2,512,128]{3,2,1,0:T(8,128)(2,1)S(1)} %rest_pick.1.refs_7_), channel_id=1, source_target_pairs={{0,16},{1,17},{2,18},{3,19},{4,20},{5,21},{6,22},{7,23},{16,32},{1... | collective-permute-start | bytes 1572872 | tf_op jit(solution)/shard_map/rest_x/ppermute | solution.py:33
  56.8 5.4 %collective-permute-start.8 = (bf16[512,128]{1,0:T(8,128)(2,1)S(1)}, bf16[512,128]{1,0:T(8,128)(2,1)S(1)}, u32[]{:S(2)}, u32[]{:S(2)}) collective-permute-start(bf16[512,128]{1,0:T(8,128)(2,1)S(1)} %get-tuple-element.30), channel_id=1, source_target_pairs={{0,12},{1,13},{2,14},{3,15},{4,0},{5,1},{6,2},{7,3},{8,4},{9,5},{1... | collective-permute-start | bytes 393224 | tf_op jit(solution)/shard_map/attended_z/ppermute | solution.py:33
  59.0 7.2 %collective-permute-start.9 = (bf16[512,128]{1,0:T(8,128)(2,1)S(1)}, bf16[512,128]{1,0:T(8,128)(2,1)S(1)}, u32[]{:S(2)}, u32[]{:S(2)}) collective-permute-start(bf16[512,128]{1,0:T(8,128)(2,1)S(1)} %get-tuple-element.31), channel_id=1, source_target_pairs={{0,8},{1,9},{2,10},{3,11},{4,12},{5,13},{6,14},{7,15},{8,0},{9,1},... | collective-permute-start | bytes 393224 | tf_op jit(solution)/shard_map/attended_z/ppermute | solution.py:33
  60.5 5.8 %collective-permute-start.10 = (bf16[512,128]{1,0:T(8,128)(2,1)S(1)}, bf16[512,128]{1,0:T(8,128)(2,1)S(1)}, u32[]{:S(2)}, u32[]{:S(2)}) collective-permute-start(bf16[512,128]{1,0:T(8,128)(2,1)S(1)} %get-tuple-element.32), channel_id=1, source_target_pairs={{0,4},{1,5},{2,6},{3,7},{4,8},{5,9},{6,10},{7,11},{8,12},{9,13},{1... | collective-permute-start | bytes 393224 | tf_op jit(solution)/shard_map/attended_z/ppermute | solution.py:33
  62.2 12.9 %collective-permute-start.13 = (bf16[640,1280]{1,0:T(8,128)(2,1)S(1)}, bf16[640,1280]{1,0:T(8,128)(2,1)S(1)}, u32[]{:S(2)}, u32[]{:S(2)}) collective-permute-start(bf16[640,1280]{1,0:T(8,128)(2,1)S(1)} %get-tuple-element.34), channel_id=1, source_target_pairs={{0,1},{1,0},{2,3},{3,2},{4,5},{5,4},{6,7},{7,6},{8,9},{9,8},{10,11... | collective-permute-start | bytes 4915208 | tf_op jit(solution)/shard_map/weights_core/ppermute | solution.py:33
  71.5 3.6 %collective-permute-start.12 = (bf16[5,512,128]{2,1,0:T(8,128)(2,1)S(1)}, bf16[5,512,128]{2,1,0:T(8,128)(2,1)S(1)}, u32[]{:S(2)}, u32[]{:S(2)}) collective-permute-start(bf16[5,512,128]{2,1,0:T(8,128)(2,1)S(1)} %bitcast_dynamic-update-slice_fusion.refs_1_), channel_id=1, source_target_pairs={{0,1},{1,0},{2,3},{3,2},{4,5},{5,4},{6,7},{7,6},{8,9},{9,8},{10,11... | collective-permute-start | bytes 1966088 | tf_op jit(solution)/shard_map/attended_core/ppermute | solution.py:33
  73.8 20.2 %collective-permute-start.17 = (bf16[640,1280]{1,0:T(8,128)(2,1)S(1)}, bf16[640,1280]{1,0:T(8,128)(2,1)S(1)}, u32[]{:S(2)}, u32[]{:S(2)}) collective-permute-start(bf16[640,1280]{1,0:T(8,128)(2,1)S(1)} %get-tuple-element.37), channel_id=1, source_target_pairs={{0,1},{1,0},{2,3},{3,2},{4,5},{5,4},{6,7},{7,6},{8,9},{9,8},{10,11... | collective-permute-start | bytes 4915208 | tf_op jit(solution)/shard_map/weights_far_core/ppermute | solution.py:33
  75.1 16.3 %collective-permute-start.14 = (bf16[5,512,128]{2,1,0:T(8,128)(2,1)S(1)}, bf16[5,512,128]{2,1,0:T(8,128)(2,1)S(1)}, u32[]{:S(2)}, u32[]{:S(2)}) collective-permute-start(bf16[5,512,128]{2,1,0:T(8,128)(2,1)S(1)} %bitcast_dynamic-update-slice_fusion.refs_1_), channel_id=1, source_target_pairs={{0,2},{1,3},{2,0},{3,1},{4,6},{5,7},{6,4},{7,5},{8,10},{9,11},{10,... | collective-permute-start | bytes 1966088 | tf_op jit(solution)/shard_map/attended_y/ppermute | solution.py:33
  91.4 2.6 %collective-permute-start.16 = (bf16[5,512,128]{2,1,0:T(8,128)(2,1)S(1)}, bf16[5,512,128]{2,1,0:T(8,128)(2,1)S(1)}, u32[]{:S(2)}, u32[]{:S(2)}) collective-permute-start(bf16[5,512,128]{2,1,0:T(8,128)(2,1)S(1)} %collective-permute-done.14.refs_1_), channel_id=1, source_target_pairs={{0,1},{1,0},{2,3},{3,2},{4,5},{5,4},{6,7},{7,6},{8,9},{9,8},{10,11... | collective-permute-start | bytes 1966088 | tf_op jit(solution)/shard_map/far_core/ppermute | solution.py:33
